TPU v7x, 128 devices: a whole 4x4x4 slice. The times are simulated.
128 devices in a mesh: section: 2 (over y_lo), dp: 4 (over y_hi, core), expert: 16 (over z, x).
Axes of the slice: x: 4, y: 4 (y_hi: 2, y_lo: 2; y = y_hi * 2 + y_lo), z: 4, core: 2. Of those that a mesh axis runs over, the one named last changes fastest.
Arguments:
- inputs: bfloat16 [2, 8192, 1024], P(None, ('dp', 'expert')), may hold values from -6 to 6
- cotangent: bfloat16 [2, 8192, 1024], P(None, ('dp', 'expert')), may hold values from -6 to 6
- offsets: int32 [2, 8192], P(None, ('dp', 'expert')), may hold values from 0 to 2047, as said below
- routes: int32 [2, 2, 8192, 8], P('section', None, ('dp', 'expert')), may hold values from 0 to 31, all different within a row; in each aligned block of 128 rows (0 to 127, 128 to 255, ..., all dimensions but the last counted through in order) at most 33 rows name the same one
- w_query: bfloat16 [2, 1024, 1024], P('section'), may hold values from -0.1875 to 0.1875
- w_key: bfloat16 [2, 1024, 512], P('section'), may hold values from -0.1875 to 0.1875
- w_value: bfloat16 [2, 1024, 512], P('section'), may hold values from -0.1875 to 0.1875
- w_out: bfloat16 [2, 1024, 1024], P('section'), may hold values from -1 to 1
- norm_attn: bfloat16 [2, 1024], P('section'), may hold values from 0.5 to 1.5
- norm_moe: bfloat16 [2, 1024], P('section'), may hold values from 0.5 to 1.5
- w_router: bfloat16 [2, 1024, 32], P('section'), may hold values from -0.09375 to 0.09375
- w_gate: bfloat16 [2, 32, 1024, 512], P('section', 'expert', 'dp'), may hold values from -0.1875 to 0.1875
- w_up: bfloat16 [2, 32, 1024, 512], P('section', 'expert', 'dp'), may hold values from -0.1875 to 0.1875
- w_down: bfloat16 [2, 32, 1024, 512], P('section', 'expert', 'dp'), may hold values from -0.75 to 0.75
Outputs:
- acts: bfloat16 [2, 2, 8192, 1024], P('section', None, ('dp', 'expert'))
- in_grads: bfloat16 [2, 2, 8192, 1024], P('section', None, ('dp', 'expert'))
- grad_query: float32 [2, 1024, 1024], P('section')
- grad_key: float32 [2, 1024, 512], P('section')
- grad_value: float32 [2, 1024, 512], P('section')
- grad_out: float32 [2, 1024, 1024], P('section')
- grad_norm_attn: float32 [2, 1024], P('section')
- grad_norm_moe: float32 [2, 1024], P('section')
- grad_router: float32 [2, 1024, 32], P('section')
- grad_gate: float32 [2, 32, 1024, 512], P('section', 'expert', 'dp')
- grad_up: float32 [2, 32, 1024, 512], P('section', 'expert', 'dp')
- grad_down: float32 [2, 32, 1024, 512], P('section', 'expert', 'dp')
Inputs may be any that keep to these rules, and one draw needn't show every extreme that they name: `offsets`: A token's value equals the previous token's or its own index within its group of 2048 consecutive tokens, and the first token of a group has 0; every group holds a sequence that begins within its first 128 tokens and ends within its last 128. `routes`: in each aligned block of 128 rows (one device's tokens of one layer and micro-batch), no expert is named by more than 33 rows.
All inputs are finite; a program needn't handle non-finite values.
Results may differ from a plain program's by a relative error of at most 0.025.
Values may be sent and summed in bfloat16 or wider, within the bound.
A program may use at most 320 MiB of HBM per device.

v0:
```python
import jax
import jax.numpy as jnp
from jax import lax
from jax.sharding import PartitionSpec as P

HEAD = 64


norm_eps = 1e-06
masked_score = -1e30
rope_base = 10000.0


def passed_along(x, axis, by):
    peers = lax.axis_size(axis)
    pairs = [(i, i + by) for i in range(peers) if 0 <= i + by < peers]
    return lax.ppermute(x, axis, pairs)


def shortened(x):

    def short(part):
        return part.astype(jnp.bfloat16) if part.dtype == jnp.float32 else part

    return jax.tree.map(short, x)


def rotate_half(values):
    middle = values.shape[-1] // 2
    return jnp.concatenate([-values[..., middle:], values[..., :middle]], axis=-1)


def rotate_back(values):
    middle = values.shape[-1] // 2
    return jnp.concatenate([values[..., middle:], -values[..., :middle]], axis=-1)


def rope_angles(positions, head_size):
    steps_half = jnp.arange(head_size // 2, dtype=jnp.float32) * 2.0 / head_size
    frequency = rope_base ** (-steps_half)
    angles = positions.astype(jnp.float32)[:, None] * frequency[None, :]
    angles = jnp.concatenate([angles, angles], axis=-1)
    return (jnp.cos(angles)[:, None, :], jnp.sin(angles)[:, None, :])


def visible_keys(seq_offsets, tok_rows, group_len):
    local_index = lax.axis_index("expert") * tok_rows + jnp.arange(tok_rows, dtype=jnp.int32)
    key_index = jnp.arange(group_len, dtype=jnp.int32)
    visible = (key_index[None, :] <= local_index[:, None]) & (
        key_index[None, :] >= seq_offsets[:, None]
    )
    return (local_index, visible)


def slot_layout(route_ids, expert_count, capacity):
    flat_routes = route_ids.reshape(-1)
    expert_hits = (
        flat_routes[:, None] == jnp.arange(expert_count, dtype=jnp.int32)[None, :]
    ).astype(jnp.int32)
    slot_rank = jnp.sum((jnp.cumsum(expert_hits, axis=0) - 1) * expert_hits, axis=1)
    return flat_routes * capacity + slot_rank


def forward_layer(layer_input, seq_offsets, route_ids, dense_weights, expert_weights):
    w_query, w_key, w_value, w_out, gain_attn, gain_moe, w_router = dense_weights
    w_gate, w_up, w_down = expert_weights
    tok_rows, width = layer_input.shape
    head_size = HEAD
    head_count = w_query.shape[1] // head_size
    key_heads = w_key.shape[1] // head_size
    query_share = head_count // key_heads
    expert_count = w_router.shape[1]
    top_count = route_ids.shape[1]
    spread = lax.axis_size("expert")
    per_device = w_gate.shape[0]
    group_len = tok_rows * spread
    capacity = tok_rows * top_count // expert_count + 1
    attn_scale = lax.rsqrt(jnp.mean(layer_input * layer_input, axis=-1, keepdims=True) + norm_eps)
    attn_normed = layer_input * attn_scale
    attn_in = (attn_normed * gain_attn).astype(jnp.bfloat16)
    local_index, visible = visible_keys(seq_offsets, tok_rows, group_len)
    cosine, sine = rope_angles(local_index - seq_offsets, head_size)
    query_lin = jnp.dot(attn_in, w_query, preferred_element_type=jnp.float32).reshape(
        tok_rows, head_count, head_size
    )
    key_lin = jnp.dot(attn_in, w_key, preferred_element_type=jnp.float32).reshape(
        tok_rows, key_heads, head_size
    )
    value_new = jnp.dot(attn_in, w_value, preferred_element_type=jnp.float32).astype(jnp.bfloat16)
    query_rot = (query_lin * cosine + rotate_half(query_lin) * sine).astype(jnp.bfloat16)
    query_rot = query_rot.reshape(tok_rows, key_heads, query_share, head_size)
    key_rot = (
        (key_lin * cosine + rotate_half(key_lin) * sine)
        .astype(jnp.bfloat16)
        .reshape(tok_rows, key_heads * head_size)
    )
    keys_all, values_all = (
        lax.all_gather(key_rot, "expert", axis=0, tiled=True),
        lax.all_gather(value_new, "expert", axis=0, tiled=True),
    )
    keys_grid = keys_all.reshape(group_len, key_heads, head_size)
    values_grid = values_all.reshape(group_len, key_heads, head_size)
    scores = (
        jnp.einsum("tkgd,skd->kgts", query_rot, keys_grid, preferred_element_type=jnp.float32)
        * 0.125
    )
    scores = jnp.where(visible, scores, masked_score)
    row_max = jnp.max(scores, axis=-1, keepdims=True)
    expo = jnp.exp(scores - row_max)
    total = jnp.sum(expo, axis=-1, keepdims=True)
    probs = (expo / total).astype(jnp.bfloat16)
    log_total = row_max + jnp.log(total)
    attended = jnp.einsum("kgts,skd->tkgd", probs, values_grid, preferred_element_type=jnp.float32)
    attended = attended.astype(jnp.bfloat16).reshape(tok_rows, head_count * head_size)
    hidden = layer_input + jnp.dot(attended, w_out, preferred_element_type=jnp.float32)
    moe_scale = lax.rsqrt(jnp.mean(hidden * hidden, axis=-1, keepdims=True) + norm_eps)
    moe_normed = hidden * moe_scale
    moe_in = (moe_normed * gain_moe).astype(jnp.bfloat16)
    logits = jnp.dot(moe_in, w_router, preferred_element_type=jnp.float32)
    gates = jax.nn.softmax(jnp.take_along_axis(logits, route_ids, axis=1), axis=-1)
    slot_index = slot_layout(route_ids, expert_count, capacity)
    token_of = jnp.arange(tok_rows * top_count, dtype=jnp.int32) // top_count
    outgoing = (
        jnp.zeros((expert_count * capacity, width), jnp.bfloat16)
        .at[slot_index]
        .set(moe_in[token_of])
    )
    outgoing = outgoing.reshape(spread, per_device, capacity, width)
    expert_rows = lax.all_to_all(outgoing, "expert", split_axis=0, concat_axis=2, tiled=True)[0]
    gate_lin = jnp.einsum("jrd,jdf->jrf", expert_rows, w_gate, preferred_element_type=jnp.float32)
    up_lin = jnp.einsum("jrd,jdf->jrf", expert_rows, w_up, preferred_element_type=jnp.float32)
    inner = (jax.nn.silu(gate_lin) * up_lin).astype(jnp.bfloat16)
    produced = jnp.einsum("jrf,jdf->jrd", inner, w_down, preferred_element_type=jnp.float32).astype(
        jnp.bfloat16
    )
    returned = lax.all_to_all(
        produced[None], "expert", split_axis=2, concat_axis=0, tiled=True
    ).reshape(expert_count * capacity, width)
    picked = returned[slot_index].reshape(tok_rows, top_count, width)
    mixture = jnp.sum(gates[:, :, None] * picked, axis=1)
    layer_output = hidden + mixture
    saved = (
        seq_offsets,
        route_ids,
        attn_scale,
        attn_normed,
        attn_in,
        query_rot,
        keys_all,
        values_all,
        log_total,
        attended,
        moe_scale,
        moe_normed,
        moe_in,
        gates,
        slot_index,
        expert_rows,
        gate_lin,
        up_lin,
        inner,
        picked,
    )
    return (layer_output, saved)


def backward_layer(grad_output, saved, dense_weights, expert_weights):
    (
        seq_offsets,
        route_ids,
        attn_scale,
        attn_normed,
        attn_in,
        query_rot,
        keys_all,
        values_all,
        log_total,
        attended,
        moe_scale,
        moe_normed,
        moe_in,
        gates,
        slot_index,
        expert_rows,
        gate_lin,
        up_lin,
        inner,
        picked,
    ) = saved
    w_query, w_key, w_value, w_out, gain_attn, gain_moe, w_router = dense_weights
    w_gate, w_up, w_down = expert_weights
    tok_rows, width = grad_output.shape
    head_size = HEAD
    head_count = w_query.shape[1] // head_size
    key_heads = w_key.shape[1] // head_size
    expert_count = w_router.shape[1]
    top_count = route_ids.shape[1]
    spread = lax.axis_size("expert")
    per_device = w_gate.shape[0]
    group_len = tok_rows * spread
    capacity = tok_rows * top_count // expert_count + 1
    gate_grad = jnp.sum(grad_output[:, None, :] * picked, axis=-1)
    slot_grad = (
        (gates[:, :, None] * grad_output[:, None, :])
        .astype(jnp.bfloat16)
        .reshape(tok_rows * top_count, width)
    )
    send_grad = (
        jnp.zeros((expert_count * capacity, width), jnp.bfloat16).at[slot_index].set(slot_grad)
    )
    send_grad = send_grad.reshape(spread, per_device, capacity, width)
    produced_grad = lax.all_to_all(send_grad, "expert", split_axis=0, concat_axis=2, tiled=True)[0]
    inner_grad = jnp.einsum(
        "jrd,jdf->jrf", produced_grad, w_down, preferred_element_type=jnp.float32
    )
    down_w_grad = jnp.einsum(
        "jrd,jrf->jdf", produced_grad, inner, preferred_element_type=jnp.float32
    )
    sigmoid_gate = jax.nn.sigmoid(gate_lin)
    silu_value = gate_lin * sigmoid_gate
    gate_lin_grad = (
        inner_grad * up_lin * sigmoid_gate * (1.0 + gate_lin * (1.0 - sigmoid_gate))
    ).astype(jnp.bfloat16)
    up_lin_grad = (inner_grad * silu_value).astype(jnp.bfloat16)
    gate_w_grad = jnp.einsum(
        "jrd,jrf->jdf", expert_rows, gate_lin_grad, preferred_element_type=jnp.float32
    )
    up_w_grad = jnp.einsum(
        "jrd,jrf->jdf", expert_rows, up_lin_grad, preferred_element_type=jnp.float32
    )
    rows_grad = jnp.einsum(
        "jrf,jdf->jrd", gate_lin_grad, w_gate, preferred_element_type=jnp.float32
    )
    rows_grad = (
        rows_grad
        + jnp.einsum("jrf,jdf->jrd", up_lin_grad, w_up, preferred_element_type=jnp.float32)
    ).astype(jnp.bfloat16)
    back_grad = lax.all_to_all(
        rows_grad[None], "expert", split_axis=2, concat_axis=0, tiled=True
    ).reshape(expert_count * capacity, width)
    moe_in_grad = jnp.sum(
        back_grad[slot_index].reshape(tok_rows, top_count, width).astype(jnp.float32), axis=1
    )
    chosen_grad = gates * (gate_grad - jnp.sum(gates * gate_grad, axis=-1, keepdims=True))
    expert_match = route_ids[:, :, None] == jnp.arange(expert_count, dtype=jnp.int32)[None, None, :]
    logit_grad = jnp.sum(jnp.where(expert_match, chosen_grad[:, :, None], 0.0), axis=1).astype(
        jnp.bfloat16
    )
    router_grad = jnp.einsum("td,te->de", moe_in, logit_grad, preferred_element_type=jnp.float32)
    moe_in_grad = moe_in_grad + jnp.einsum(
        "te,de->td", logit_grad, w_router, preferred_element_type=jnp.float32
    )
    gain_moe_grad = jnp.sum(moe_in_grad * moe_normed, axis=0)
    normed_grad = moe_in_grad * gain_moe
    hidden_grad = grad_output + moe_scale * (
        normed_grad - moe_normed * jnp.mean(normed_grad * moe_normed, axis=-1, keepdims=True)
    )
    attn_grad = hidden_grad.astype(jnp.bfloat16)
    out_w_grad = jnp.einsum("ti,td->id", attended, attn_grad, preferred_element_type=jnp.float32)
    attended_grad = jnp.einsum(
        "td,id->ti", attn_grad, w_out, preferred_element_type=jnp.float32
    ).astype(jnp.bfloat16)
    attended_grad = attended_grad.reshape(query_rot.shape)
    keys_grid = keys_all.reshape(group_len, key_heads, head_size)
    values_grid = values_all.reshape(group_len, key_heads, head_size)
    local_index, visible = visible_keys(seq_offsets, tok_rows, group_len)
    scores = (
        jnp.einsum("tkgd,skd->kgts", query_rot, keys_grid, preferred_element_type=jnp.float32)
        * 0.125
    )
    probs_exact = jnp.where(visible, jnp.exp(scores - log_total), 0.0)
    probs_grad = jnp.einsum(
        "tkgd,skd->kgts", attended_grad, values_grid, preferred_element_type=jnp.float32
    )
    delta = jnp.sum(probs_exact * probs_grad, axis=-1, keepdims=True)
    score_grad = (probs_exact * (probs_grad - delta)).astype(jnp.bfloat16)
    query_grad = (
        jnp.einsum("kgts,skd->tkgd", score_grad, keys_grid, preferred_element_type=jnp.float32)
        * 0.125
    )
    key_grad_all = (
        jnp.einsum("kgts,tkgd->skd", score_grad, query_rot, preferred_element_type=jnp.float32)
        * 0.125
    )
    value_grad_all = jnp.einsum(
        "kgts,tkgd->skd",
        probs_exact.astype(jnp.bfloat16),
        attended_grad,
        preferred_element_type=jnp.float32,
    )
    key_grad, value_grad = (
        lax.psum_scatter(
            key_grad_all.reshape(group_len, key_heads * head_size).astype(jnp.bfloat16),
            "expert",
            scatter_dimension=0,
            tiled=True,
        ).astype(jnp.float32),
        lax.psum_scatter(
            value_grad_all.reshape(group_len, key_heads * head_size).astype(jnp.bfloat16),
            "expert",
            scatter_dimension=0,
            tiled=True,
        ).astype(jnp.float32),
    )
    cosine, sine = rope_angles(local_index - seq_offsets, head_size)
    query_grad = query_grad.reshape(tok_rows, head_count, head_size)
    query_lin_grad = (
        (query_grad * cosine + rotate_back(query_grad * sine))
        .astype(jnp.bfloat16)
        .reshape(tok_rows, head_count * head_size)
    )
    key_grad = key_grad.reshape(tok_rows, key_heads, head_size)
    key_lin_grad = (
        (key_grad * cosine + rotate_back(key_grad * sine))
        .astype(jnp.bfloat16)
        .reshape(tok_rows, key_heads * head_size)
    )
    value_lin_grad = value_grad.astype(jnp.bfloat16)
    query_w_grad = jnp.einsum(
        "td,te->de", attn_in, query_lin_grad, preferred_element_type=jnp.float32
    )
    key_w_grad = jnp.einsum("td,te->de", attn_in, key_lin_grad, preferred_element_type=jnp.float32)
    value_w_grad = jnp.einsum(
        "td,te->de", attn_in, value_lin_grad, preferred_element_type=jnp.float32
    )
    attn_in_grad = jnp.einsum(
        "te,de->td", query_lin_grad, w_query, preferred_element_type=jnp.float32
    )
    attn_in_grad = attn_in_grad + jnp.einsum(
        "te,de->td", key_lin_grad, w_key, preferred_element_type=jnp.float32
    )
    attn_in_grad = attn_in_grad + jnp.einsum(
        "te,de->td", value_lin_grad, w_value, preferred_element_type=jnp.float32
    )
    gain_attn_grad = jnp.sum(attn_in_grad * attn_normed, axis=0)
    normed_attn_grad = attn_in_grad * gain_attn
    input_grad = hidden_grad + attn_scale * (
        normed_attn_grad
        - attn_normed * jnp.mean(normed_attn_grad * attn_normed, axis=-1, keepdims=True)
    )
    dense_part = (
        query_w_grad,
        key_w_grad,
        value_w_grad,
        out_w_grad,
        gain_attn_grad,
        gain_moe_grad,
        router_grad,
    )
    return (input_grad, dense_part, (gate_w_grad, up_w_grad, down_w_grad))


def on_device(
    inputs,
    cotangent,
    offsets,
    routes,
    w_query,
    w_key,
    w_value,
    w_out,
    norm_attn,
    norm_moe,
    w_router,
    w_gate,
    w_up,
    w_down,
):
    first_section = lax.axis_index("section") == 0
    micro, tok_rows, width = inputs.shape
    dense_weights = (
        w_query[0],
        w_key[0],
        w_value[0],
        w_out[0],
        norm_attn[0].astype(jnp.float32),
        norm_moe[0].astype(jnp.float32),
        w_router[0],
    )
    expert_weights = (
        lax.all_gather(w_gate[0], "dp", axis=1, tiled=True),
        lax.all_gather(w_up[0], "dp", axis=1, tiled=True),
        lax.all_gather(w_down[0], "dp", axis=1, tiled=True),
    )
    carried = jnp.zeros((tok_rows, width), jnp.bfloat16)
    produced_list, saved_list = ([], [])
    for moment in range(micro + 1):
        early_batch = min(moment, micro - 1)
        late_batch = max(moment - 1, 0)
        fresh = inputs[early_batch]
        layer_input = jnp.where(first_section, fresh, carried).astype(jnp.float32)
        seq_offsets = jnp.where(first_section, offsets[early_batch], offsets[late_batch])
        route_ids = jnp.where(first_section, routes[0, early_batch], routes[0, late_batch])
        layer_output, saved = forward_layer(
            layer_input, seq_offsets, route_ids, dense_weights, expert_weights
        )
        sent = layer_output.astype(jnp.bfloat16)
        produced_list.append(sent)
        saved_list.append(saved)
        if moment < micro:
            carried = passed_along(sent, "section", 1)
    acts = jnp.stack(
        [
            jnp.where(first_section, produced_list[batch_index], produced_list[batch_index + 1])
            for batch_index in range(micro)
        ]
    )[None]
    carried_grad = jnp.zeros((tok_rows, width), jnp.bfloat16)
    grad_list = []
    dense_total = None
    expert_total = None
    for moment in range(micro + 1):
        saved = jax.tree.map(
            lambda lower, upper: jnp.where(first_section, lower, upper),
            saved_list[max(moment - 1, 0)],
            saved_list[min(moment + 1, micro)],
        )
        active = jnp.where(first_section, moment > 0, moment < micro)
        top_grad = cotangent[min(moment, micro - 1)]
        grad_input = jnp.where(first_section, carried_grad, top_grad).astype(jnp.float32)
        input_grad, dense_part, expert_part = backward_layer(
            grad_input, saved, dense_weights, expert_weights
        )
        dense_part = jax.tree.map(lambda value: jnp.where(active, value, 0.0), dense_part)
        expert_part = jax.tree.map(lambda value: jnp.where(active, value, 0.0), expert_part)
        sent_grad = input_grad.astype(jnp.bfloat16)
        grad_list.append(sent_grad)
        if dense_total is None:
            dense_total = dense_part
            expert_total = expert_part
        else:
            dense_total = jax.tree.map(jnp.add, dense_total, dense_part)
            expert_total = jax.tree.map(jnp.add, expert_total, expert_part)
        if moment < micro:
            carried_grad = passed_along(sent_grad, "section", -1)
    in_grads = jnp.stack(
        [
            jnp.where(first_section, grad_list[batch_index + 1], grad_list[batch_index])
            for batch_index in range(micro)
        ]
    )[None]
    dense_total = lax.psum(dense_total, ("dp", "expert"))
    gate_grad, up_grad, down_grad = jax.tree.map(
        lambda part: part.astype(jnp.float32),
        lax.psum_scatter(shortened(expert_total), "dp", scatter_dimension=1, tiled=True),
    )
    query_grad, key_grad, value_grad, out_grad, attn_gain_grad, moe_gain_grad, router_grad = (
        dense_total
    )
    return (
        acts,
        in_grads,
        query_grad[None],
        key_grad[None],
        value_grad[None],
        out_grad[None],
        attn_gain_grad[None],
        moe_gain_grad[None],
        router_grad[None],
        gate_grad[None],
        up_grad[None],
        down_grad[None],
    )


def solution(mesh):
    return jax.shard_map(
        on_device,
        mesh=mesh,
        in_specs=(
            P(None, ("dp", "expert"), None),
            P(None, ("dp", "expert"), None),
            P(None, ("dp", "expert")),
            P("section", None, ("dp", "expert"), None),
            P("section", None, None),
            P("section", None, None),
            P("section", None, None),
            P("section", None, None),
            P("section", None),
            P("section", None),
            P("section", None, None),
            P("section", "expert", "dp", None),
            P("section", "expert", "dp", None),
            P("section", "expert", "dp", None),
        ),
        out_specs=(
            P("section", None, ("dp", "expert"), None),
            P("section", None, ("dp", "expert"), None),
            P("section", None, None),
            P("section", None, None),
            P("section", None, None),
            P("section", None, None),
            P("section", None),
            P("section", None),
            P("section", None, None),
            P("section", "expert", "dp", None),
            P("section", "expert", "dp", None),
            P("section", "expert", "dp", None),
        ),
        check_vma=False,
    )
```

profile of v0, /device:TPU:1, one launch (start us, length us, event | category | flops | bytes accessed | tf_op | source)
XLA Modules:
  0.0 2385.6 jit_solution(15323992603110662444)
XLA Ops:
  30.7 9.0 reduce-window.24
  40.2 9.0 reduce-window.20
  49.7 9.0 reduce-window.26
  69.1 10.0 fusion.18
  79.1 9.2 fusion.15
  88.3 24.3 %all-gather.13.cloned.1.call-done = bf16[2048,512]{1,0:T(8,128)(2,1)} async-done(((bf16[128,512]{1,0:T(8,128)(2,1)}), bf16[2048,512]{1,0:T(8,128)(2,1)}) %all-gather.13.cloned.1.call-update) | async-done | bytes 2097168 | tf_op jit(solution)/shard_map/all_gather | solution.py:99
  116.5 9.5 fusion.182
  127.6 14.2 scatter_custom_fusion
  156.8 27.6 %all-to-all-done = bf16[16,2,33,1024]{3,1,2,0:T(2,128)(2,1)} async-done(((bf16[16,2,33,1024]{3,1,2,0:T(2,128)(2,1)}), bf16[16,2,33,1024]{3,1,2,0:T(2,128)(2,1)}, u32[]{:S(2)}, u32[]{:S(2)}) %all-to-all-start) | async-done | bytes 2162720 | tf_op jit(solution)/shard_map/all_to_all | solution.py:129
  211.6 7.0 gather_fusion.6
  219.0 25.1 %all-to-all-done.1 = bf16[1,2,528,1024]{3,1,0,2:T(2,128)(2,1)} async-done(((bf16[1,2,528,1024]{3,1,0,2:T(2,128)(2,1)}), bf16[1,2,528,1024]{3,1,0,2:T(2,128)(2,1)}, u32[]{:S(2)}, u32[]{:S(2)}) %all-to-all-start.1) | async-done | bytes 2162720 | tf_op jit(solution)/shard_map/all_to_all | solution.py:136
  252.2 7.9 gather_fusion
  277.8 37.5 %all-gather.19.cloned.1.call-done = bf16[2048,512]{1,0:T(8,128)(2,1)} async-done(((bf16[128,512]{1,0:T(8,128)(2,1)}), bf16[2048,512]{1,0:T(8,128)(2,1)}) %all-gather.19.cloned.1.call-update) | async-done | bytes 2097168 | tf_op jit(solution)/shard_map/all_gather | solution.py:98
  319.6 10.0 fusion.19
  329.7 9.2 fusion.16
  338.9 23.7 all-gather.17.cloned.1.call-done
  366.5 9.4 fusion.181
  377.5 14.5 scatter_custom_fusion.1
  400.2 32.4 %all_to_all.180 = bf16[16,2,33,1024]{3,1,2,0:T(2,128)(2,1)S(1)} all-to-all(bf16[16,2,33,1024]{3,1,2,0:T(2,128)(2,1)S(1)} %copy.469), channel_id=1, replica_groups=mesh['section'=2,'dp'=4,'expert'=16] {'expert'}, dimensions={0} | all-to-all | bytes 4325376 | tf_op jit(solution)/shard_map/all_to_all | solution.py:129
  458.5 15.8 all-to-all-done.3
  482.3 8.0 gather_fusion.1
  501.4 7.7 scatter_custom_fusion.3
  518.7 8.0 all-to-all-start.6
  530.2 23.5 all-to-all-done.6
  566.7 7.4 all-to-all-start.7
  578.7 30.9 %all-to-all-done.7 = bf16[1,2,528,1024]{3,1,0,2:T(2,128)(2,1)} async-done(((bf16[1,2,528,1024]{3,1,0,2:T(2,128)(2,1)}), bf16[1,2,528,1024]{3,1,0,2:T(2,128)(2,1)}, u32[]{:S(2)}, u32[]{:S(2)}) %all-to-all-start.7) | async-done | bytes 2162720 | tf_op jit(solution)/shard_map/all_to_all | solution.py:238
  617.8 7.9 gather_fusion.3
  634.6 10.1 fusion.20
  644.7 9.3 fusion.17
  658.0 9.7 fusion.180
  678.2 9.8 fusion.303
  695.5 13.1 fusion.10
  708.6 12.5 fusion.12
  729.1 14.3 scatter_custom_fusion.2
  758.8 10.4 bitcast_convert_fusion.2
  782.9 8.8 all-to-all-done.4
  811.9 22.5 reduce-scatter.28.cloned.1.call-done
  838.9 75.2 %reduce-scatter.30.cloned.1.call-done = bf16[128,512]{1,0:T(8,128)(2,1)} async-done(((bf16[2048,512]{1,0:T(8,128)(2,1)}), bf16[128,512]{1,0:T(8,128)(2,1)}) %reduce-scatter.30.cloned.1.call-update) | async-done | bytes 131088
  934.6 7.9 gather_fusion.2
  947.0 7.5 scatter_custom_fusion.4
  962.9 31.4 %all_to_all.181 = bf16[16,2,33,1024]{3,1,2,0:T(2,128)(2,1)S(1)} all-to-all(bf16[16,2,33,1024]{3,1,2,0:T(2,128)(2,1)S(1)} %copy.503), channel_id=1, replica_groups=mesh['section'=2,'dp'=4,'expert'=16] {'expert'}, dimensions={0} | all-to-all | bytes 4325376 | tf_op jit(solution)/shard_map/all_to_all | solution.py:212
  1016.5 9.7 fusion.304
  1026.2 7.4 all-to-all-done.9
  1041.7 7.9 gather_fusion.4
  1058.1 12.2 fusion.5
  1070.3 12.3 fusion.7
  1090.7 10.3 bitcast_convert_fusion.1
  1114.1 55.8 %reduce-scatter.32.cloned.1.call-done = bf16[128,512]{1,0:T(8,128)(2,1)} async-done(((bf16[2048,512]{1,0:T(8,128)(2,1)}), bf16[128,512]{1,0:T(8,128)(2,1)}) %reduce-scatter.32.cloned.1.call-update) | async-done | bytes 131088
  1173.6 74.1 %reduce-scatter.34.cloned.1.call-done = bf16[128,512]{1,0:T(8,128)(2,1)} async-done(((bf16[2048,512]{1,0:T(8,128)(2,1)}), bf16[128,512]{1,0:T(8,128)(2,1)}) %reduce-scatter.34.cloned.1.call-update) | async-done | bytes 131088
  1266.5 7.5 scatter_custom_fusion.5
  1282.4 30.3 %all_to_all.182 = bf16[16,2,33,1024]{3,1,2,0:T(2,128)(2,1)S(1)} all-to-all(bf16[16,2,33,1024]{3,1,2,0:T(2,128)(2,1)S(1)} %copy.516), channel_id=1, replica_groups=mesh['section'=2,'dp'=4,'expert'=16] {'expert'}, dimensions={0} | all-to-all | bytes 4325376 | tf_op jit(solution)/shard_map/all_to_all | solution.py:212
  1334.8 9.7 fusion.305
  1344.6 7.3 all-to-all-done.11
  1360.0 7.9 gather_fusion.5
  1375.8 14.4 fusion
  1390.2 12.3 fusion.2
  1410.7 10.3 bitcast_convert_fusion
  1434.4 7.3 broadcast_select_fusion
  1509.0 54.6 %reduce-scatter.38.cloned.1.call-done = bf16[128,512]{1,0:T(8,128)(2,1)} async-done(((bf16[2048,512]{1,0:T(8,128)(2,1)}), bf16[128,512]{1,0:T(8,128)(2,1)}) %reduce-scatter.38.cloned.1.call-update) | async-done | bytes 131088
  1573.0 32.4 %reduce-scatter.26.cloned.1.call-done = bf16[2,256,512]{2,1,0:T(8,128)(2,1)} async-done(((bf16[2,1024,512]{2,1,0:T(8,128)(2,1)}), bf16[2,256,512]{2,1,0:T(8,128)(2,1)}) %reduce-scatter.26.cloned.1.call-update) | async-done | bytes 524304 | tf_op jit(solution)/shard_map/reduce_scatter | solution.py:445
  1607.5 38.3 %reduce-scatter.24.cloned.1.call-done = bf16[2,256,512]{2,1,0:T(8,128)(2,1)} async-done(((bf16[2,1024,512]{2,1,0:T(8,128)(2,1)}), bf16[2,256,512]{2,1,0:T(8,128)(2,1)}) %reduce-scatter.24.cloned.1.call-update) | async-done | bytes 524304 | tf_op jit(solution)/shard_map/reduce_scatter | solution.py:445
  1647.9 38.1 %reduce-scatter.22.cloned.1.call-done = bf16[2,256,512]{2,1,0:T(8,128)(2,1)} async-done(((bf16[2,1024,512]{2,1,0:T(8,128)(2,1)}), bf16[2,256,512]{2,1,0:T(8,128)(2,1)}) %reduce-scatter.22.cloned.1.call-update) | async-done | bytes 524304 | tf_op jit(solution)/shard_map/reduce_scatter | solution.py:445
  1691.3 137.4 %all-reduce = (f32[1,1024]{1,0:T(1,128)}, f32[1,1024]{1,0:T(1,128)}) all-reduce(f32[1,1024]{1,0:T(1,128)S(1)} %bitcast.1100, f32[1,1024]{1,0:T(1,128)S(1)} %bitcast.1099), channel_id=1, replica_groups=mesh['section'=2,'dp'=4,'expert'=16] {'dp','expert'}, use_global_device_ids=true, to_apply=%region_70.72 | all-reduce | flops 2048 | bytes 16384 | tf_op jit(solution)/shard_map/psum | solution.py:442
  1831.0 534.8 %all-reduce.4.cloned.1.call-done = (f32[1,1024,1024]{2,1,0:T(8,128)}, f32[1,1024,512]{2,1,0:T(8,128)}, f32[1,1024,512]{2,1,0:T(8,128)}, f32[1,1024,1024]{2,1,0:T(8,128)}, f32[1,1024,32]{1,2,0:T(8,128)}) async-done(((f32[1,1024,1024]{2,1,0:T(8,128)}, f32[1,1024,512]{2,1,0:T(8,128)}, f32[1,1024,512]{2,1,0:T(8,128)}, f32[1,1024,1024]{2,1,0:T(8,128)}, f32[1,1024,32]{1,2,0:T(8,128)}), ...) | async-done | bytes 12714000 | tf_op jit(solution)/shard_map/psum | solution.py:442
  (878 shorter events, 585.2 us)
Async XLA Ops:
  7.2 118.9 %copy-start = (bf16[1,1024,1024]{2,1,0:T(8,128)(2,1)S(1)}, bf16[1,1024,1024]{2,1,0:T(8,128)(2,1)}, u32[]{:S(2)}) copy-start(bf16[1,1024,1024]{2,1,0:T(8,128)(2,1)} %param.23) | copy-start | bytes 6291460
  7.2 57.9 %all-gather.15.cloned.1.call-start = ((), (), s32[]{:S(2)}) async-start(), calls=%async_computation.22 | async-start | bytes 2228224 | tf_op jit(solution)/shard_map/all_gather | solution.py:98
  17.5 95.1 %all-gather.13.cloned.1.call-start = ((), (), s32[]{:S(2)}) async-start(), calls=%async_computation.21 | async-start | bytes 2228224 | tf_op jit(solution)/shard_map/all_gather | solution.py:99
  19.8 137.0 %all-gather.25.cloned.1.call-start = ((), (), s32[]{:S(2)}) async-start(), calls=%async_computation.30 | async-start | bytes 2621440 | tf_op jit(solution)/shard_map/all_gather | solution.py:381
  20.5 168.8 %all-gather.27.cloned.1.call-start = ((), (), s32[]{:S(2)}) async-start(), calls=%async_computation.31 | async-start | bytes 2621440 | tf_op jit(solution)/shard_map/all_gather | solution.py:382
  59.8 67.7 %copy-start.215 = (s32[1024]{0:T(1024)}, s32[1024]{0:T(1024)S(1)}, u32[]{:S(2)}) copy-start(s32[1024]{0:T(1024)S(1)} %broadcast_clamp_fusion.6) | copy-start | bytes 12292
  79.1 37.4 %copy-start.168 = (f32[8,2,128]{2,1,0:T(2,128)}, f32[8,2,128]{2,1,0:T(2,128)S(1)}, u32[]{:S(2)}) copy-start(f32[8,2,128]{2,1,0:T(2,128)S(1)} %get-tuple-element.169) | copy-start | bytes 24580
  88.3 37.8 %copy-start.183 = (f32[8,2,128]{2,1,0:T(2,128)}, f32[8,2,128]{2,1,0:T(2,128)S(1)}, u32[]{:S(2)}) copy-start(f32[8,2,128]{2,1,0:T(2,128)S(1)} %fusion.15) | copy-start | bytes 24580
  127.6 83.9 %copy-start.100 = (bf16[128,1024]{1,0:T(8,128)(2,1)}, bf16[128,1024]{1,0:T(8,128)(2,1)S(1)}, u32[]{:S(2)}) copy-start(bf16[128,1024]{1,0:T(8,128)(2,1)S(1)} %multiply_convert_fusion.11) | copy-start | bytes 786436
  151.5 32.9 %all-to-all-start = ((bf16[16,2,33,1024]{3,1,2,0:T(2,128)(2,1)}), bf16[16,2,33,1024]{3,1,2,0:T(2,128)(2,1)}, u32[]{:S(2)}, u32[]{:S(2)}) async-start(bf16[16,2,33,1024]{3,1,2,0:T(2,128)(2,1)} %copy.452), calls=%async_computation | async-start | bytes 4325376 | tf_op jit(solution)/shard_map/all_to_all | solution.py:129
  156.2 40.6 %all-gather.29.cloned.1.call-start = ((), (), s32[]{:S(2)}) async-start(), calls=%async_computation.32 | async-start | bytes 2621440 | tf_op jit(solution)/shard_map/all_gather | solution.py:383
  203.7 40.4 %all-to-all-start.1 = ((bf16[1,2,528,1024]{3,1,0,2:T(2,128)(2,1)}), bf16[1,2,528,1024]{3,1,0,2:T(2,128)(2,1)}, u32[]{:S(2)}, u32[]{:S(2)}) async-start(bf16[1,2,528,1024]{3,1,0,2:T(2,128)(2,1)} %copy.455), calls=%async_computation.1 | async-start | bytes 4325376 | tf_op jit(solution)/shard_map/all_to_all | solution.py:136
  210.5 104.8 %all-gather.19.cloned.1.call-start = ((), (), s32[]{:S(2)}) async-start(), calls=%async_computation.24 | async-start | bytes 2228224 | tf_op jit(solution)/shard_map/all_gather | solution.py:98
  218.9 281.8 %copy-start.179 = (f32[128,8]{0,1:T(8,128)}, f32[128,8]{0,1:T(8,128)S(1)}, u32[]{:S(2)}) copy-start(f32[128,8]{0,1:T(8,128)S(1)} %fusion.333) | copy-start | bytes 12292
  263.2 5.8 collective-permute-start
  269.2 106.8 %copy-start.6 = (bf16[128,1024]{1,0:T(8,128)(2,1)}, bf16[128,1024]{1,0:T(8,128)(2,1)S(1)}, u32[]{:S(2)}) copy-start(bf16[128,1024]{1,0:T(8,128)(2,1)S(1)} %get-tuple-element.62) | copy-start | bytes 786436
  272.2 90.4 %all-gather.17.cloned.1.call-start = ((), (), s32[]{:S(2)}) async-start(), calls=%async_computation.23 | async-start | bytes 2228224 | tf_op jit(solution)/shard_map/all_gather | solution.py:99
  277.8 51.9 %copy-start.13 = (bf16[128,16,64]{0,2,1:T(8,128)(2,1)}, bf16[128,16,64]{0,2,1:T(8,128)(2,1)S(1)}, u32[]{:S(2)}) copy-start(bf16[128,16,64]{0,2,1:T(8,128)(2,1)S(1)} %fusion.231) | copy-start | bytes 786436
  376.6 252.1 %copy-start.207 = (f32[128]{0:T(128)}, f32[128]{0:T(128)S(1)}, u32[]{:S(2)}) copy-start(f32[128]{0:T(128)S(1)} %add_rsqrt_fusion.2) | copy-start | bytes 1540
  377.4 72.8 %copy-start.97 = (bf16[128,1024]{1,0:T(8,128)(2,1)}, bf16[128,1024]{1,0:T(8,128)(2,1)S(1)}, u32[]{:S(2)}) copy-start(bf16[128,1024]{1,0:T(8,128)(2,1)S(1)} %multiply_convert_fusion.10) | copy-start | bytes 786436
  443.7 30.6 %all-to-all-start.3 = ((bf16[1,2,528,1024]{3,1,0,2:T(2,128)(2,1)}), bf16[1,2,528,1024]{3,1,0,2:T(2,128)(2,1)}, u32[]{:S(2)}, u32[]{:S(2)}) async-start(bf16[1,2,528,1024]{3,1,0,2:T(2,128)(2,1)} %copy.472), calls=%async_computation.3 | async-start | bytes 4325376 | tf_op jit(solution)/shard_map/all_to_all | solution.py:136
  457.7 42.9 %copy-start.160 = (f32[128,8]{0,1:T(8,128)}, f32[128,8]{0,1:T(8,128)S(1)}, u32[]{:S(2)}) copy-start(f32[128,8]{0,1:T(8,128)S(1)} %get-tuple-element.60) | copy-start | bytes 12292
  457.7 42.9 %copy-start.198 = (f32[128]{0:T(128)}, f32[128]{0:T(128)S(1)}, u32[]{:S(2)}) copy-start(f32[128]{0:T(128)S(1)} %get-tuple-element.59) | copy-start | bytes 1540
  457.7 42.9 %copy-start.204 = (f32[128]{0:T(128)}, f32[128]{0:T(128)S(1)}, u32[]{:S(2)}) copy-start(f32[128]{0:T(128)S(1)} %fusion.336) | copy-start | bytes 1540
  496.1 30.5 %collective-permute-start.1 = (bf16[128,1024]{1,0:T(8,128)(2,1)}, bf16[128,1024]{1,0:T(8,128)(2,1)}, u32[]{:S(2)}, u32[]{:S(2)}) collective-permute-start(bf16[128,1024]{1,0:T(8,128)(2,1)} %get-tuple-element.45), channel_id=1, source_target_pairs={{0,64},{1,65},{2,66},{3,67},{4,68},{5,69},{6,70},{7,71},{8,72},{9,... | collective-permute-start | bytes 786440 | tf_op jit(solution)/shard_map/ppermute | solution.py:17
  518.7 35.0 %all-to-all-start.6 = ((bf16[16,2,33,1024]{3,1,2,0:T(2,128)(2,1)}), bf16[16,2,33,1024]{3,1,2,0:T(2,128)(2,1)}, u32[]{:S(2)}, u32[]{:S(2)}) async-start(bf16[16,2,33,1024]{3,1,2,0:T(2,128)(2,1)} %copy.490), calls=%async_computation.6 | async-start | bytes 4325376 | tf_op jit(solution)/shard_map/all_to_all | solution.py:212
  526.6 104.0 %all-gather.23.cloned.1.call-start = ((), (), s32[]{:S(2)}) async-start(), calls=%async_computation.26 | async-start | bytes 2228224 | tf_op jit(solution)/shard_map/all_gather | solution.py:98
  526.9 140.9 %copy-start.4 = (bf16[128,1024]{1,0:T(8,128)(2,1)}, bf16[128,1024]{1,0:T(8,128)(2,1)S(1)}, u32[]{:S(2)}) copy-start(bf16[128,1024]{1,0:T(8,128)(2,1)S(1)} %get-tuple-element.58) | copy-start | bytes 786436
  527.6 48.6 %copy-start.162 = (f32[128]{0:T(128)}, f32[128]{0:T(128)S(1)}, u32[]{:S(2)}) copy-start(f32[128]{0:T(128)S(1)} %get-tuple-element.150) | copy-start | bytes 1540
  566.7 43.0 %all-to-all-start.7 = ((bf16[1,2,528,1024]{3,1,0,2:T(2,128)(2,1)}), bf16[1,2,528,1024]{3,1,0,2:T(2,128)(2,1)}, u32[]{:S(2)}, u32[]{:S(2)}) async-start(bf16[1,2,528,1024]{3,1,0,2:T(2,128)(2,1)} %copy.492), calls=%async_computation.7 | async-start | bytes 4325376 | tf_op jit(solution)/shard_map/all_to_all | solution.py:238
  574.2 79.9 %all-gather.21.cloned.1.call-start = ((), (), s32[]{:S(2)}) async-start(), calls=%async_computation.25 | async-start | bytes 2228224 | tf_op jit(solution)/shard_map/all_gather | solution.py:99
  575.3 259.1 %reduce-scatter.28.cloned.1.call-start = ((), (), s32[]{:S(2)}) async-start(), calls=%async_computation.33 | async-start | bytes 2228224
  576.1 52.6 %copy-start.166 = (bf16[128,32]{0,1:T(8,128)(2,1)}, bf16[128,32]{0,1:T(8,128)(2,1)S(1)}, u32[]{:S(2)}) copy-start(bf16[128,32]{0,1:T(8,128)(2,1)S(1)} %select_reduce_fusion.2) | copy-start | bytes 24580
  578.7 55.9 %copy-start.18 = (bf16[128,16,64]{0,2,1:T(8,128)(2,1)}, bf16[128,16,64]{0,2,1:T(8,128)(2,1)S(1)}, u32[]{:S(2)}) copy-start(bf16[128,16,64]{0,2,1:T(8,128)(2,1)S(1)} %fusion.233) | copy-start | bytes 786436
  688.9 40.1 %copy-start.94 = (bf16[128,1024]{1,0:T(8,128)(2,1)}, bf16[128,1024]{1,0:T(8,128)(2,1)S(1)}, u32[]{:S(2)}) copy-start(bf16[128,1024]{1,0:T(8,128)(2,1)S(1)} %get-tuple-element.141) | copy-start | bytes 786436
  753.0 38.7 %all-to-all-start.4 = ((bf16[16,2,33,1024]{3,1,2,0:T(2,128)(2,1)}), bf16[16,2,33,1024]{3,1,2,0:T(2,128)(2,1)}, u32[]{:S(2)}, u32[]{:S(2)}) async-start(bf16[16,2,33,1024]{3,1,2,0:T(2,128)(2,1)} %copy.484), calls=%async_computation.4 | async-start | bytes 4325376 | tf_op jit(solution)/shard_map/all_to_all | solution.py:129
  758.6 155.5 %reduce-scatter.30.cloned.1.call-start = ((), (), s32[]{:S(2)}) async-start(), calls=%async_computation.34 | async-start | bytes 2228224
  774.0 61.6 %copy-start.145 = (f32[128,64]{0,1:T(8,128)}, f32[128,64]{0,1:T(8,128)S(1)}, u32[]{:S(2)}) copy-start(f32[128,64]{0,1:T(8,128)S(1)} %get-tuple-element.116) | copy-start | bytes 98308
  806.7 119.8 %all-to-all-start.5 = ((bf16[1,2,528,1024]{3,1,0,2:T(2,128)(2,1)}), bf16[1,2,528,1024]{3,1,0,2:T(2,128)(2,1)}, u32[]{:S(2)}, u32[]{:S(2)}) async-start(bf16[1,2,528,1024]{3,1,0,2:T(2,128)(2,1)} %copy.487), calls=%async_computation.5 | async-start | bytes 4325376 | tf_op jit(solution)/shard_map/all_to_all | solution.py:136
  835.4 78.7 %copy-start.7 = (bf16[128,1024]{1,0:T(8,128)(2,1)S(1)}, bf16[128,1024]{1,0:T(8,128)(2,1)}, u32[]{:S(2)}) copy-start(bf16[128,1024]{1,0:T(8,128)(2,1)} %copy-done.6) | copy-start | bytes 786436
  835.4 78.7 %copy-start.21 = (bf16[2,128,1024]{2,1,0:T(8,128)(2,1)S(1)}, bf16[2,128,1024]{2,1,0:T(8,128)(2,1)}, u32[]{:S(2)}) copy-start(bf16[2,128,1024]{2,1,0:T(8,128)(2,1)} %param.16) | copy-start | bytes 1572868
  835.4 78.7 %copy-start.173 = (f32[128]{0:T(128)S(1)}, f32[128]{0:T(128)}, u32[]{:S(2)}) copy-start(f32[128]{0:T(128)} %copy-done.172) | copy-start | bytes 1540
  835.4 78.7 %copy-start.182 = (f32[128]{0:T(128)S(1)}, f32[128]{0:T(128)}, u32[]{:S(2)}) copy-start(f32[128]{0:T(128)} %copy-done.181) | copy-start | bytes 1540
  836.2 80.5 %copy-start.229 = (f32[128]{0:T(128)S(1)}, f32[128]{0:T(128)}, u32[]{:S(2)}) copy-start(f32[128]{0:T(128)} %get-tuple-element.151) | copy-start | bytes 1540
  838.9 80.2 %copy-start.95 = (bf16[128,1024]{1,0:T(8,128)(2,1)S(1)}, bf16[128,1024]{1,0:T(8,128)(2,1)}, u32[]{:S(2)}) copy-start(bf16[128,1024]{1,0:T(8,128)(2,1)} %copy-done.94) | copy-start | bytes 786436
  917.8 24.7 %collective-permute-start.2 = (bf16[128,1024]{1,0:T(8,128)(2,1)}, bf16[128,1024]{1,0:T(8,128)(2,1)}, u32[]{:S(2)}, u32[]{:S(2)}) collective-permute-start(bf16[128,1024]{1,0:T(8,128)(2,1)} %add_convert_fusion.8), channel_id=1, source_target_pairs={{64,0},{65,1},{66,2},{67,3},{68,4},{69,5},{70,6},{71,7},{72,8},{73... | collective-permute-start | bytes 786440 | tf_op jit(solution)/shard_map/ppermute | solution.py:17
  1003.8 29.8 %all-to-all-start.9 = ((bf16[1,2,528,1024]{3,1,0,2:T(2,128)(2,1)}), bf16[1,2,528,1024]{3,1,0,2:T(2,128)(2,1)}, u32[]{:S(2)}, u32[]{:S(2)}) async-start(bf16[1,2,528,1024]{3,1,0,2:T(2,128)(2,1)} %copy.505), calls=%async_computation.9 | async-start | bytes 4325376 | tf_op jit(solution)/shard_map/all_to_all | solution.py:238
  1008.3 161.6 %reduce-scatter.32.cloned.1.call-start = ((), (), s32[]{:S(2)}) async-start(), calls=%async_computation.35 | async-start | bytes 2228224
  1090.6 157.1 %reduce-scatter.34.cloned.1.call-start = ((), (), s32[]{:S(2)}) async-start(), calls=%async_computation.36 | async-start | bytes 2228224
  1171.0 76.7 %copy-start.5 = (bf16[128,1024]{1,0:T(8,128)(2,1)S(1)}, bf16[128,1024]{1,0:T(8,128)(2,1)}, u32[]{:S(2)}) copy-start(bf16[128,1024]{1,0:T(8,128)(2,1)} %copy-done.4) | copy-start | bytes 786436
  1171.0 76.7 %copy-start.163 = (f32[128]{0:T(128)S(1)}, f32[128]{0:T(128)}, u32[]{:S(2)}) copy-start(f32[128]{0:T(128)} %copy-done.162) | copy-start | bytes 1540
  1172.3 78.0 %copy-start.125 = (bf16[128,512]{0,1:T(8,128)(2,1)}, bf16[128,512]{0,1:T(8,128)(2,1)S(1)}, u32[]{:S(2)}) copy-start(bf16[128,512]{0,1:T(8,128)(2,1)S(1)} %fusion.256) | copy-start | bytes 393220
  1172.3 78.0 %copy-start.218 = (f32[128]{0:T(128)S(1)}, f32[128]{0:T(128)}, u32[]{:S(2)}) copy-start(f32[128]{0:T(128)} %get-tuple-element.152) | copy-start | bytes 1540
  1251.4 7.6 collective-permute-start.3
  1322.2 29.7 %all-to-all-start.11 = ((bf16[1,2,528,1024]{3,1,0,2:T(2,128)(2,1)}), bf16[1,2,528,1024]{3,1,0,2:T(2,128)(2,1)}, u32[]{:S(2)}, u32[]{:S(2)}) async-start(bf16[1,2,528,1024]{3,1,0,2:T(2,128)(2,1)} %copy.518), calls=%async_computation.11 | async-start | bytes 4325376 | tf_op jit(solution)/shard_map/all_to_all | solution.py:238
  1326.7 177.7 %reduce-scatter.36.cloned.1.call-start = ((), (), s32[]{:S(2)}) async-start(), calls=%async_computation.37 | async-start | bytes 2228224
  1410.6 153.1 %reduce-scatter.38.cloned.1.call-start = ((), (), s32[]{:S(2)}) async-start(), calls=%async_computation.38 | async-start | bytes 2228224
  1424.9 180.4 %reduce-scatter.26.cloned.1.call-start = ((), (), s32[]{:S(2)}) async-start(), calls=%async_computation.29 | async-start | bytes 2621440 | tf_op jit(solution)/shard_map/reduce_scatter | solution.py:445
  1434.3 211.4 %reduce-scatter.24.cloned.1.call-start = ((), (), s32[]{:S(2)}) async-start(), calls=%async_computation.28 | async-start | bytes 2621440 | tf_op jit(solution)/shard_map/reduce_scatter | solution.py:445
  1449.2 236.9 %reduce-scatter.22.cloned.1.call-start = ((), (), s32[]{:S(2)}) async-start(), calls=%async_computation.27 | async-start | bytes 2621440 | tf_op jit(solution)/shard_map/reduce_scatter | solution.py:445
  1482.9 883.0 %all-reduce.4.cloned.1.call-start = ((), (), s32[]{:S(2)}) async-start(), calls=%async_computation.39 | async-start | bytes 25427968 | tf_op jit(solution)/shard_map/psum | solution.py:442
  1688.4 140.4 %copy-start.64 = (f32[128,1024]{1,0:T(8,128)S(1)}, f32[128,1024]{1,0:T(8,128)}, u32[]{:S(2)}) copy-start(f32[128,1024]{1,0:T(8,128)} %copy-done.62) | copy-start | bytes 1572868
  1688.4 140.4 %copy-start.228 = (f32[128]{0:T(128)S(1)}, f32[128]{0:T(128)}, u32[]{:S(2)}) copy-start(f32[128]{0:T(128)} %get-tuple-element.149) | copy-start | bytes 1540
  1690.0 140.2 %copy-start.137 = (bf16[1,128,1024]{2,1,0:T(8,128)(2,1)S(1)}, bf16[1,128,1024]{2,1,0:T(8,128)(2,1)}, u32[]{:S(2)}) copy-start(bf16[1,128,1024]{2,1,0:T(8,128)(2,1)} %get-tuple-element.36) | copy-start | bytes 786436
  (210 other events, 1344.0 us)
Sparse Core Ops, SparseCore 0:
  17.6 47.4 all-gather.14
  67.9 44.6 all-gather.12
  114.3 27.3 all-gather.24
  143.2 26.0 all-gather.26
  170.8 26.0 all-gather.28
  272.3 42.9 all-gather.18
  318.1 44.5 all-gather.16
  530.3 68.6 all-gather.22
  601.7 49.3 all-gather.20
  729.2 105.1 reduce-scatter.27
  838.0 76.0 reduce-scatter.29
  1090.7 79.1 reduce-scatter.31
  1174.1 73.5 reduce-scatter.33
  1410.7 75.8 reduce-scatter.35
  1490.1 73.5 reduce-scatter.37
  1566.2 39.1 reduce-scatter.25
  1608.0 37.6 reduce-scatter.23
  1648.3 37.7 reduce-scatter.21
  1690.4 675.4 all-reduce.3
where the time goes:
time: 2420 us; the launch traced here: 2390 us
  waiting for transfers between devices  1170 us (48%)
  local copies, waits for them, and re-layouts  371 us (15%)
  matrix products  338 us (14%)
  blocking collectives  231 us (10%)
  other arithmetic  196 us (8%)
  starting transfers between devices  60.2 us (2%)
    psum x1, waiting for transfers between devices, on_device(): dense_total = lax.psum(dense_total, ('dp', 'expert'))  535 us
    unnamed x25, waiting for transfers between devices  284 us
    psum x1, blocking collectives, on_device(): dense_total = lax.psum(dense_total, ('dp', 'expert'))  137 us
    reduce_scatter x3, waiting for transfers between devices, on_device(): lax.psum_scatter(shortened(expert_total), 'dp', scatter_dimension=1, tile...  109 us
    unnamed x500, local copies, waits for them, and re-layouts  68.2 us
    all_to_all x2, blocking collectives, backward_layer(): lax.all_to_all(send_grad, 'expert', split_axis=0, concat_axis=2, tiled=True)  61.7 us
  transfers between devices with their start and end apart: 32, of which 24 were waited for; matrix products, arithmetic and copies ran while one was open for 22% of the time, Pallas kernels for 0%

commit v1 on v0

v1 whole, which is shorter than its diff:
```python
import jax
import jax.numpy as jnp
from jax import lax
from jax.experimental import pallas as pl
from jax.experimental.pallas import tpu as pltpu

from jax.sharding import PartitionSpec as P

HEAD = 64
MESH = pl.DeviceIdType.MESH
bf16 = jnp.bfloat16
f32 = jnp.float32
norm_eps = 1e-06
masked_score = -1e30
rope_base = 10000.0


def ring_places():
    me = lax.axis_index("expert")
    z, x = lax.div(me, 4), lax.rem(me, 4)
    xr, xl = lax.rem(x + 1, 4), lax.rem(x + 3, 4)
    zr, zl = lax.rem(z + 1, 4), lax.rem(z + 3, 4)
    near = (z * 4 + xr, z * 4 + xl, zr * 4 + x, zl * 4 + x)
    return z, x, xr, xl, zr, zl, near


def greet(near):
    barrier = pltpu.get_barrier_semaphore()
    for other in near:
        pl.semaphore_signal(barrier, inc=1, device_id={"expert": other}, device_id_type=MESH)
    pl.semaphore_wait(barrier, 4)


def gather_kernel(x_ref, out_ref, send, recv, own_sem):
    z, x, xr, xl, zr, zl, (dxr, dxl, dzr, dzl) = ring_places()
    rows = x_ref.shape[0]
    half, quarter = rows // 2, rows // 4
    own = pltpu.make_async_copy(x_ref, out_ref.at[z, x], own_sem)
    own.start()
    greet((dxr, dxl, dzr, dzl))

    def copy(i, src, dst, to):
        c = pltpu.make_async_remote_copy(
            src_ref=src, dst_ref=dst, send_sem=send.at[i], recv_sem=recv.at[i],
            device_id={"expert": to}, device_id_type=MESH)
        c.start()
        return c

    A, B = pl.ds(0, half), pl.ds(half, half)
    A0, A1 = pl.ds(0, quarter), pl.ds(quarter, quarter)
    B0, B1 = pl.ds(half, quarter), pl.ds(half + quarter, quarter)
    a_r = copy(0, x_ref.at[A], out_ref.at[z, x, A], dxr)
    a_l = copy(1, x_ref.at[A], out_ref.at[z, x, A], dxl)
    b_r = copy(2, x_ref.at[B], out_ref.at[z, x, B], dzr)
    b_l = copy(3, x_ref.at[B], out_ref.at[z, x, B], dzl)
    a_r.wait_recv()
    a2_r = copy(4, out_ref.at[z, xl, A0], out_ref.at[z, xl, A0], dxr)
    a_l.wait_recv()
    a2_l = copy(5, out_ref.at[z, xr, A1], out_ref.at[z, xr, A1], dxl)
    b_r.wait_recv()
    b2_r = copy(6, out_ref.at[zl, x, B0], out_ref.at[zl, x, B0], dzr)
    b_l.wait_recv()
    b2_l = copy(7, out_ref.at[zr, x, B1], out_ref.at[zr, x, B1], dzl)
    own.wait()
    a2_r.wait_recv()
    a2_l.wait_recv()
    c_r = copy(8, out_ref.at[z, :, A], out_ref.at[z, :, A], dzr)
    c_l = copy(9, out_ref.at[z, :, A], out_ref.at[z, :, A], dzl)
    b2_r.wait_recv()
    b2_l.wait_recv()
    d_r = copy(10, out_ref.at[:, x, B], out_ref.at[:, x, B], dxr)
    d_l = copy(11, out_ref.at[:, x, B], out_ref.at[:, x, B], dxl)
    c_r.wait_recv()
    c2_r = copy(12, out_ref.at[zl, :, A0], out_ref.at[zl, :, A0], dzr)
    c_l.wait_recv()
    c2_l = copy(13, out_ref.at[zr, :, A1], out_ref.at[zr, :, A1], dzl)
    d_r.wait_recv()
    d2_r = copy(14, out_ref.at[:, xl, B0], out_ref.at[:, xl, B0], dxr)
    d_l.wait_recv()
    d2_l = copy(15, out_ref.at[:, xr, B1], out_ref.at[:, xr, B1], dxl)
    for c in (c2_r, c2_l, d2_r, d2_l):
        c.wait_recv()
    for c in (a_r, a_l, b_r, b_l, a2_r, a2_l, b2_r, b2_l, c_r, c_l, d_r, d_l, c2_r, c2_l, d2_r, d2_l):
        c.wait_send()


def gather_rows(x, ident):
    rows, cols = x.shape
    out = pl.pallas_call(
        gather_kernel,
        out_shape=jax.ShapeDtypeStruct((4, 4, rows, cols), x.dtype),
        in_specs=[pl.BlockSpec(memory_space=pl.ANY)],
        out_specs=pl.BlockSpec(memory_space=pl.ANY),
        scratch_shapes=[
            pltpu.SemaphoreType.DMA((16,)),
            pltpu.SemaphoreType.DMA((16,)),
            pltpu.SemaphoreType.DMA,
        ],
        compiler_params=pltpu.CompilerParams(collective_id=ident, has_side_effects=True),
        name="gather_rows",
    )(x)
    return out.reshape(16 * rows, cols)


def scatter_kernel(x_ref, out_ref, s1, l1, s2, l2, t0, m1, n1, m2, n2, send, recv):
    z, x, xr, xl, zr, zl, (dxr, dxl, dzr, dzl) = ring_places()
    x2, z2 = lax.rem(x + 2, 4), lax.rem(z + 2, 4)
    rows = x_ref.shape[2]
    half, quarter = rows // 2, rows // 4
    greet((dxr, dxl, dzr, dzl))

    def copy(i, src, dst, to):
        c = pltpu.make_async_remote_copy(
            src_ref=src, dst_ref=dst, send_sem=send.at[i], recv_sem=recv.at[i],
            device_id={"expert": to}, device_id_type=MESH)
        c.start()
        return c

    A0, A1 = pl.ds(0, quarter), pl.ds(quarter, quarter)
    B0, B1 = pl.ds(half, quarter), pl.ds(half + quarter, quarter)

    def total(*parts):
        acc = parts[0].astype(f32)
        for p in parts[1:]:
            acc = acc + p.astype(f32)
        return acc

    c0 = copy(0, x_ref.at[z2, :, A0], l1.at[0], dzr)
    c1 = copy(1, x_ref.at[z2, :, A1], l1.at[1], dzl)
    c2 = copy(2, x_ref.at[:, x2, B0], l1.at[2], dxr)
    c3 = copy(3, x_ref.at[:, x2, B1], l1.at[3], dxl)
    c4 = copy(4, x_ref.at[zr, :, A1], l2.at[0, 1], dzr)
    c5 = copy(5, x_ref.at[zl, :, A0], l2.at[1, 0], dzl)
    c6 = copy(6, x_ref.at[:, xr, B1], l2.at[2, 1], dxr)
    c7 = copy(7, x_ref.at[:, xl, B0], l2.at[3, 0], dxl)
    c0.wait_recv()
    s1[0] = total(x_ref[zr, :, A0], l1[0]).astype(s1.dtype)
    c8 = copy(8, s1.at[0], l2.at[0, 0], dzr)
    c1.wait_recv()
    s1[1] = total(x_ref[zl, :, A1], l1[1]).astype(s1.dtype)
    c9 = copy(9, s1.at[1], l2.at[1, 1], dzl)
    c2.wait_recv()
    s1[2] = total(x_ref[:, xr, B0], l1[2]).astype(s1.dtype)
    c10 = copy(10, s1.at[2], l2.at[2, 0], dxr)
    c3.wait_recv()
    s1[3] = total(x_ref[:, xl, B1], l1[3]).astype(s1.dtype)
    c11 = copy(11, s1.at[3], l2.at[3, 1], dxl)
    c4.wait_recv()
    c9.wait_recv()
    t0[0, 1] = total(x_ref[z, :, A1], l2[0, 1], l2[1, 1]).astype(t0.dtype)
    c5.wait_recv()
    c8.wait_recv()
    t0[0, 0] = total(x_ref[z, :, A0], l2[0, 0], l2[1, 0]).astype(t0.dtype)
    e0 = copy(12, t0.at[0, 0, x2], m1.at[0], dxr)
    e1 = copy(13, t0.at[0, 1, x2], m1.at[1], dxl)
    e4 = copy(14, t0.at[0, 1, xr], m2.at[0, 1], dxr)
    e5 = copy(15, t0.at[0, 0, xl], m2.at[1, 0], dxl)
    c6.wait_recv()
    c11.wait_recv()
    t0[1, 1] = total(x_ref[:, x, B1], l2[2, 1], l2[3, 1]).astype(t0.dtype)
    c7.wait_recv()
    c10.wait_recv()
    t0[1, 0] = total(x_ref[:, x, B0], l2[2, 0], l2[3, 0]).astype(t0.dtype)
    e2 = copy(16, t0.at[1, 0, z2], m1.at[2], dzr)
    e3 = copy(17, t0.at[1, 1, z2], m1.at[3], dzl)
    e6 = copy(18, t0.at[1, 1, zr], m2.at[2, 1], dzr)
    e7 = copy(19, t0.at[1, 0, zl], m2.at[3, 0], dzl)
    e0.wait_recv()
    n1[0] = total(t0[0, 0, xr], m1[0]).astype(n1.dtype)
    e8 = copy(20, n1.at[0], m2.at[0, 0], dxr)
    e1.wait_recv()
    n1[1] = total(t0[0, 1, xl], m1[1]).astype(n1.dtype)
    e9 = copy(21, n1.at[1], m2.at[1, 1], dxl)
    e2.wait_recv()
    n1[2] = total(t0[1, 0, zr], m1[2]).astype(n1.dtype)
    e10 = copy(22, n1.at[2], m2.at[2, 0], dzr)
    e3.wait_recv()
    n1[3] = total(t0[1, 1, zl], m1[3]).astype(n1.dtype)
    e11 = copy(23, n1.at[3], m2.at[3, 1], dzl)
    e4.wait_recv()
    e9.wait_recv()
    out_ref[A1] = total(t0[0, 1, x], m2[0, 1], m2[1, 1])
    e5.wait_recv()
    e8.wait_recv()
    out_ref[A0] = total(t0[0, 0, x], m2[0, 0], m2[1, 0])
    e6.wait_recv()
    e11.wait_recv()
    out_ref[B1] = total(t0[1, 1, z], m2[2, 1], m2[3, 1])
    e7.wait_recv()
    e10.wait_recv()
    out_ref[B0] = total(t0[1, 0, z], m2[2, 0], m2[3, 0])
    for c in (c0, c1, c2, c3, c4, c5, c6, c7, c8, c9, c10, c11,
              e0, e1, e2, e3, e4, e5, e6, e7, e8, e9, e10, e11):
        c.wait_send()


def scatter_sum(x, ident):
    rows, cols = x.shape[0] // 16, x.shape[1]
    q = rows // 4
    return pl.pallas_call(
        scatter_kernel,
        out_shape=jax.ShapeDtypeStruct((rows, cols), jnp.float32),
        in_specs=[pl.BlockSpec(memory_space=pltpu.VMEM)],
        out_specs=pl.BlockSpec(memory_space=pltpu.VMEM),
        scratch_shapes=[
            pltpu.VMEM((4, 4, q, cols), bf16),
            pltpu.VMEM((4, 4, q, cols), bf16),
            pltpu.VMEM((1, 1, 16, 128), bf16),
            pltpu.VMEM((4, 2, 4, q, cols), bf16),
            pltpu.VMEM((2, 2, 4, q, cols), bf16),
            pltpu.VMEM((4, q, cols), bf16),
            pltpu.VMEM((4, q, cols), bf16),
            pltpu.VMEM((4, 2, q, cols), bf16),
            pltpu.VMEM((1, 16, 128), bf16),
            pltpu.SemaphoreType.DMA((24,)),
            pltpu.SemaphoreType.DMA((24,)),
        ],
        compiler_params=pltpu.CompilerParams(
            collective_id=ident, has_side_effects=True, vmem_limit_bytes=48 << 20),
        name="scatter_sum",
    )(x.reshape(4, 4, rows, cols))


def spec(shape, index):
    return pl.BlockSpec(shape, index)


def fixed(shape):
    return pl.BlockSpec(shape, lambda *_: (0,) * len(shape), pipeline_mode=pl.Buffered(1))


def whole():
    return pl.BlockSpec(memory_space=pltpu.VMEM)


def local_call(kernel, outs, name, grid=None, in_specs=None, out_specs=None, flops=0, moved=0):
    params = pltpu.CompilerParams(vmem_limit_bytes=52 << 20)
    kinds = dict(
        out_shape=[jax.ShapeDtypeStruct(s, d) for s, d in outs],
        compiler_params=params,
        name=name,
        cost_estimate=pl.CostEstimate(flops=flops, bytes_accessed=moved, transcendentals=0),
    )
    if grid is None:
        kinds["out_specs"] = [whole()] * len(outs)
        return lambda *a: pl.pallas_call(kernel, in_specs=[whole()] * len(a), **kinds)(*a)
    return pl.pallas_call(kernel, grid=grid, in_specs=in_specs, out_specs=out_specs, **kinds)


def dot(a, b):
    return jnp.dot(a, b, preferred_element_type=f32)


def dot_t(a, b):
    return lax.dot_general(a, b, (((1,), (1,)), ((), ())), preferred_element_type=f32)


def t_dot(a, b):
    return lax.dot_general(a, b, (((0,), (0,)), ((), ())), preferred_element_type=f32)


def lanes(shape):
    return lax.broadcasted_iota(jnp.int32, shape, len(shape) - 1)


def turned(u, cosine, sine):
    chunks = []
    for c in range(u.shape[1] // 128):
        part = u[:, 128 * c : 128 * c + 128]
        low = lax.rem(lanes(part.shape), 64) < 32
        rot = jnp.where(low, -pltpu.roll(part, 96, 1), pltpu.roll(part, 32, 1))
        chunks.append(part * cosine + rot * sine)
    return jnp.concatenate(chunks, axis=1)


def rms(x):
    return lax.rsqrt(jnp.mean(x * x, axis=-1, keepdims=True) + norm_eps)


def pre_kernel(x_ref, gain_ref, cos_ref, sin_ref, wq_ref, wk_ref, wv_ref, a_ref, q_ref, kv_ref):
    x = x_ref[...].astype(f32)
    a = (x * rms(x) * gain_ref[...]).astype(bf16)
    a_ref[...] = a
    cosine, sine = cos_ref[...], sin_ref[...]
    q_ref[...] = turned(dot(a, wq_ref[...]), cosine, sine).astype(bf16)
    kv_ref[:, :512] = turned(dot(a, wk_ref[...]), cosine, sine).astype(bf16)
    kv_ref[:, 512:] = dot(a, wv_ref[...]).astype(bf16)


def head_rows(q):
    q = q.astype(f32)
    left, right = q[:, :128], q[:, 128:]
    low = lanes(left.shape) < 64
    parts = [
        jnp.where(low, left, 0.0),
        jnp.where(low, pltpu.roll(left, 64, 1), 0.0),
        jnp.where(low, 0.0, pltpu.roll(right, 64, 1)),
        jnp.where(low, 0.0, right),
    ]
    return parts


def head_lanes(p0, p1, p2, p3):
    low = lanes(p0.shape) < 64
    left = jnp.where(low, p0, pltpu.roll(p1, 64, 1))
    right = jnp.where(low, pltpu.roll(p2, 64, 1), p3)
    return jnp.concatenate([left, right], axis=1)


def attend_kernel(q_ref, k_ref, v_ref, lo_ref, hi_ref, o_ref, p_ref):
    key = lax.broadcasted_iota(jnp.int32, (128, 2048), 1)
    seen = (key >= lo_ref[...]) & (key <= hi_ref[...])
    k, v = k_ref[...], v_ref[...]
    outs = []
    for h, q in enumerate(head_rows(q_ref[...])):
        s = dot_t((q * 0.125).astype(bf16), k)
        s = jnp.where(seen, s, masked_score)
        e = jnp.exp(s - jnp.max(s, axis=-1, keepdims=True))
        p = (e * (1.0 / jnp.sum(e, axis=-1, keepdims=True))).astype(bf16)
        p_ref[0, 128 * h : 128 * h + 128, :] = p
        outs.append(dot(p, v))
    o_ref[...] = head_lanes(*outs).astype(bf16)


def attend(q, kv, lo, hi):
    return local_call(
        attend_kernel,
        [((128, 1024), bf16), ((4, 512, 2048), bf16)],
        "attend",
        grid=(4,),
        in_specs=[
            spec((128, 256), lambda i: (0, i)),
            spec((2048, 128), lambda i: (0, i)),
            spec((2048, 128), lambda i: (0, i + 4)),
            fixed((128, 1)),
            fixed((128, 1)),
        ],
        out_specs=[
            spec((128, 256), lambda i: (0, i)),
            spec((1, 512, 2048), lambda i: (i, 0, 0)),
        ],
        flops=2 * 2 * 2048 * 2048 * 128,
        moved=13 << 20,
    )(q, kv, kv, lo, hi)


def attend_back_kernel(q_ref, o_ref, do_ref, k_ref, v_ref, p_ref, dq_ref, dkv_ref):
    k, v = k_ref[...], v_ref[...]
    do = do_ref[...]
    prod = do.astype(f32) * o_ref[...].astype(f32)
    low = lanes((128, 128)) < 64
    left, right = prod[:, :128], prod[:, 128:]
    deltas = [
        jnp.sum(jnp.where(low, left, 0.0), axis=1, keepdims=True),
        jnp.sum(jnp.where(low, 0.0, left), axis=1, keepdims=True),
        jnp.sum(jnp.where(low, right, 0.0), axis=1, keepdims=True),
        jnp.sum(jnp.where(low, 0.0, right), axis=1, keepdims=True),
    ]
    do_rows = [r.astype(bf16) for r in head_rows(do)]
    q_rows = [(r * 0.125).astype(bf16) for r in head_rows(q_ref[...])]
    dqs, dss = [], []
    for h in range(4):
        dp = dot_t(do_rows[h], v)
        p = p_ref[0, 128 * h : 128 * h + 128, :].astype(f32)
        ds = (p * (dp - deltas[h])).astype(bf16)
        dss.append(ds)
        dqs.append(dot(ds, k) * 0.125)
    dq_ref[...] = head_lanes(*dqs)
    dkv_ref[:, :128] = t_dot(jnp.concatenate(dss, axis=0), jnp.concatenate(q_rows, axis=0)).astype(bf16)
    dkv_ref[:, 128:] = t_dot(p_ref[0], jnp.concatenate(do_rows, axis=0)).astype(bf16)


def attend_back(q, o, do, kv, probs):
    side = spec((128, 256), lambda i: (0, i))
    return local_call(
        attend_back_kernel,
        [((128, 1024), f32), ((2048, 1024), bf16)],
        "attend_back",
        grid=(4,),
        in_specs=[
            side,
            side,
            side,
            spec((2048, 128), lambda i: (0, i)),
            spec((2048, 128), lambda i: (0, i + 4)),
            spec((1, 512, 2048), lambda i: (i, 0, 0)),
        ],
        out_specs=[side, spec((2048, 256), lambda i: (0, i))],
        flops=4 * 2 * 2048 * 2048 * 128,
        moved=17 << 20,
    )(q, o, do, kv, kv, probs)


def post_kernel(x_ref, o_ref, wo_ref, gain_ref, h_ref, b_ref):
    h = x_ref[...].astype(f32) + dot(o_ref[...], wo_ref[...])
    h_ref[...] = h
    b_ref[...] = (h * rms(h) * gain_ref[...]).astype(bf16)


def chosen_gates(b, wr, mask):
    logits = dot(b, wr)
    chosen = mask.astype(f32) > 0.5
    top = jnp.max(jnp.where(chosen, logits, masked_score), axis=-1, keepdims=True)
    e = jnp.where(chosen, jnp.exp(jnp.where(chosen, logits - top, 0.0)), 0.0)
    return e / jnp.sum(e, axis=-1, keepdims=True)


def experts_kernel(b_ref, mask_ref, wr_ref, pick_ref, wg_ref, wu_ref, wd_ref, y_ref, gu_ref, gate_ref):
    b = b_ref[...]
    gates = chosen_gates(b, wr_ref[...], mask_ref[...])
    cols = []
    y = None
    for j in range(2):
        gate = jnp.sum(gates * pick_ref[j : j + 1, :], axis=1, keepdims=True)
        cols.append(gate)
        g = dot(b, wg_ref[j])
        u = dot(b, wu_ref[j])
        gu_ref[:, 1024 * j : 1024 * j + 512] = g.astype(bf16)
        gu_ref[:, 1024 * j + 512 : 1024 * j + 1024] = u.astype(bf16)
        inner = g * jax.nn.sigmoid(g) * u
        part = dot_t((inner * gate).astype(bf16), wd_ref[j])
        y = part if y is None else y + part
    y_ref[...] = y.astype(bf16)
    lane = lanes(gate_ref.shape)
    gate_ref[...] = jnp.where(lane == 0, cols[0], jnp.where(lane == 1, cols[1], 0.0))


TILE = 256


def tile(cols):
    return spec((TILE, cols), lambda i: (i, 0))


def experts(b_all, mask_all, wr, pick, wg, wu, wd):
    rows = b_all.shape[0]
    return local_call(
        experts_kernel,
        [((rows, 1024), bf16), ((rows, 2048), bf16), ((rows, 128), f32)],
        "experts",
        grid=(rows // TILE,),
        in_specs=[
            tile(1024),
            tile(32),
            fixed((1024, 32)),
            fixed((8, 32)),
            fixed((2, 1024, 512)),
            fixed((2, 1024, 512)),
            fixed((2, 1024, 512)),
        ],
        out_specs=[tile(1024), tile(2048), tile(128)],
        flops=6 * 2 * 2048 * 1024 * 512,
        moved=24 << 20,
    )(b_all, mask_all, wr, pick, wg, wu, wd)


def experts_back_kernel(
    dout_ref, gu_ref, gate_ref, wr_ref, pick_ref, wg_ref, wu_ref, wd_ref, db_ref, dgu_ref, in_ref, coef_ref
):
    dout = dout_ref[...]
    lane = lanes(gate_ref.shape)
    all_gates = gate_ref[...]
    db = None
    coef = None
    for j in range(2):
        gate = jnp.sum(jnp.where(lane == j, all_gates, 0.0), axis=1, keepdims=True)
        g = gu_ref[:, 1024 * j : 1024 * j + 512].astype(f32)
        u = gu_ref[:, 1024 * j + 512 : 1024 * j + 1024].astype(f32)
        back = dot(dout, wd_ref[j])
        sig = jax.nn.sigmoid(g)
        silu = g * sig
        inner = silu * u
        dgate = jnp.sum(inner * back, axis=1, keepdims=True)
        in_ref[:, 512 * j : 512 * j + 512] = (inner * gate).astype(bf16)
        dinner = back * gate
        dg = (dinner * u * sig * (1.0 + g * (1.0 - sig))).astype(bf16)
        du = (dinner * silu).astype(bf16)
        dgu_ref[:, 1024 * j : 1024 * j + 512] = dg
        dgu_ref[:, 1024 * j + 512 : 1024 * j + 1024] = du
        part = dot_t(dg, wg_ref[j]) + dot_t(du, wu_ref[j])
        share = gate * dgate * pick_ref[j : j + 1, :]
        db = part if db is None else db + part
        coef = share if coef is None else coef + share
    coef = coef.astype(bf16)
    coef_ref[...] = coef
    db_ref[...] = (db + dot_t(coef, wr_ref[...])).astype(bf16)


def experts_back(dout_all, gu, gate, wr, pick, wg, wu, wd):
    rows = dout_all.shape[0]
    return local_call(
        experts_back_kernel,
        [((rows, 1024), bf16), ((rows, 2048), bf16), ((rows, 1024), bf16), ((rows, 32), bf16)],
        "experts_back",
        grid=(rows // TILE,),
        in_specs=[
            tile(1024),
            tile(2048),
            tile(128),
            fixed((1024, 32)),
            fixed((8, 32)),
            fixed((2, 1024, 512)),
            fixed((2, 1024, 512)),
            fixed((2, 1024, 512)),
        ],
        out_specs=[tile(1024), tile(2048), tile(1024), tile(32)],
        flops=6 * 2 * 2048 * 1024 * 512,
        moved=36 << 20,
    )(dout_all, gu, gate, wr, pick, wg, wu, wd)


def mid_back_kernel(
    sum_ref, dout_ref, mix_ref, h_ref, b_ref, gain_ref, wr_ref, mask_ref, wo_ref,
    dh_ref, dattn_ref, do_ref, router_ref, gain_grad_ref,
):
    dout = dout_ref[...].astype(f32)
    b = b_ref[...]
    wr = wr_ref[...]
    h = h_ref[...]
    r = rms(h)
    n = h * r
    gates = chosen_gates(b, wr, mask_ref[...])
    level = jnp.sum(dout * mix_ref[...], axis=-1, keepdims=True)
    taken = (gates * -level).astype(bf16)
    router_ref[...] = t_dot(b, taken)
    db = sum_ref[...] + dot_t(taken, wr)
    gain_grad_ref[...] = jnp.broadcast_to(jnp.sum(db * n, axis=0, keepdims=True), gain_grad_ref.shape)
    ng = db * gain_ref[...]
    dh = dout + r * (ng - n * jnp.mean(ng * n, axis=-1, keepdims=True))
    dh_ref[...] = dh
    dattn = dh.astype(bf16)
    dattn_ref[...] = dattn
    do_ref[...] = dot_t(dattn, wo_ref[...]).astype(bf16)


def end_back_kernel(
    dq_ref, dkv_ref, cos_ref, sin_ref, wq_ref, wk_ref, wv_ref, x_ref, gain_ref, dh_ref,
    dq_lin_ref, dkv_lin_ref, dx_ref, gain_grad_ref,
):
    cosine, sine = cos_ref[...], -sin_ref[...]
    dq = turned(dq_ref[...], cosine, sine).astype(bf16)
    dkv = dkv_ref[...]
    dk = jnp.concatenate([dkv[:, 256 * i : 256 * i + 128] for i in range(4)], axis=1)
    dv = jnp.concatenate([dkv[:, 256 * i + 128 : 256 * i + 256] for i in range(4)], axis=1)
    dk = turned(dk, cosine, sine).astype(bf16)
    dv = dv.astype(bf16)
    dq_lin_ref[...] = dq
    dkv_lin_ref[:, :512] = dk
    dkv_lin_ref[:, 512:] = dv
    da = dot_t(dq, wq_ref[...]) + dot_t(dk, wk_ref[...]) + dot_t(dv, wv_ref[...])
    x = x_ref[...].astype(f32)
    r = rms(x)
    n = x * r
    gain_grad_ref[...] = jnp.broadcast_to(jnp.sum(da * n, axis=0, keepdims=True), gain_grad_ref.shape)
    ng = da * gain_ref[...]
    dx = dh_ref[...] + r * (ng - n * jnp.mean(ng * n, axis=-1, keepdims=True))
    dx_ref[...] = dx.astype(bf16)


def dense_grads_kernel(a_ref, o_ref, dq_ref, dkv_ref, dattn_ref, *rest):
    small_ref, out_ref = rest if len(rest) == 2 else (None, rest[0])
    a = a_ref[...]
    gq = t_dot(a, dq_ref[...]).astype(bf16)
    gkv = t_dot(a, dkv_ref[...]).astype(bf16)
    go = t_dot(o_ref[...], dattn_ref[...]).astype(bf16)
    for t in range(2):
        part = slice(64 * t, 64 * t + 64)
        out_ref[t, 0:64, 0:1024] = gq[part]
        out_ref[t, 64:128, 0:1024] = gkv[part]
        out_ref[t, 128:192, 0:1024] = go[part]
        if small_ref is not None:
            out_ref[t, 0:64, 1024:1152] = small_ref[part, :]
            out_ref[t, 64:192, 1024:1152] = jnp.zeros((128, 128), bf16)


def dense_grads(a, o, dq, dkv, dattn, small=None):
    cols = 1024 if small is None else 1152
    narrow = spec((128, 128), lambda i: (0, i))
    args = (a, o, dq, dkv, dattn) + (() if small is None else (small,))
    return local_call(
        dense_grads_kernel,
        [((16, 192, cols), bf16)],
        "dense_grads",
        grid=(8,),
        in_specs=[narrow, narrow] + [fixed((128, 1024))] * 3
        + ([] if small is None else [spec((128, 128), lambda i: (i, 0))]),
        out_specs=[spec((2, 192, cols), lambda i: (i, 0, 0))],
        flops=3 * 2 * 128 * 1024 * 1024,
        moved=8 << 20,
    )(*args)[0]


def cross_kernel(own_ref, other_ref, out_ref, land, mine, send, recv):
    section, dp = lax.axis_index("section"), lax.axis_index("dp")
    partners = (
        {"section": 1 - section},
        {"dp": dp + 1 - 2 * lax.rem(dp, 2)},
        {"dp": lax.rem(dp + 2, 4)},
    )
    barrier = pltpu.get_barrier_semaphore()
    for to in partners:
        pl.semaphore_signal(barrier, inc=1, device_id=to, device_id_type=MESH)
    pl.semaphore_wait(barrier, 3)
    copies = []
    for i, to in enumerate(partners):
        src = other_ref if i == 0 else mine.at[i - 1]
        c = pltpu.make_async_remote_copy(
            src_ref=src, dst_ref=land.at[i], send_sem=send.at[i], recv_sem=recv.at[i],
            device_id=to, device_id_type=MESH)
        c.start()
        copies.append(c)
        c.wait_recv()
        before = own_ref[...] if i == 0 else mine[i - 1].astype(f32)
        after = (before + land[i].astype(f32)).astype(bf16)
        if i < 2:
            mine[i] = after
        else:
            out_ref[...] = after
    for c in copies:
        c.wait_send()


def cross_sum(own, other, ident):
    rows, cols = own.shape
    return pl.pallas_call(
        cross_kernel,
        out_shape=jax.ShapeDtypeStruct((rows, cols), bf16),
        in_specs=[whole(), whole()],
        out_specs=whole(),
        scratch_shapes=[
            pltpu.VMEM((3, rows, cols), bf16),
            pltpu.VMEM((2, rows, cols), bf16),
            pltpu.SemaphoreType.DMA((3,)),
            pltpu.SemaphoreType.DMA((3,)),
        ],
        compiler_params=pltpu.CompilerParams(
            collective_id=ident, has_side_effects=True, vmem_limit_bytes=24 << 20),
        name="cross_sum",
    )(own, other)


def forward(x, place, dense, experts_w, masks):
    cosine, sine, lo, hi, pick = place
    wq, wk, wv, wo, gain_attn, gain_moe, wr = dense
    mask_all = masks[1]
    a, q, kv = local_call(
        pre_kernel, [((128, 1024), bf16)] * 3, "pre", flops=2 * 128 * 1024 * 2048, moved=6 << 20
    )(x, gain_attn, cosine, sine, wq, wk, wv)
    kv_all = gather_rows(kv, 1)
    o, probs = attend(q, kv_all, lo, hi)
    h, b = local_call(
        post_kernel, [((128, 1024), f32), ((128, 1024), bf16)], "post",
        flops=2 * 128 * 1024 * 1024, moved=4 << 20,
    )(x, o, wo, gain_moe)
    b_all = gather_rows(b, 1)
    y, gu, gate = experts(b_all, mask_all, wr, pick, *experts_w)
    mix = scatter_sum(y, 2)
    out = (h + mix).astype(bf16)
    return out, (x, a, q, kv_all, o, probs, h, b, b_all, gu, gate, mix)


def backward(dout, saved, place, dense, experts_w, masks):
    cosine, sine, lo, hi, pick = place
    wq, wk, wv, wo, gain_attn, gain_moe, wr = dense
    mask_own = masks[0]
    x, a, q, kv_all, o, probs, h, b, b_all, gu, gate, mix = saved
    dout_all = gather_rows(dout, 1)
    db_part, dgu, inner, coef = experts_back(dout_all, gu, gate, wr, pick, *experts_w)
    db_sum = scatter_sum(db_part, 2)
    up_grad = lax.dot_general(b_all, dgu, (((0,), (0,)), ((), ())), preferred_element_type=f32)
    down_grad = lax.dot_general(dout_all, inner, (((0,), (0,)), ((), ())), preferred_element_type=f32)
    expert_grad = jnp.concatenate([up_grad.astype(bf16), down_grad.astype(bf16)], axis=1)
    expert_grad = lax.psum_scatter(expert_grad, "dp", scatter_dimension=0, tiled=True)
    router_part = lax.dot_general(b_all, coef, (((0,), (0,)), ((), ())), preferred_element_type=f32)
    dh, dattn, do, router_own, gain_moe_grad = local_call(
        mid_back_kernel,
        [((128, 1024), f32), ((128, 1024), bf16), ((128, 1024), bf16), ((1024, 32), f32), ((8, 1024), f32)],
        "mid_back", flops=2 * 128 * 1024 * 1024, moved=5 << 20,
    )(db_sum, dout, mix, h, b, gain_moe, wr, mask_own, wo)
    dq, dkv = attend_back(q, o, do, kv_all, probs)
    dkv_sum = scatter_sum(dkv, 2)
    dq_lin, dkv_lin, dx, gain_attn_grad = local_call(
        end_back_kernel,
        [((128, 1024), bf16), ((128, 1024), bf16), ((128, 1024), bf16), ((8, 1024), f32)],
        "end_back", flops=2 * 128 * 1024 * 2048, moved=8 << 20,
    )(dq, dkv_sum, cosine, sine, wq, wk, wv, x, gain_attn, dh)
    small = jnp.concatenate(
        [
            router_part + router_own,
            gain_attn_grad[0][:, None],
            gain_moe_grad[0][:, None],
            jnp.zeros((1024, 30), f32),
        ],
        axis=1,
    ).astype(bf16)
    return dx, expert_grad, (a, o, dq_lin, dkv_lin, dattn), small


def swapped(x):
    return lax.ppermute(x, "section", [(0, 1), (1, 0)])


def on_device(
    inputs, cotangent, offsets, routes, w_query, w_key, w_value, w_out,
    norm_attn, norm_moe, w_router, w_gate, w_up, w_down,
):
    section = lax.axis_index("section")
    expert = lax.axis_index("expert")
    first = section == 0

    def by_layer(own, other):
        return jnp.where(first, own, other), jnp.where(first, other, own)

    def mine(pair):
        return jnp.where(first, pair[0], pair[1])

    ids = lax.broadcasted_iota(jnp.int32, (1, 1, 1, 32), 3)
    mask_both = jnp.any(routes[0][:, :, :, None] == ids, axis=2).astype(bf16)
    mask_own = mine(mask_both)
    mask_away = jnp.where(first, mask_both[1], mask_both[0])
    start = expert * 64

    def part(w):
        return lax.dynamic_slice_in_dim(w, start, 64, axis=0)

    rows = jnp.concatenate(
        [part(w_query[0]), jnp.concatenate([part(w_key[0]), part(w_value[0])], axis=1), part(w_out[0])],
        axis=0,
    )
    small = jnp.concatenate(
        [part(w_router[0]), part(norm_attn[0][:, None]), part(norm_moe[0][:, None]),
         jnp.zeros((64, 30), bf16)], axis=1)
    extra = jnp.concatenate([mask_away, jnp.zeros((128, 32), bf16)], axis=1)
    extra = jnp.concatenate([extra, small], axis=0)
    extra = jnp.concatenate([extra, jnp.zeros((192, 64), bf16)], axis=1)
    payload = swapped(jnp.concatenate([rows, extra], axis=1))
    mask_other = payload[0:128, 1024:1056]
    own_rows = jnp.concatenate([mask_own, jnp.zeros((64, 32), bf16)], axis=0)
    payload = jnp.concatenate([payload[:, :1088], own_rows, payload[:, 1120:]], axis=1)
    got = gather_rows(payload, 3).reshape(16, 192, 1152)
    other_q = got[:, 0:64, :1024].reshape(1024, 1024)
    other_kv = got[:, 64:128, :1024].reshape(1024, 1024)
    other_o = got[:, 128:192, :1024].reshape(1024, 1024)
    other_small = got[:, 128:192, 1024:1088].reshape(1024, 64)
    all_other = got[:, 0:128, 1024:1056].reshape(2048, 32)
    all_own = got[:, 0:128, 1088:1120].reshape(2048, 32)
    pairs = [
        by_layer(w_query[0], other_q),
        by_layer(w_key[0], other_kv[:, :512]),
        by_layer(w_value[0], other_kv[:, 512:]),
        by_layer(w_out[0], other_o),
        by_layer(norm_attn.astype(f32), other_small[:, 32][None].astype(f32)),
        by_layer(norm_moe.astype(f32), other_small[:, 33][None].astype(f32)),
        by_layer(w_router[0], other_small[:, :32]),
    ]
    dense = [tuple(p[l] for p in pairs) for l in range(2)]
    masks_own = by_layer(mask_own, mask_other)
    masks_all = by_layer(all_own, all_other)
    masks = [(masks_own[l], masks_all[l]) for l in range(2)]

    shards = (w_gate[0], w_up[0], w_down[0])
    away = tuple(swapped(w) for w in shards)
    expert_w = []
    for l in range(2):
        expert_w.append(tuple(
            lax.all_gather(by_layer(w, v)[l], "dp", axis=1, tiled=True) for w, v in zip(shards, away)))

    seq = mine(offsets)
    local = expert * 128 + jnp.arange(128, dtype=jnp.int32)
    steps = jnp.arange(HEAD // 2, dtype=f32) * 2.0 / HEAD
    angles = (local - seq).astype(f32)[:, None] * (rope_base ** (-steps))[None, :]
    cosine = jnp.tile(jnp.cos(angles), (1, 4))
    sine = jnp.tile(jnp.sin(angles), (1, 4))
    pick = (
        lax.broadcasted_iota(jnp.int32, (8, 32), 1)
        == 2 * expert + lax.broadcasted_iota(jnp.int32, (8, 32), 0)
    ).astype(f32)
    place = (cosine, sine, seq[:, None], local[:, None], pick)

    x0 = mine(inputs)
    out0, saved0 = forward(x0, place, dense[0], expert_w[0], masks[0])
    out1, saved1 = forward(out0, place, dense[1], expert_w[1], masks[1])
    cot = mine(cotangent)
    dx1, eg1, dg1, small1 = backward(cot, saved1, place, dense[1], expert_w[1], masks[1])
    dense1 = scatter_sum(dense_grads(*dg1).reshape(3072, 1024), 4)
    dx0, eg0, dg0, small0 = backward(dx1, saved0, place, dense[0], expert_w[0], masks[0])
    dense0 = scatter_sum(
        dense_grads(*dg0, jnp.concatenate([small0, small1], axis=1)).reshape(3072, 1152), 5)

    def in_place(l0, l1):
        got = swapped(jnp.where(first, l1, l0))
        own = jnp.where(first, l0, l1)
        return jnp.stack([jnp.where(first, own, got), jnp.where(first, got, own)])[None]

    acts = in_place(out0, out1)
    in_grads = in_place(dx0, dx1)

    blank = jnp.zeros((192, 64), f32)
    full0 = jnp.concatenate([dense0[:, :1088], blank], axis=1)
    full1 = jnp.concatenate([dense1, dense0[:, 1088:], blank], axis=1)
    own = jnp.where(first, full0, full1)
    other = jnp.where(first, full1, full0).astype(bf16)
    summed = gather_rows(cross_sum(own, other, 6), 3).reshape(16, 192, 1152)
    grad_query = summed[:, 0:64, :1024].reshape(1024, 1024).astype(f32)
    grad_kv = summed[:, 64:128, :1024].reshape(1024, 1024).astype(f32)
    grad_out = summed[:, 128:192, :1024].reshape(1024, 1024).astype(f32)
    grad_small = summed[:, 0:64, 1024:1088].reshape(1024, 64).astype(f32)

    eg_away = swapped(jnp.where(first, eg1, eg0))
    eg = jnp.where(first, eg0, eg1).astype(f32) + eg_away.astype(f32)

    def both(lo, hi):
        return jnp.stack([eg[:, lo : lo + 512], eg[:, hi : hi + 512]])[None]

    return (
        acts,
        in_grads,
        grad_query[None],
        grad_kv[None, :, :512],
        grad_kv[None, :, 512:],
        grad_out[None],
        grad_small[:, 32][None],
        grad_small[:, 33][None],
        grad_small[None, :, :32],
        both(0, 1024),
        both(512, 1536),
        both(2048, 2560),
    )


def solution(mesh):
    token = P(None, ("dp", "expert"), None)
    layer_token = P("section", None, ("dp", "expert"), None)
    matrix = P("section", None, None)
    gain = P("section", None)
    expert = P("section", "expert", "dp", None)
    return jax.shard_map(
        on_device,
        mesh=mesh,
        in_specs=(
            token, token, P(None, ("dp", "expert")), layer_token,
            matrix, matrix, matrix, matrix, gain, gain, matrix, expert, expert, expert,
        ),
        out_specs=(
            layer_token, layer_token, matrix, matrix, matrix, matrix, gain, gain, matrix,
            expert, expert, expert,
        ),
        check_vma=False,
    )
```

time: 2420 us -> 953 us (0.39); the launches traced: 2390 us -> 946 us
  waiting for transfers between devices: 1170 us -> 64.7 us
  Pallas kernels: 0 us -> 700 us
  local copies, waits for them, and re-layouts: 371 us -> 63.8 us
  matrix products: 338 us -> 41 us
  blocking collectives: 231 us -> 0 us
  other arithmetic: 196 us -> 49.3 us
  starting transfers between devices: 60.2 us -> 11.3 us
    pallas_call x0 -> x35, Pallas kernels: none -> 700 us  [the longest x8 248 us: gather_rows(): pl.pallas_call(gather_kernel, out_shape=jax.ShapeDtypeStruct((4, 4, rows,...]
    psum x1 -> x0, waiting for transfers between devices: 535 us -> none  [on_device(): dense_total = lax.psum(dense_total, ('dp', 'expert'))]
    dot_general x93 -> x6, matrix products: 338 us -> 41 us  [the longest x2 19.5 us: backward(): lax.dot_general(b_all, dgu, (((0,), (0,)), ((), ())), preferred_element_t...]
    unnamed x25 -> x8, waiting for transfers between devices: 284 us -> 0.64 us
    all_to_all x9 -> x0, waiting for transfers between devices: 146 us -> none  [the longest x3 45.7 us: backward_layer(): lax.all_to_all(rows_grad[None], 'expert', split_axis=2, concat_axis=0, ti...]
    psum x1 -> x0, blocking collectives: 137 us -> none  [on_device(): dense_total = lax.psum(dense_total, ('dp', 'expert'))]
    reduce_scatter x3 -> x2, waiting for transfers between devices: 109 us -> 0.01 us  [backward(): lax.psum_scatter(expert_grad, 'dp', scatter_dimension=0, tiled=True)]
    all_to_all x3 -> x0, blocking collectives: 94 us -> none  [the longest x2 61.7 us: backward_layer(): lax.all_to_all(send_grad, 'expert', split_axis=0, concat_axis=2, tiled=True)]
  transfers between devices with their start and end apart: 32 -> 15, of which waited for: 24 -> 4; matrix products, arithmetic and copies ran while one was open for 22% -> 10% of each run, Pallas kernels for 0% -> 69%
where the time goes in v1:
time: 953 us; the launch traced here: 946 us
  Pallas kernels  700 us (73%)
  waiting for transfers between devices  64.7 us (7%)
  local copies, waits for them, and re-layouts  63.8 us (7%)
  other arithmetic  49.3 us (5%)
  matrix products  41 us (4%)
  between operations  15.5 us (2%)
  starting transfers between devices  11.3 us (1%)
    pallas_call x8, Pallas kernels, gather_rows(): pl.pallas_call(gather_kernel, out_shape=jax.ShapeDtypeStruct((4, 4, rows,...  248 us
    pallas_call x8, Pallas kernels, scatter_sum(): pl.pallas_call(scatter_kernel, out_shape=jax.ShapeDtypeStruct((rows, cols...  196 us
    pallas_call x1, Pallas kernels, cross_sum(): pl.pallas_call(cross_kernel, out_shape=jax.ShapeDtypeStruct((rows, cols),...  69.8 us
    ppermute x7, waiting for transfers between devices, swapped(): return lax.ppermute(x, 'section', [(0, 1), (1, 0)])  64 us
    pallas_call x2, Pallas kernels, experts_back(): local_call(experts_back_kernel, [((rows, 1024), bf16), ((rows, 2048), bf1...  49.6 us
    pallas_call x2, Pallas kernels, experts(): local_call(experts_kernel, [((rows, 1024), bf16), ((rows, 2048), bf16), (...  40.1 us
    pallas_call x2, Pallas kernels, attend(): local_call(attend_kernel, [((128, 1024), bf16), ((4, 512, 2048), bf16)],...  32.1 us
    unnamed x148, local copies, waits for them, and re-layouts  30.3 us
  transfers between devices with their start and end apart: 15, of which 4 were waited for; matrix products, arithmetic and copies ran while one was open for 10% of the time, Pallas kernels for 69%

profile of v1, /device:TPU:1, one launch (start us, length us, event | category | flops | bytes accessed | tf_op | source)
XLA Modules:
  0.0 946.0 jit_solution(4254605618803297440)
XLA Ops:
  7.2 2.2 collective-permute-start.3
  9.4 11.4 %collective-permute-done.3 = bf16[2,256,512]{2,1,0:T(8,128)(2,1)S(1)} collective-permute-done((bf16[2,256,512]{2,1,0:T(8,128)(2,1)}, bf16[2,256,512]{2,1,0:T(8,128)(2,1)S(1)}, u32[]{:S(2)}, u32[]{:S(2)}) %collective-permute-start.3) | collective-permute-done | bytes 524320 | tf_op jit(solution)/shard_map/ppermute | solution.py:700
  24.7 10.6 %collective-permute-done.2 = bf16[2,256,512]{2,1,0:T(8,128)(2,1)S(1)} collective-permute-done((bf16[2,256,512]{2,1,0:T(8,128)(2,1)}, bf16[2,256,512]{2,1,0:T(8,128)(2,1)S(1)}, u32[]{:S(2)}, u32[]{:S(2)}) %collective-permute-start.2) | collective-permute-done | bytes 524320 | tf_op jit(solution)/shard_map/ppermute | solution.py:700
  39.0 21.7 %collective-permute-done.1 = bf16[2,256,512]{2,1,0:T(8,128)(2,1)S(1)} collective-permute-done((bf16[2,256,512]{2,1,0:T(8,128)(2,1)S(1)}, bf16[2,256,512]{2,1,0:T(8,128)(2,1)S(1)}, u32[]{:S(2)}, u32[]{:S(2)}) %collective-permute-start.1) | collective-permute-done | bytes 524320 | tf_op jit(solution)/shard_map/ppermute | solution.py:700
  71.5 30.4 %gather_rows.13 = bf16[4,4,128,1024]{3,2,1,0:T(8,128)(2,1)} custom-call(bf16[128,1024]{1,0:T(8,128)(2,1)} %select_bitcast_fusion.2.x_ref.dout_ref), custom_call_target="tpu_custom_call" | custom-call | tf_op jit(solution)/shard_map/gather_rows/pallas_call | solution.py:89
  104.0 41.3 %gather_rows.8 = bf16[4,4,192,1152]{3,2,1,0:T(8,128)(2,1)} custom-call(bf16[192,1152]{1,0:T(8,128)(2,1)} %concatenate.51.x_ref), custom_call_target="tpu_custom_call" | custom-call | tf_op jit(solution)/shard_map/gather_rows/pallas_call | solution.py:89
  146.8 6.3 fusion.15
  155.3 7.1 bitcast_select_fusion
  162.4 3.4 pre.2
  167.3 28.0 %gather_rows.9 = bf16[4,4,128,1024]{3,2,1,0:T(8,128)(2,1)} custom-call(bf16[128,1024]{1,0:T(8,128)(2,1)} %copy-done.39), custom_call_target="tpu_custom_call" | custom-call | tf_op jit(solution)/shard_map/gather_rows/pallas_call | solution.py:89
  195.3 16.0 %attend.2 = (bf16[128,1024]{1,0:T(8,128)(2,1)S(1)}, bf16[4,512,2048]{2,1,0:T(8,128)(2,1)}) custom-call(bf16[128,1024]{1,0:T(8,128)(2,1)S(1)} %get-tuple-element.62.q_ref, bf16[2048,1024]{1,0:T(8,128)(2,1)} %bitcast.164, bf16[2048,1024]{1,0:T(8,128)(2,1)} %bitcast.165, s32[128,1]{1,0:T(8,128)S(1)} %copy.68.lo_ref, s32[128,1]{1,0:T(8,128)S(1)} %iota_add_fusion.hi_ref), custom_call_target="tpu_custom_call" | custom-call | flops 2147483648 | bytes 13631488 | tf_op jit(solution)/shard_map/attend/pallas_call | solution.py:326
  214.1 24.7 %gather_rows.10 = bf16[4,4,128,1024]{3,2,1,0:T(8,128)(2,1)} custom-call(bf16[128,1024]{1,0:T(8,128)(2,1)} %copy-done.20), custom_call_target="tpu_custom_call" | custom-call | tf_op jit(solution)/shard_map/gather_rows/pallas_call | solution.py:89
  238.9 2.3 broadcast_select_fusion.7
  241.2 20.1 %experts.2 = (bf16[2048,1024]{1,0:T(8,128)(2,1)}, bf16[2048,2048]{1,0:T(8,128)(2,1)}, f32[2048,128]{1,0:T(8,128)S(1)}) custom-call(bf16[2048,1024]{1,0:T(8,128)(2,1)} %bitcast.179, bf16[2048,32]{1,0:T(8,128)(2,1)S(1)} %bitcast.163, bf16[1024,32]{1,0:T(8,128)(2,1)S(1)} %get-tuple-element.157.wr_ref, f32[8,32]{1,0:T(8,128)S(1)} %fusion.9.pick_ref, ...), custom_call_target="tpu_custom_call" | custom-call | flops 12884901888 | bytes 25165824 | tf_op jit(solution)/shard_map/experts/pallas_call | solution.py:437
  261.3 2.6 copy-done.10
  263.8 19.7 %scatter_sum.8.mix_ref = f32[128,1024]{1,0:T(8,128)S(1)} custom-call(bf16[4,4,128,1024]{3,2,1,0:T(8,128)(2,1)S(1)} %bitcast.161), custom_call_target="tpu_custom_call" | custom-call | tf_op jit(solution)/shard_map/scatter_sum/pallas_call | solution.py:200
  283.7 3.2 pre.3
  287.5 24.6 %gather_rows.11 = bf16[4,4,128,1024]{3,2,1,0:T(8,128)(2,1)} custom-call(bf16[128,1024]{1,0:T(8,128)(2,1)} %copy-done.40), custom_call_target="tpu_custom_call" | custom-call | tf_op jit(solution)/shard_map/gather_rows/pallas_call | solution.py:89
  312.2 16.0 %attend.3 = (bf16[128,1024]{1,0:T(8,128)(2,1)S(1)}, bf16[4,512,2048]{2,1,0:T(8,128)(2,1)}) custom-call(bf16[128,1024]{1,0:T(8,128)(2,1)S(1)} %get-tuple-element.68.q_ref, bf16[2048,1024]{1,0:T(8,128)(2,1)} %bitcast.168, bf16[2048,1024]{1,0:T(8,128)(2,1)} %bitcast.169, s32[128,1]{1,0:T(8,128)S(1)} %copy.68.lo_ref, s32[128,1]{1,0:T(8,128)S(1)} %iota_add_fusion.hi_ref), custom_call_target="tpu_custom_call" | custom-call | flops 2147483648 | bytes 13631488 | tf_op jit(solution)/shard_map/attend/pallas_call | solution.py:326
  328.3 2.2 post.3
  332.0 23.6 %gather_rows.12 = bf16[4,4,128,1024]{3,2,1,0:T(8,128)(2,1)} custom-call(bf16[128,1024]{1,0:T(8,128)(2,1)} %copy-done.22), custom_call_target="tpu_custom_call" | custom-call | tf_op jit(solution)/shard_map/gather_rows/pallas_call | solution.py:89
  355.7 20.1 %experts.3 = (bf16[2048,1024]{1,0:T(8,128)(2,1)}, bf16[2048,2048]{1,0:T(8,128)(2,1)}, f32[2048,128]{1,0:T(8,128)S(1)}) custom-call(bf16[2048,1024]{1,0:T(8,128)(2,1)} %bitcast.182, bf16[2048,32]{1,0:T(8,128)(2,1)S(1)} %bitcast.162, bf16[1024,32]{1,0:T(8,128)(2,1)S(1)} %get-tuple-element.156.wr_ref, f32[8,32]{1,0:T(8,128)S(1)} %fusion.9.pick_ref, ...), custom_call_target="tpu_custom_call" | custom-call | flops 12884901888 | bytes 25165824 | tf_op jit(solution)/shard_map/experts/pallas_call | solution.py:437
  375.8 24.8 %experts_back.2 = (bf16[2048,1024]{1,0:T(8,128)(2,1)}, bf16[2048,2048]{1,0:T(8,128)(2,1)}, bf16[2048,1024]{1,0:T(8,128)(2,1)}, bf16[2048,32]{1,0:T(8,128)(2,1)S(1)}) custom-call(bf16[2048,1024]{1,0:T(8,128)(2,1)} %bitcast.189, bf16[2048,2048]{1,0:T(8,128)(2,1)} %get-tuple-element.74.gu_ref, f32[2048,128]{1,0:T(8,128)S(1)} %get-tuple-element.75.gate_ref, ...), custom_call_target="tpu_custom_call" | custom-call | flops 12884901888 | bytes 37748736 | tf_op jit(solution)/shard_map/experts_back/pallas_call | solution.py:491
  400.6 7.2 convolution_convert_fusion.2
  407.8 9.6 %convolution_convert_fusion = bf16[1024,2048]{1,0:T(8,128)(2,1)S(1)} fusion(bf16[2048,1024]{1,0:T(8,128)(2,1)S(1)} %bitcast.184, bf16[2048,2048]{1,0:T(8,128)(2,1)S(1)} %copy-done.71), kind=kOutput, calls=%fused_computation.2 | convolution fusion | flops 8592031744 | bytes 16777216 | tf_op jit(solution)/shard_map/dot_general | solution.py:670
  417.5 3.1 pad_maximum_fusion.1
  421.9 2.2 copy-done.6
  424.1 18.8 %scatter_sum.9.mix_ref = f32[128,1024]{1,0:T(8,128)S(1)} custom-call(bf16[4,4,128,1024]{3,2,1,0:T(8,128)(2,1)S(1)} %bitcast.157), custom_call_target="tpu_custom_call" | custom-call | tf_op jit(solution)/shard_map/scatter_sum/pallas_call | solution.py:200
  443.6 25.0 %scatter_sum.10.sum_ref = f32[128,1024]{1,0:T(8,128)S(1)} custom-call(bf16[4,4,128,1024]{3,2,1,0:T(8,128)(2,1)S(1)} %bitcast.158), custom_call_target="tpu_custom_call" | custom-call | tf_op jit(solution)/shard_map/scatter_sum/pallas_call | solution.py:200
  469.4 4.6 mid_back.2
  474.8 12.8 %attend_back.2 = (f32[128,1024]{1,0:T(8,128)S(1)}, bf16[2048,1024]{1,0:T(8,128)(2,1)}) custom-call(bf16[128,1024]{1,0:T(8,128)(2,1)S(1)} %get-tuple-element.68.q_ref, bf16[128,1024]{1,0:T(8,128)(2,1)S(1)} %get-tuple-element.70.o_ref, bf16[128,1024]{1,0:T(8,128)(2,1)S(1)} %get-tuple-element.77.do_ref, bf16[2048,1024]{1,0:T(8,128)(2,1)} %bitcast.170, ...), custom_call_target="tpu_custom_call" | custom-call | flops 4294967296 | bytes 17825792 | tf_op jit(solution)/shard_map/attend_back/pallas_call | solution.py:375
  487.6 2.2 copy-done.8
  489.8 20.7 %scatter_sum.11.dkv_ref = f32[128,1024]{1,0:T(8,128)S(1)} custom-call(bf16[4,4,128,1024]{3,2,1,0:T(8,128)(2,1)S(1)} %bitcast.159), custom_call_target="tpu_custom_call" | custom-call | tf_op jit(solution)/shard_map/scatter_sum/pallas_call | solution.py:200
  511.3 4.1 end_back.2
  516.8 26.9 %gather_rows.14 = bf16[4,4,128,1024]{3,2,1,0:T(8,128)(2,1)} custom-call(bf16[128,1024]{1,0:T(8,128)(2,1)} %copy-done.3), custom_call_target="tpu_custom_call" | custom-call | tf_op jit(solution)/shard_map/gather_rows/pallas_call | solution.py:89
  544.9 24.8 %experts_back.3 = (bf16[2048,1024]{1,0:T(8,128)(2,1)}, bf16[2048,2048]{1,0:T(8,128)(2,1)}, bf16[2048,1024]{1,0:T(8,128)(2,1)}, bf16[2048,32]{1,0:T(8,128)(2,1)S(1)}) custom-call(bf16[2048,1024]{1,0:T(8,128)(2,1)} %bitcast.191, bf16[2048,2048]{1,0:T(8,128)(2,1)} %get-tuple-element.83.gu_ref, f32[2048,128]{1,0:T(8,128)S(1)} %copy-done.50, ...), custom_call_target="tpu_custom_call" | custom-call | flops 12884901888 | bytes 37748736 | tf_op jit(solution)/shard_map/experts_back/pallas_call | solution.py:491
  569.8 7.2 convolution_convert_fusion.3
  577.0 9.8 %convolution_convert_fusion.1 = bf16[1024,2048]{1,0:T(8,128)(2,1)S(1)} fusion(bf16[2048,1024]{1,0:T(8,128)(2,1)S(1)} %bitcast.180, bf16[2048,2048]{1,0:T(8,128)(2,1)S(1)} %copy-done.70), kind=kOutput, calls=%fused_computation.3 | convolution fusion | flops 8592031744 | bytes 16777216 | tf_op jit(solution)/shard_map/dot_general | solution.py:670
  586.8 3.1 pad_maximum_fusion
  592.1 4.1 collective-permute-start.4
  597.9 2.2 copy-done.5
  600.1 19.5 %scatter_sum.12.sum_ref = f32[128,1024]{1,0:T(8,128)S(1)} custom-call(bf16[4,4,128,1024]{3,2,1,0:T(8,128)(2,1)S(1)} %bitcast.156), custom_call_target="tpu_custom_call" | custom-call | tf_op jit(solution)/shard_map/scatter_sum/pallas_call | solution.py:200
  620.4 3.8 mid_back.3
  625.0 13.0 %attend_back.3 = (f32[128,1024]{1,0:T(8,128)S(1)}, bf16[2048,1024]{1,0:T(8,128)(2,1)}) custom-call(bf16[128,1024]{1,0:T(8,128)(2,1)S(1)} %get-tuple-element.62.q_ref, bf16[128,1024]{1,0:T(8,128)(2,1)S(1)} %get-tuple-element.64.o_ref, bf16[128,1024]{1,0:T(8,128)(2,1)S(1)} %get-tuple-element.86.do_ref, bf16[2048,1024]{1,0:T(8,128)(2,1)} %bitcast.166, ...), custom_call_target="tpu_custom_call" | custom-call | flops 4294967296 | bytes 17825792 | tf_op jit(solution)/shard_map/attend_back/pallas_call | solution.py:375
  637.9 3.4 copy-done.9
  641.3 22.9 %scatter_sum.13.dkv_ref = f32[128,1024]{1,0:T(8,128)S(1)} custom-call(bf16[4,4,128,1024]{3,2,1,0:T(8,128)(2,1)S(1)} %bitcast.160), custom_call_target="tpu_custom_call" | custom-call | tf_op jit(solution)/shard_map/scatter_sum/pallas_call | solution.py:200
  665.9 4.2 end_back.3
  672.5 4.0 fusion.1
  676.6 3.2 fusion
  679.8 3.6 concatenate.52.rest_0_
  683.4 5.9 dense_grads.2
  689.3 30.3 %scatter_sum.14 = f32[192,1152]{1,0:T(8,128)S(1)} custom-call(bf16[4,4,192,1152]{3,2,1,0:T(8,128)(2,1)} %bitcast.175), custom_call_target="tpu_custom_call" | custom-call | tf_op jit(solution)/shard_map/scatter_sum/pallas_call | solution.py:200
  719.8 5.7 dense_grads.3
  725.5 39.2 %scatter_sum.15 = f32[192,1024]{1,0:T(8,128)S(1)} custom-call(bf16[4,4,192,1024]{3,2,1,0:T(8,128)(2,1)} %bitcast.178), custom_call_target="tpu_custom_call" | custom-call | tf_op jit(solution)/shard_map/scatter_sum/pallas_call | solution.py:200
  765.0 69.8 %cross_sum.1.x_ref = bf16[192,1152]{1,0:T(8,128)(2,1)S(1)} custom-call(f32[192,1152]{1,0:T(8,128)S(1)} %select_select_fusion.own_ref, bf16[192,1152]{1,0:T(8,128)(2,1)S(1)} %select_convert_fusion.other_ref), custom_call_target="tpu_custom_call" | custom-call | tf_op jit(solution)/shard_map/cross_sum/pallas_call | solution.py:625
  835.6 48.3 %gather_rows.15 = bf16[4,4,192,1152]{3,2,1,0:T(8,128)(2,1)} custom-call(bf16[192,1152]{1,0:T(8,128)(2,1)} %copy-done.19), custom_call_target="tpu_custom_call" | custom-call | tf_op jit(solution)/shard_map/gather_rows/pallas_call | solution.py:89
  884.9 5.5 fusion.14
  890.4 2.5 bitcast_convert_fusion
  892.9 2.6 bitcast_convert_fusion.2
  895.5 2.8 broadcast_select_fusion
  902.0 4.8 slice_bitcast_fusion
  906.8 2.5 bitcast_convert_fusion.1
  913.0 20.3 %collective-permute-done.6 = bf16[256,3072]{1,0:T(8,128)(2,1)} collective-permute-done((bf16[256,3072]{1,0:T(8,128)(2,1)}, bf16[256,3072]{1,0:T(8,128)(2,1)}, u32[]{:S(2)}, u32[]{:S(2)}) %collective-permute-start.6) | collective-permute-done | bytes 1572896 | tf_op jit(solution)/shard_map/ppermute | solution.py:700
  933.3 2.2 convert_add_fusion
  (250 shorter events, 60.2 us)
Async XLA Ops:
  7.2 30.3 %copy-start.63 = (bf16[1,2,256,512]{3,2,1,0:T(8,128)(2,1)S(1)}, bf16[1,2,256,512]{3,2,1,0:T(8,128)(2,1)}, u32[]{:S(2)}) copy-start(bf16[1,2,256,512]{3,2,1,0:T(8,128)(2,1)} %param.25) | copy-start | bytes 1572868
  7.2 234.0 %all-gather.11.cloned.1.call-start = ((), (), s32[]{:S(2)}) async-start(), calls=%async_computation.4 | async-start | bytes 2621440 | tf_op jit(solution)/shard_map/all_gather | solution.py:766
  7.2 13.7 %collective-permute-start.3 = (bf16[2,256,512]{2,1,0:T(8,128)(2,1)}, bf16[2,256,512]{2,1,0:T(8,128)(2,1)S(1)}, u32[]{:S(2)}, u32[]{:S(2)}) collective-permute-start(bf16[2,256,512]{2,1,0:T(8,128)(2,1)} %bitcast.196), channel_id=1, source_target_pairs={{0,64},{64,0},{1,65},{65,1},{2,66},{66,2},{3,67},{67,3},{4,68},{68... | collective-permute-start | bytes 1572872 | tf_op jit(solution)/shard_map/ppermute | solution.py:700
  9.4 53.0 %copy-start.65 = (bf16[1,1024,32]{1,2,0:T(8,128)(2,1)S(1)}, bf16[1,1024,32]{1,2,0:T(8,128)(2,1)}, u32[]{:S(2)}) copy-start(bf16[1,1024,32]{1,2,0:T(8,128)(2,1)} %param.24) | copy-start | bytes 196612
  9.4 54.9 %copy-start.66 = (s32[1,2,128,8]{2,3,1,0:T(8,128)S(1)}, s32[1,2,128,8]{2,3,1,0:T(8,128)}, u32[]{:S(2)}) copy-start(s32[1,2,128,8]{2,3,1,0:T(8,128)} %param.17) | copy-start | bytes 24580
  9.4 55.9 %copy-start.59 = (bf16[1,1024,512]{2,1,0:T(8,128)(2,1)S(1)}, bf16[1,1024,512]{2,1,0:T(8,128)(2,1)}, u32[]{:S(2)}) copy-start(bf16[1,1024,512]{2,1,0:T(8,128)(2,1)} %param.20) | copy-start | bytes 3145732
  23.0 218.2 %all-gather.9.cloned.1.call-start = ((), (), s32[]{:S(2)}) async-start(), calls=%async_computation.3 | async-start | bytes 2621440 | tf_op jit(solution)/shard_map/all_gather | solution.py:766
  23.1 12.3 %collective-permute-start.2 = (bf16[2,256,512]{2,1,0:T(8,128)(2,1)}, bf16[2,256,512]{2,1,0:T(8,128)(2,1)S(1)}, u32[]{:S(2)}, u32[]{:S(2)}) collective-permute-start(bf16[2,256,512]{2,1,0:T(8,128)(2,1)} %bitcast.197), channel_id=1, source_target_pairs={{0,64},{64,0},{1,65},{65,1},{2,66},{66,2},{3,67},{67,3},{4,68},{68... | collective-permute-start | bytes 1572872 | tf_op jit(solution)/shard_map/ppermute | solution.py:700
  37.4 33.3 %copy-start.64 = (bf16[2,128,1024]{2,1,0:T(8,128)(2,1)S(1)}, bf16[2,128,1024]{2,1,0:T(8,128)(2,1)}, u32[]{:S(2)}) copy-start(bf16[2,128,1024]{2,1,0:T(8,128)(2,1)} %param.15) | copy-start | bytes 1572868
  37.5 203.7 %all-gather.7.cloned.1.call-start = ((), (), s32[]{:S(2)}) async-start(), calls=%async_computation.2 | async-start | bytes 2621440 | tf_op jit(solution)/shard_map/all_gather | solution.py:766
  37.5 23.2 %collective-permute-start.1 = (bf16[2,256,512]{2,1,0:T(8,128)(2,1)S(1)}, bf16[2,256,512]{2,1,0:T(8,128)(2,1)S(1)}, u32[]{:S(2)}, u32[]{:S(2)}) collective-permute-start(bf16[2,256,512]{2,1,0:T(8,128)(2,1)S(1)} %bitcast.198), channel_id=1, source_target_pairs={{0,64},{64,0},{1,65},{65,1},{2,66},{66,2},{3,67},{67,3},{4,68},{68... | collective-permute-start | bytes 1572872 | tf_op jit(solution)/shard_map/ppermute | solution.py:700
  61.8 293.9 %all-gather.17.cloned.1.call-start = ((), (), s32[]{:S(2)}) async-start(), calls=%async_computation.7 | async-start | bytes 2621440 | tf_op jit(solution)/shard_map/all_gather | solution.py:766
  62.3 293.3 %all-gather.15.cloned.1.call-start = ((), (), s32[]{:S(2)}) async-start(), calls=%async_computation.6 | async-start | bytes 2621440 | tf_op jit(solution)/shard_map/all_gather | solution.py:766
  67.3 288.4 %all-gather.13.cloned.1.call-start = ((), (), s32[]{:S(2)}) async-start(), calls=%async_computation.5 | async-start | bytes 2621440 | tf_op jit(solution)/shard_map/all_gather | solution.py:766
  68.3 34.7 %collective-permute-start = (bf16[192,1152]{1,0:T(8,128)(2,1)}, bf16[192,1152]{1,0:T(8,128)(2,1)S(1)}, u32[]{:S(2)}, u32[]{:S(2)}) collective-permute-start(bf16[192,1152]{1,0:T(8,128)(2,1)} %concatenate.49), channel_id=1, source_target_pairs={{0,64},{64,0},{1,65},{65,1},{2,66},{66,2},{3,67},{67,3},{4,68},{68... | collective-permute-start | bytes 1327112 | tf_op jit(solution)/shard_map/ppermute | solution.py:700
  103.0 42.4 %copy-start.62 = (bf16[192,1152]{1,0:T(8,128)(2,1)}, bf16[192,1152]{1,0:T(8,128)(2,1)S(1)}, u32[]{:S(2)}) copy-start(bf16[192,1152]{1,0:T(8,128)(2,1)S(1)} %collective-permute-done) | copy-start | bytes 1327108
  104.0 42.7 %copy-start.68 = (bf16[1,1024]{1,0:T(2,128)(2,1)S(1)}, bf16[1,1024]{1,0:T(2,128)(2,1)}, u32[]{:S(2)}) copy-start(bf16[1,1024]{1,0:T(2,128)(2,1)} %param.23) | copy-start | bytes 6148
  104.0 42.8 %copy-start.69 = (bf16[1,1024]{1,0:T(2,128)(2,1)S(1)}, bf16[1,1024]{1,0:T(2,128)(2,1)}, u32[]{:S(2)}) copy-start(bf16[1,1024]{1,0:T(2,128)(2,1)} %param.22) | copy-start | bytes 6148
  146.8 6.3 copy-start.60
  155.3 740.2 %reduce-scatter.5.cloned.1.call-start = ((), (), s32[]{:S(2)}) async-start(), calls=%async_computation.9 | async-start | bytes 7864320 | tf_op jit(solution)/shard_map/reduce_scatter | solution.py:673
  214.1 69.4 %copy-start.14 = (f32[128,1024]{1,0:T(8,128)}, f32[128,1024]{1,0:T(8,128)S(1)}, u32[]{:S(2)}) copy-start(f32[128,1024]{1,0:T(8,128)S(1)} %get-tuple-element.65.h_ref) | copy-start | bytes 1572868
  261.3 25.6 %copy-start.49 = (f32[2048,128]{1,0:T(8,128)}, f32[2048,128]{1,0:T(8,128)S(1)}, u32[]{:S(2)}) copy-start(f32[2048,128]{1,0:T(8,128)S(1)} %get-tuple-element.84.gate_ref) | copy-start | bytes 3145732
  261.3 2.6 copy-start.10
  283.6 28.6 %copy-start = (f32[128,1024]{1,0:T(8,128)}, f32[128,1024]{1,0:T(8,128)S(1)}, u32[]{:S(2)}) copy-start(f32[128,1024]{1,0:T(8,128)S(1)} %scatter_sum.8.mix_ref) | copy-start | bytes 1572868
  287.5 40.7 %copy-start.41 = (bf16[128,1024]{1,0:T(8,128)(2,1)}, bf16[128,1024]{1,0:T(8,128)(2,1)S(1)}, u32[]{:S(2)}) copy-start(bf16[128,1024]{1,0:T(8,128)(2,1)S(1)} %get-tuple-element.104.a_ref) | copy-start | bytes 786436
  328.3 27.4 %copy-start.28 = (bf16[16,128,32]{2,1,0:T(8,128)(2,1)S(1)}, bf16[16,128,32]{2,1,0:T(8,128)(2,1)}, u32[]{:S(2)}) copy-start(bf16[16,128,32]{2,1,0:T(8,128)(2,1)} %get-tuple-element.121) | copy-start | bytes 393220
  375.8 24.8 %copy-start.57 = (bf16[4,4,128,1024]{3,2,1,0:T(8,128)(2,1)S(1)}, bf16[4,4,128,1024]{3,2,1,0:T(8,128)(2,1)}, u32[]{:S(2)}) copy-start(bf16[4,4,128,1024]{3,2,1,0:T(8,128)(2,1)} %gather_rows.13) | copy-start | bytes 12582916
  400.6 7.2 copy-start.24
  400.6 7.2 copy-start.53
  400.6 7.2 copy-start.71
  420.6 474.9 %reduce-scatter.3.cloned.1.call-start = ((), (), s32[]{:S(2)}) async-start(), calls=%async_computation.8 | async-start | bytes 7864320 | tf_op jit(solution)/shard_map/reduce_scatter | solution.py:673
  424.0 19.6 %copy-start.7 = (bf16[2048,1024]{1,0:T(8,128)(2,1)S(1)}, bf16[2048,1024]{1,0:T(8,128)(2,1)}, u32[]{:S(2)}) copy-start(bf16[2048,1024]{1,0:T(8,128)(2,1)} %get-tuple-element.76) | copy-start | bytes 12582916
  424.0 45.4 %copy-start.11 = (bf16[128,1024]{1,0:T(8,128)(2,1)S(1)}, bf16[128,1024]{1,0:T(8,128)(2,1)}, u32[]{:S(2)}) copy-start(bf16[128,1024]{1,0:T(8,128)(2,1)} %select_bitcast_fusion.2.x_ref.dout_ref) | copy-start | bytes 786436
  424.0 45.4 %copy-start.23 = (bf16[128,1024]{1,0:T(8,128)(2,1)S(1)}, bf16[128,1024]{1,0:T(8,128)(2,1)}, u32[]{:S(2)}) copy-start(bf16[128,1024]{1,0:T(8,128)(2,1)} %copy-done.22) | copy-start | bytes 786436
  474.8 12.8 %copy-start.43 = (bf16[128,1024]{1,0:T(8,128)(2,1)}, bf16[128,1024]{1,0:T(8,128)(2,1)S(1)}, u32[]{:S(2)}) copy-start(bf16[128,1024]{1,0:T(8,128)(2,1)S(1)} %get-tuple-element.107.dattn_ref) | copy-start | bytes 786436
  516.8 53.0 %copy-start.47 = (bf16[128,1024]{1,0:T(8,128)(2,1)}, bf16[128,1024]{1,0:T(8,128)(2,1)S(1)}, u32[]{:S(2)}) copy-start(bf16[128,1024]{1,0:T(8,128)(2,1)S(1)} %get-tuple-element.106.dkv_ref) | copy-start | bytes 786436
  544.9 24.8 %copy-start.58 = (bf16[4,4,128,1024]{3,2,1,0:T(8,128)(2,1)S(1)}, bf16[4,4,128,1024]{3,2,1,0:T(8,128)(2,1)}, u32[]{:S(2)}) copy-start(bf16[4,4,128,1024]{3,2,1,0:T(8,128)(2,1)} %gather_rows.14) | copy-start | bytes 12582916
  569.7 7.2 copy-start.26
  569.7 7.2 copy-start.51
  569.8 7.2 copy-start.70
  591.2 29.3 %copy-start.4 = (bf16[128,1024]{1,0:T(8,128)(2,1)S(1)}, bf16[128,1024]{1,0:T(8,128)(2,1)}, u32[]{:S(2)}) copy-start(bf16[128,1024]{1,0:T(8,128)(2,1)} %copy-done.3) | copy-start | bytes 786436
  591.2 29.3 %copy-start.21 = (bf16[128,1024]{1,0:T(8,128)(2,1)S(1)}, bf16[128,1024]{1,0:T(8,128)(2,1)}, u32[]{:S(2)}) copy-start(bf16[128,1024]{1,0:T(8,128)(2,1)} %copy-done.20) | copy-start | bytes 786436
  592.1 317.2 %collective-permute-start.4 = (bf16[128,1024]{1,0:T(8,128)(2,1)}, bf16[128,1024]{1,0:T(8,128)(2,1)}, u32[]{:S(2)}, u32[]{:S(2)}) collective-permute-start(bf16[128,1024]{1,0:T(8,128)(2,1)} %get-tuple-element.116), channel_id=1, source_target_pairs={{0,64},{64,0},{1,65},{65,1},{2,66},{66,2},{3,67},{67,3},{4,68},{68... | collective-permute-start | bytes 786440 | tf_op jit(solution)/shard_map/ppermute | solution.py:700
  625.0 13.0 %copy-start.33 = (bf16[128,1024]{1,0:T(8,128)(2,1)}, bf16[128,1024]{1,0:T(8,128)(2,1)S(1)}, u32[]{:S(2)}) copy-start(bf16[128,1024]{1,0:T(8,128)(2,1)S(1)} %get-tuple-element.95.dattn_ref) | copy-start | bytes 786436
  637.9 3.4 copy-start.9
  665.0 7.5 copy-start.25
  670.8 5.7 copy-start.37
  670.8 5.7 copy-start.27
  671.7 4.8 copy-start.52
  672.5 238.7 %collective-permute-start.5 = (bf16[128,1024]{1,0:T(8,128)(2,1)}, bf16[128,1024]{1,0:T(8,128)(2,1)}, u32[]{:S(2)}, u32[]{:S(2)}) collective-permute-start(bf16[128,1024]{1,0:T(8,128)(2,1)} %broadcast_select_fusion.9), channel_id=1, source_target_pairs={{0,64},{64,0},{1,65},{65,1},{2,66},{66,2},{3,67},{67,3},{4,68},{68... | collective-permute-start | bytes 786440 | tf_op jit(solution)/shard_map/ppermute | solution.py:700
  676.6 6.8 copy-start.32
  676.6 6.8 copy-start.34
  676.6 6.8 copy-start.36
  676.6 6.8 copy-start.38
  689.3 30.4 %copy-start.42 = (bf16[128,1024]{1,0:T(8,128)(2,1)S(1)}, bf16[128,1024]{1,0:T(8,128)(2,1)}, u32[]{:S(2)}) copy-start(bf16[128,1024]{1,0:T(8,128)(2,1)} %copy-done.41) | copy-start | bytes 786436
  689.3 30.4 %copy-start.44 = (bf16[128,1024]{1,0:T(8,128)(2,1)S(1)}, bf16[128,1024]{1,0:T(8,128)(2,1)}, u32[]{:S(2)}) copy-start(bf16[128,1024]{1,0:T(8,128)(2,1)} %copy-done.43) | copy-start | bytes 786436
  689.3 30.4 %copy-start.46 = (bf16[128,1024]{1,0:T(8,128)(2,1)S(1)}, bf16[128,1024]{1,0:T(8,128)(2,1)}, u32[]{:S(2)}) copy-start(bf16[128,1024]{1,0:T(8,128)(2,1)} %copy-done.45) | copy-start | bytes 786436
  689.3 30.4 %copy-start.48 = (bf16[128,1024]{1,0:T(8,128)(2,1)S(1)}, bf16[128,1024]{1,0:T(8,128)(2,1)}, u32[]{:S(2)}) copy-start(bf16[128,1024]{1,0:T(8,128)(2,1)} %copy-done.47) | copy-start | bytes 786436
  725.5 39.3 %copy-start.67 = (pred[1152]{0:T(1024)(128)(4,1)S(1)}, pred[1152]{0:T(1024)(128)(4,1)}, u32[]{:S(2)}) copy-start(pred[1152]{0:T(1024)(128)(4,1)} %constant.45.clone.1) | copy-start | bytes 3460
  898.3 35.0 %collective-permute-start.6 = (bf16[256,3072]{1,0:T(8,128)(2,1)}, bf16[256,3072]{1,0:T(8,128)(2,1)}, u32[]{:S(2)}, u32[]{:S(2)}) collective-permute-start(bf16[256,3072]{1,0:T(8,128)(2,1)} %broadcast_select_fusion), channel_id=1, source_target_pairs={{0,64},{64,0},{1,65},{65,1},{2,66},{66,2},{3,67},{67,3},{4,68},{68... | collective-permute-start | bytes 4718600 | tf_op jit(solution)/shard_map/ppermute | solution.py:700
  902.0 4.8 copy-start.54
  906.8 2.5 copy-start.61
  906.8 26.5 %copy-start.55 = (bf16[256,3072]{1,0:T(8,128)(2,1)S(1)}, bf16[256,3072]{1,0:T(8,128)(2,1)}, u32[]{:S(2)}) copy-start(bf16[256,3072]{1,0:T(8,128)(2,1)} %reduce-scatter.5.cloned.1.call-done) | copy-start | bytes 4718596
  906.8 26.5 %copy-start.56 = (bf16[256,3072]{1,0:T(8,128)(2,1)S(1)}, bf16[256,3072]{1,0:T(8,128)(2,1)}, u32[]{:S(2)}) copy-start(bf16[256,3072]{1,0:T(8,128)(2,1)} %reduce-scatter.3.cloned.1.call-done) | copy-start | bytes 4718596
  (23 other events, 22.8 us)
Sparse Core Ops, SparseCore 0:
  23.1 38.9 all-gather.10
  63.8 31.4 all-gather.8
  97.6 25.9 all-gather.6
  125.1 26.0 all-gather.16
  153.2 26.0 all-gather.14
  181.4 26.0 all-gather.12
  420.8 88.3 reduce-scatter.4
  590.1 105.2 reduce-scatter.2

commit v2 on v1

v2 whole, which is shorter than its diff:
```python
import functools

import jax
import jax.numpy as jnp
from jax import lax
from jax.experimental import pallas as pl
from jax.experimental.pallas import tpu as pltpu

from jax.sharding import PartitionSpec as P

HEAD = 64
MESH = pl.DeviceIdType.MESH
bf16 = jnp.bfloat16
f32 = jnp.float32
norm_eps = 1e-06
masked_score = -1e30
rope_base = 10000.0


def ring_places():
    me = lax.axis_index("expert")
    z, x = lax.div(me, 4), lax.rem(me, 4)
    xr, xl = lax.rem(x + 1, 4), lax.rem(x + 3, 4)
    zr, zl = lax.rem(z + 1, 4), lax.rem(z + 3, 4)
    near = (z * 4 + xr, z * 4 + xl, zr * 4 + x, zl * 4 + x)
    return z, x, xr, xl, zr, zl, near


def gather_kernel(kind, x_ref, *refs):
    split = kind != "plain"
    if kind == "weights":
        side_ref, wq_ref, wk_ref, wv_ref, wo_ref, out_all, side_out = refs[:7]
    elif split:
        side_ref, out_all, side_out = refs[:3]
    else:
        out_all = refs[0]
    send, recv, own_sem = refs[-3:]
    z, x, xr, xl, zr, zl, (dxr, dxl, dzr, dzl) = ring_places()
    x2, z2 = lax.rem(x + 2, 4), lax.rem(z + 2, 4)
    section, dp = lax.axis_index("section"), lax.axis_index("dp")
    core = lax.rem(dp, 2)
    rows, cols = x_ref.shape
    half, quarter = rows // 2, rows // 4
    locals_ = []
    if kind == "weights":
        out_ref = out_all.at[1 - section, core]
        moves = (
            (wq_ref.at[:, :, :, pl.ds(0, 512)], 0, 0),
            (wq_ref.at[:, :, :, pl.ds(512, 512)], 1, 0),
            (wk_ref, 0, 64),
            (wv_ref, 1, 64),
            (wo_ref.at[:, :, :, pl.ds(0, 512)], 0, 128),
            (wo_ref.at[:, :, :, pl.ds(512, 512)], 1, 128),
        )
        for i, (src, side, row) in enumerate(moves):
            dst = out_all.at[section, side, :, :, pl.ds(row, 64), pl.ds(0, 512)]
            c = pltpu.make_async_copy(src, dst, own_sem.at[1 + i])
            c.start()
            locals_.append(c)
    elif split:
        out_ref = out_all.at[core]
    else:
        out_ref = out_all
    own = pltpu.make_async_copy(x_ref, out_ref.at[z, x], own_sem.at[0])
    own.start()
    other_core, other_section = {"dp": dp + 1 - 2 * core}, {"section": 1 - section}
    barrier = pltpu.get_barrier_semaphore()
    greeted = [{"expert": d} for d in (dxr, dxl, dzr, dzl)]
    if split:
        greeted += [other_core, other_section]
    for to in greeted:
        pl.semaphore_signal(barrier, inc=1, device_id=to, device_id_type=MESH)
    pl.semaphore_wait(barrier, len(greeted))

    def send_to(i, src, dst, to):
        c = pltpu.make_async_remote_copy(
            src_ref=src, dst_ref=dst, send_sem=send.at[i], recv_sem=recv.at[i],
            device_id=to, device_id_type=MESH)
        c.start()
        return c

    def copy(i, src, dst, to):
        return send_to(i, src, dst, {"expert": to})

    forwards = []

    def forward(*piece):
        if split:
            there = out_ref.at[piece]
            forwards.append(send_to(17 + len(forwards), there, there, other_core))

    A, B = pl.ds(0, half), pl.ds(half, half)
    A0, A1 = pl.ds(0, quarter), pl.ds(quarter, quarter)
    B0, B1 = pl.ds(half, quarter), pl.ds(half + quarter, quarter)
    every = slice(None)
    a_r = copy(0, x_ref.at[A], out_ref.at[z, x, A], dxr)
    a_l = copy(1, x_ref.at[A], out_ref.at[z, x, A], dxl)
    b_r = copy(2, x_ref.at[B], out_ref.at[z, x, B], dzr)
    b_l = copy(3, x_ref.at[B], out_ref.at[z, x, B], dzl)
    if split:
        swap = send_to(16, side_ref, side_out, other_section)
    a_r.wait_recv()
    a2_r = copy(4, out_ref.at[z, xl, A0], out_ref.at[z, xl, A0], dxr)
    a_l.wait_recv()
    a2_l = copy(5, out_ref.at[z, xr, A1], out_ref.at[z, xr, A1], dxl)
    b_r.wait_recv()
    b2_r = copy(6, out_ref.at[zl, x, B0], out_ref.at[zl, x, B0], dzr)
    b_l.wait_recv()
    b2_l = copy(7, out_ref.at[zr, x, B1], out_ref.at[zr, x, B1], dzl)
    own.wait()
    a2_r.wait_recv()
    a2_l.wait_recv()
    c_r = copy(8, out_ref.at[z, :, A], out_ref.at[z, :, A], dzr)
    c_l = copy(9, out_ref.at[z, :, A], out_ref.at[z, :, A], dzl)
    b2_r.wait_recv()
    b2_l.wait_recv()
    d_r = copy(10, out_ref.at[:, x, B], out_ref.at[:, x, B], dxr)
    d_l = copy(11, out_ref.at[:, x, B], out_ref.at[:, x, B], dxl)
    forward(z, every, A)
    forward(every, x, B)
    c_r.wait_recv()
    c2_r = copy(12, out_ref.at[zl, :, A0], out_ref.at[zl, :, A0], dzr)
    c_l.wait_recv()
    c2_l = copy(13, out_ref.at[zr, :, A1], out_ref.at[zr, :, A1], dzl)
    d_r.wait_recv()
    d2_r = copy(14, out_ref.at[:, xl, B0], out_ref.at[:, xl, B0], dxr)
    d_l.wait_recv()
    d2_l = copy(15, out_ref.at[:, xr, B1], out_ref.at[:, xr, B1], dxl)
    forward(zl, every, A)
    forward(zr, every, A)
    forward(every, xl, B)
    forward(every, xr, B)
    c2_r.wait_recv()
    forward(z2, every, A0)
    c2_l.wait_recv()
    forward(z2, every, A1)
    d2_r.wait_recv()
    forward(every, x2, B0)
    d2_l.wait_recv()
    forward(every, x2, B1)
    for c in (a_r, a_l, b_r, b_l, a2_r, a2_l, b2_r, b2_l, c_r, c_l, d_r, d_l, c2_r, c2_l, d2_r, d2_l):
        c.wait_send()
    if split:
        for c in forwards + [swap]:
            c.wait_recv()
            c.wait_send()
    for c in locals_:
        c.wait()


def gather_call(ident, kind, outs, in_memory, *args):
    anywhere, memory = pl.BlockSpec(memory_space=pl.ANY), pl.BlockSpec(memory_space=pltpu.VMEM)
    return pl.pallas_call(
        functools.partial(gather_kernel, kind),
        out_shape=outs,
        in_specs=[memory if held else anywhere for held in in_memory],
        out_specs=[anywhere] * len(outs),
        scratch_shapes=[
            pltpu.SemaphoreType.DMA((27,)),
            pltpu.SemaphoreType.DMA((27,)),
            pltpu.SemaphoreType.DMA((7,)),
        ],
        compiler_params=pltpu.CompilerParams(
            collective_id=ident, has_side_effects=True, vmem_limit_bytes=56 << 20),
        name="gather_" + kind,
    )(*args)


def gather_rows(x, ident):
    rows, cols = x.shape
    out = gather_call(ident, "plain", [jax.ShapeDtypeStruct((4, 4, rows, cols), x.dtype)], (True,), x)[0]
    return out.reshape(16 * rows, cols)


def gather_split(x, side, ident):
    rows, cols = x.shape
    out, side_out = gather_call(
        ident, "split",
        [jax.ShapeDtypeStruct((2, 4, 4, rows, cols), x.dtype), jax.ShapeDtypeStruct(side.shape, side.dtype)],
        (True, False), x, side)
    return out.reshape(2, 16, rows, cols), side_out


def gather_weights(x, side, wq, wk, wv, wo, ident):
    rows, cols = x.shape
    parts = [w.reshape(4, 4, 64, w.shape[1]) for w in (wq, wk, wv, wo)]
    out, side_out = gather_call(
        ident, "weights",
        [jax.ShapeDtypeStruct((2, 2, 4, 4, rows, cols), x.dtype), jax.ShapeDtypeStruct(side.shape, side.dtype)],
        (True, False) + (True,) * 4, x, side, *parts)
    return out.reshape(2, 2, 16, rows, cols), side_out


def scatter_kernel(split, x_ref, out_ref, loc, *refs):
    if split:
        land, core_send, core_recv = refs[0], refs[-2], refs[-1]
        refs = refs[1:-2]
    s1, l1, l2, t0, m1, n1, m2, send, recv, loc_sem = refs
    z, x, xr, xl, zr, zl, (dxr, dxl, dzr, dzl) = ring_places()
    x2, z2 = lax.rem(x + 2, 4), lax.rem(z + 2, 4)
    dp = lax.axis_index("dp")
    core = lax.rem(dp, 2)
    rows = x_ref.shape[-2]
    half, quarter = rows // 2, rows // 4
    A0, A1 = pl.ds(0, quarter), pl.ds(quarter, quarter)
    B0, B1 = pl.ds(half, quarter), pl.ds(half + quarter, quarter)
    every = slice(None)
    pieces = (
        (z2, every, A0), (z2, every, A1), (every, x2, B0), (every, x2, B1),
        (zr, every, A1), (zl, every, A0), (every, xr, B1), (every, xl, B0),
        (zr, every, A0), (zl, every, A1), (every, xr, B0), (every, xl, B1),
        (z, every, A0), (z, every, A1), (every, x, B0), (every, x, B1),
    )
    part = x_ref.at[core] if split else x_ref
    skip = 0 if split else 8
    held = []
    for i, piece in enumerate(pieces[skip:]):
        c = pltpu.make_async_copy(part.at[piece], loc.at[i], loc_sem.at[i])
        c.start()
        held.append(c)
    other_core = {"dp": dp + 1 - 2 * core}
    barrier = pltpu.get_barrier_semaphore()
    greeted = [{"expert": d} for d in (dxr, dxl, dzr, dzl)] + ([other_core] if split else [])
    for to in greeted:
        pl.semaphore_signal(barrier, inc=1, device_id=to, device_id_type=MESH)
    pl.semaphore_wait(barrier, len(greeted))
    away = []
    if split:
        for i, piece in enumerate(pieces):
            c = pltpu.make_async_remote_copy(
                src_ref=x_ref.at[(1 - core,) + piece], dst_ref=land.at[i], send_sem=core_send.at[i],
                recv_sem=core_recv.at[i], device_id=other_core, device_id_type=MESH)
            c.start()
            away.append(c)

    def copy(i, src, dst, to):
        c = pltpu.make_async_remote_copy(
            src_ref=src, dst_ref=dst, send_sem=send.at[i], recv_sem=recv.at[i],
            device_id={"expert": to}, device_id_type=MESH)
        c.start()
        return c

    def total(*parts):
        acc = parts[0].astype(f32)
        for p in parts[1:]:
            acc = acc + p.astype(f32)
        return acc

    def ready(i):
        if i < skip:
            return x_ref.at[pieces[i]]
        held[i - skip].wait()
        if split:
            away[i].wait_recv()
            loc[i] = total(loc[i], land[i]).astype(bf16)
        return loc.at[i - skip]

    c0 = copy(0, ready(0), l1.at[0], dzr)
    c1 = copy(1, ready(1), l1.at[1], dzl)
    c2 = copy(2, ready(2), l1.at[2], dxr)
    c3 = copy(3, ready(3), l1.at[3], dxl)
    c4 = copy(4, ready(4), l2.at[0, 1], dzr)
    c5 = copy(5, ready(5), l2.at[1, 0], dzl)
    c6 = copy(6, ready(6), l2.at[2, 1], dxr)
    c7 = copy(7, ready(7), l2.at[3, 0], dxl)
    mine = ready(8)
    c0.wait_recv()
    s1[0] = total(mine[...], l1[0]).astype(bf16)
    c8 = copy(8, s1.at[0], l2.at[0, 0], dzr)
    mine = ready(9)
    c1.wait_recv()
    s1[1] = total(mine[...], l1[1]).astype(bf16)
    c9 = copy(9, s1.at[1], l2.at[1, 1], dzl)
    mine = ready(10)
    c2.wait_recv()
    s1[2] = total(mine[...], l1[2]).astype(bf16)
    c10 = copy(10, s1.at[2], l2.at[2, 0], dxr)
    mine = ready(11)
    c3.wait_recv()
    s1[3] = total(mine[...], l1[3]).astype(bf16)
    c11 = copy(11, s1.at[3], l2.at[3, 1], dxl)
    mine = ready(13)
    c4.wait_recv()
    c9.wait_recv()
    t0[0, 1] = total(mine[...], l2[0, 1], l2[1, 1]).astype(bf16)
    mine = ready(12)
    c5.wait_recv()
    c8.wait_recv()
    t0[0, 0] = total(mine[...], l2[0, 0], l2[1, 0]).astype(bf16)
    e0 = copy(12, t0.at[0, 0, x2], m1.at[0], dxr)
    e1 = copy(13, t0.at[0, 1, x2], m1.at[1], dxl)
    e4 = copy(14, t0.at[0, 1, xr], m2.at[0, 1], dxr)
    e5 = copy(15, t0.at[0, 0, xl], m2.at[1, 0], dxl)
    mine = ready(15)
    c6.wait_recv()
    c11.wait_recv()
    t0[1, 1] = total(mine[...], l2[2, 1], l2[3, 1]).astype(bf16)
    mine = ready(14)
    c7.wait_recv()
    c10.wait_recv()
    t0[1, 0] = total(mine[...], l2[2, 0], l2[3, 0]).astype(bf16)
    e2 = copy(16, t0.at[1, 0, z2], m1.at[2], dzr)
    e3 = copy(17, t0.at[1, 1, z2], m1.at[3], dzl)
    e6 = copy(18, t0.at[1, 1, zr], m2.at[2, 1], dzr)
    e7 = copy(19, t0.at[1, 0, zl], m2.at[3, 0], dzl)
    e0.wait_recv()
    n1[0] = total(t0[0, 0, xr], m1[0]).astype(bf16)
    e8 = copy(20, n1.at[0], m2.at[0, 0], dxr)
    e1.wait_recv()
    n1[1] = total(t0[0, 1, xl], m1[1]).astype(bf16)
    e9 = copy(21, n1.at[1], m2.at[1, 1], dxl)
    e2.wait_recv()
    n1[2] = total(t0[1, 0, zr], m1[2]).astype(bf16)
    e10 = copy(22, n1.at[2], m2.at[2, 0], dzr)
    e3.wait_recv()
    n1[3] = total(t0[1, 1, zl], m1[3]).astype(bf16)
    e11 = copy(23, n1.at[3], m2.at[3, 1], dzl)
    e4.wait_recv()
    e9.wait_recv()
    out_ref[A1] = total(t0[0, 1, x], m2[0, 1], m2[1, 1])
    e5.wait_recv()
    e8.wait_recv()
    out_ref[A0] = total(t0[0, 0, x], m2[0, 0], m2[1, 0])
    e6.wait_recv()
    e11.wait_recv()
    out_ref[B1] = total(t0[1, 1, z], m2[2, 1], m2[3, 1])
    e7.wait_recv()
    e10.wait_recv()
    out_ref[B0] = total(t0[1, 0, z], m2[2, 0], m2[3, 0])
    for c in (c0, c1, c2, c3, c4, c5, c6, c7, c8, c9, c10, c11,
              e0, e1, e2, e3, e4, e5, e6, e7, e8, e9, e10, e11):
        c.wait_send()
    for c in away:
        c.wait_send()


def scatter_sum(x, ident, split=False):
    rows, cols = x.shape[-2] // 16, x.shape[-1]
    q = rows // 4
    piece = (4, q, cols)
    count = 16 if split else 8
    scratch = [pltpu.VMEM((count,) + piece, bf16)]
    if split:
        scratch.append(pltpu.VMEM((16,) + piece, bf16))
    scratch += [
        pltpu.VMEM((4,) + piece, bf16),
        pltpu.VMEM((4,) + piece, bf16),
        pltpu.VMEM((4, 2) + piece, bf16),
        pltpu.VMEM((2, 2) + piece, bf16),
        pltpu.VMEM(piece, bf16),
        pltpu.VMEM(piece, bf16),
        pltpu.VMEM((4, 2, q, cols), bf16),
        pltpu.SemaphoreType.DMA((24,)),
        pltpu.SemaphoreType.DMA((24,)),
        pltpu.SemaphoreType.DMA((count,)),
    ]
    if split:
        scratch += [pltpu.SemaphoreType.DMA((16,)), pltpu.SemaphoreType.DMA((16,))]
    return pl.pallas_call(
        functools.partial(scatter_kernel, split),
        out_shape=jax.ShapeDtypeStruct((rows, cols), f32),
        in_specs=[pl.BlockSpec(memory_space=pl.ANY)],
        out_specs=pl.BlockSpec(memory_space=pltpu.VMEM),
        scratch_shapes=scratch,
        compiler_params=pltpu.CompilerParams(
            collective_id=ident, has_side_effects=True, vmem_limit_bytes=56 << 20),
        name="scatter_split" if split else "scatter_sum",
    )(x.reshape(x.shape[:-2] + (4, 4, rows, cols)))


def spec(shape, index):
    return pl.BlockSpec(shape, index)


def fixed(shape):
    return pl.BlockSpec(shape, lambda *_: (0,) * len(shape), pipeline_mode=pl.Buffered(1))


def whole():
    return pl.BlockSpec(memory_space=pltpu.VMEM)


def local_call(kernel, outs, name, grid=None, in_specs=None, out_specs=None, flops=0, moved=0):
    params = pltpu.CompilerParams(vmem_limit_bytes=52 << 20)
    kinds = dict(
        out_shape=[jax.ShapeDtypeStruct(s, d) for s, d in outs],
        compiler_params=params,
        name=name,
        cost_estimate=pl.CostEstimate(flops=flops, bytes_accessed=moved, transcendentals=0),
    )
    if grid is None:
        kinds["out_specs"] = [spec(s, lambda i, n=len(s): (0,) * n) for s, _ in outs]
        blocks = in_specs or {}

        def call(*args):
            ins = [blocks.get(i) or spec(a.shape, lambda i, n=a.ndim: (0,) * n) for i, a in enumerate(args)]
            return pl.pallas_call(kernel, grid=(1,), in_specs=ins, **kinds)(*args)

        return call
    return pl.pallas_call(kernel, grid=grid, in_specs=in_specs, out_specs=out_specs, **kinds)


def dot(a, b):
    return jnp.dot(a, b, preferred_element_type=f32)


def dot_t(a, b):
    return lax.dot_general(a, b, (((1,), (1,)), ((), ())), preferred_element_type=f32)


def t_dot(a, b):
    return lax.dot_general(a, b, (((0,), (0,)), ((), ())), preferred_element_type=f32)


def lanes(shape):
    return lax.broadcasted_iota(jnp.int32, shape, len(shape) - 1)


def turned(u, cosine, sine):
    chunks = []
    for c in range(u.shape[1] // 128):
        part = u[:, 128 * c : 128 * c + 128]
        low = lax.rem(lanes(part.shape), 64) < 32
        rot = jnp.where(low, -pltpu.roll(part, 96, 1), pltpu.roll(part, 32, 1))
        chunks.append(part * cosine + rot * sine)
    return jnp.concatenate(chunks, axis=1)


def rms(x):
    return lax.rsqrt(jnp.mean(x * x, axis=-1, keepdims=True) + norm_eps)


def halves(w_ref, row):
    return tuple(w_ref[0, h, :, row : row + 64, 0:512].reshape(1024, 512) for h in range(2))


def pre_kernel(x_ref, gain_ref, cos_ref, sin_ref, w_ref, a_ref, q_ref, kv_ref):
    x = x_ref[...].astype(f32)
    a = (x * rms(x) * gain_ref[...]).astype(bf16)
    a_ref[...] = a
    cosine, sine = cos_ref[...], sin_ref[...]
    for h, w in enumerate(halves(w_ref, 0)):
        q_ref[:, 512 * h : 512 * h + 512] = turned(dot(a, w), cosine, sine).astype(bf16)
    wk, wv = halves(w_ref, 64)
    kv_ref[:, :512] = turned(dot(a, wk), cosine, sine).astype(bf16)
    kv_ref[:, 512:] = dot(a, wv).astype(bf16)


def head_rows(q):
    q = q.astype(f32)
    left, right = q[:, :128], q[:, 128:]
    low = lanes(left.shape) < 64
    parts = [
        jnp.where(low, left, 0.0),
        jnp.where(low, pltpu.roll(left, 64, 1), 0.0),
        jnp.where(low, 0.0, pltpu.roll(right, 64, 1)),
        jnp.where(low, 0.0, right),
    ]
    return parts


def head_lanes(p0, p1, p2, p3):
    low = lanes(p0.shape) < 64
    left = jnp.where(low, p0, pltpu.roll(p1, 64, 1))
    right = jnp.where(low, pltpu.roll(p2, 64, 1), p3)
    return jnp.concatenate([left, right], axis=1)


def attend_kernel(q_ref, k_ref, v_ref, lo_ref, hi_ref, o_ref, p_ref):
    key = lax.broadcasted_iota(jnp.int32, (128, 2048), 1)
    seen = (key >= lo_ref[...]) & (key <= hi_ref[...])
    k, v = k_ref[...], v_ref[...]
    outs = []
    for h, q in enumerate(head_rows(q_ref[...])):
        s = dot_t((q * 0.125).astype(bf16), k)
        s = jnp.where(seen, s, masked_score)
        e = jnp.exp(s - jnp.max(s, axis=-1, keepdims=True))
        p = (e * (1.0 / jnp.sum(e, axis=-1, keepdims=True))).astype(bf16)
        p_ref[0, 128 * h : 128 * h + 128, :] = p
        outs.append(dot(p, v))
    o_ref[...] = head_lanes(*outs).astype(bf16)


def attend(q, kv, lo, hi):
    return local_call(
        attend_kernel,
        [((128, 1024), bf16), ((4, 512, 2048), bf16)],
        "attend",
        grid=(4,),
        in_specs=[
            spec((128, 256), lambda i: (0, i)),
            spec((2048, 128), lambda i: (0, i)),
            spec((2048, 128), lambda i: (0, i + 4)),
            fixed((128, 1)),
            fixed((128, 1)),
        ],
        out_specs=[
            spec((128, 256), lambda i: (0, i)),
            spec((1, 512, 2048), lambda i: (i, 0, 0)),
        ],
        flops=2 * 2 * 2048 * 2048 * 128,
        moved=13 << 20,
    )(q, kv, kv, lo, hi)


def attend_back_kernel(q_ref, o_ref, do_ref, k_ref, v_ref, p_ref, dq_ref, dkv_ref):
    k, v = k_ref[...], v_ref[...]
    do = do_ref[...]
    prod = do.astype(f32) * o_ref[...].astype(f32)
    low = lanes((128, 128)) < 64
    left, right = prod[:, :128], prod[:, 128:]
    deltas = [
        jnp.sum(jnp.where(low, left, 0.0), axis=1, keepdims=True),
        jnp.sum(jnp.where(low, 0.0, left), axis=1, keepdims=True),
        jnp.sum(jnp.where(low, right, 0.0), axis=1, keepdims=True),
        jnp.sum(jnp.where(low, 0.0, right), axis=1, keepdims=True),
    ]
    do_rows = [r.astype(bf16) for r in head_rows(do)]
    q_rows = [(r * 0.125).astype(bf16) for r in head_rows(q_ref[...])]
    dqs, dss = [], []
    for h in range(4):
        dp = dot_t(do_rows[h], v)
        p = p_ref[0, 128 * h : 128 * h + 128, :].astype(f32)
        ds = (p * (dp - deltas[h])).astype(bf16)
        dss.append(ds)
        dqs.append(dot(ds, k) * 0.125)
    dq_ref[...] = head_lanes(*dqs)
    dkv_ref[:, :128] = t_dot(jnp.concatenate(dss, axis=0), jnp.concatenate(q_rows, axis=0)).astype(bf16)
    dkv_ref[:, 128:] = t_dot(p_ref[0], jnp.concatenate(do_rows, axis=0)).astype(bf16)


def attend_back(q, o, do, kv, probs):
    side = spec((128, 256), lambda i: (0, i))
    return local_call(
        attend_back_kernel,
        [((128, 1024), f32), ((2048, 1024), bf16)],
        "attend_back",
        grid=(4,),
        in_specs=[
            side,
            side,
            side,
            spec((2048, 128), lambda i: (0, i)),
            spec((2048, 128), lambda i: (0, i + 4)),
            spec((1, 512, 2048), lambda i: (i, 0, 0)),
        ],
        out_specs=[side, spec((2048, 256), lambda i: (0, i))],
        flops=4 * 2 * 2048 * 2048 * 128,
        moved=17 << 20,
    )(q, o, do, kv, kv, probs)


def post_kernel(x_ref, o_ref, wo_ref, gain_ref, h_ref, b_ref):
    o = o_ref[...]
    h = x_ref[...].astype(f32) + jnp.concatenate([dot(o, w) for w in halves(wo_ref, 0)], axis=1)
    h_ref[...] = h
    b_ref[...] = (h * rms(h) * gain_ref[...]).astype(bf16)


def chosen_gates(b, wr, mask):
    logits = dot(b, wr)
    chosen = mask.astype(f32) > 0.5
    top = jnp.max(jnp.where(chosen, logits, masked_score), axis=-1, keepdims=True)
    e = jnp.where(chosen, jnp.exp(jnp.where(chosen, logits - top, 0.0)), 0.0)
    return e / jnp.sum(e, axis=-1, keepdims=True)


SLOTS = 80
ROWS = 1024


def experts_kernel(b_ref, mask_ref, wr_ref, pick_ref, w_ref, y_ref, x_ref, gu_ref, s_ref, gate_ref):
    row, col = lax.broadcasted_iota(jnp.int32, (256, 256), 0), lanes((256, 256))
    before = ((row < col) & ((row < 128) == (col < 128))).astype(bf16)
    slot_ids = lax.broadcasted_iota(jnp.int32, (SLOTS, 256), 0)
    second = jnp.where(lanes((1, 256)) < 128, 0.0, SLOTS // 2)
    for p in range(ROWS // 256):
        b = b_ref[256 * p : 256 * p + 256, :]
        mask = mask_ref[:, 256 * p : 256 * p + 256]
        chosen = mask.astype(f32) > 0.5
        logits = lax.dot_general(wr_ref[...], b, (((0,), (1,)), ((), ())), preferred_element_type=f32)
        top = jnp.max(jnp.where(chosen, logits, masked_score), axis=0, keepdims=True)
        e = jnp.where(chosen, jnp.exp(jnp.where(chosen, logits - top, 0.0)), 0.0)
        gates = e / jnp.sum(e, axis=0, keepdims=True)
        rank = dot(mask, before)
        for j in range(2):
            one = pick_ref[:, j : j + 1]
            gate = jnp.sum(gates * one, axis=0, keepdims=True)
            used = jnp.sum(mask.astype(f32) * one, axis=0, keepdims=True)
            place = jnp.sum(rank * one, axis=0, keepdims=True) + second
            hit = (slot_ids == place.astype(jnp.int32)) & (used > 0.5)
            s = jnp.where(hit, 1.0, 0.0)
            part = slice(SLOTS * p, SLOTS * p + SLOTS)
            gate_ref[j, part, :] = jnp.sum(s * gate, axis=1, keepdims=True)
            s = s.astype(bf16)
            s_ref[p, SLOTS * j : SLOTS * j + SLOTS, :] = s
            x_ref[j, part, :] = dot(s, b).astype(bf16)
    ys = []
    for j in range(2):
        x = x_ref[j]
        g = dot(x, w_ref[j, :, 0:512])
        u = dot(x, w_ref[j, :, 512:1024])
        gu_ref[j, :, 0:512] = g.astype(bf16)
        gu_ref[j, :, 512:1024] = u.astype(bf16)
        inner = g * jax.nn.sigmoid(g) * u
        ys.append(dot_t((inner * gate_ref[j]).astype(bf16), w_ref[j, :, 1024:1536]).astype(bf16))
    for p in range(ROWS // 256):
        part = slice(SLOTS * p, SLOTS * p + SLOTS)
        both = jnp.concatenate([ys[0][part], ys[1][part]], axis=0)
        y_ref[256 * p : 256 * p + 256, :] = t_dot(s_ref[p], both).astype(bf16)


HALF = SLOTS * ROWS // 256
FULL = 2 * HALF


def compact(cols):
    return spec((2, HALF, cols), lambda i: (0, i, 0))


def tokens(cols):
    return spec((ROWS, cols), lambda i: (i, 0))


choice = spec((ROWS // 256, 2 * SLOTS, 256), lambda i: (i, 0, 0))


def experts(b_all, mask_all, wr, pick, w):
    rows = b_all.shape[0]
    return local_call(
        experts_kernel,
        [
            ((rows, 1024), bf16), ((2, FULL, 1024), bf16), ((2, FULL, 1024), bf16),
            ((rows // 256, 2 * SLOTS, 256), bf16), ((2, FULL, 1), f32),
        ],
        "experts",
        grid=(rows // ROWS,),
        in_specs=[
            tokens(1024),
            spec((32, ROWS), lambda i: (0, i)),
            fixed((1024, 32)),
            fixed((32, 8)),
            fixed((2, 1024, 1536)),
        ],
        out_specs=[tokens(1024), compact(1024), compact(1024), choice, compact(1)],
        flops=8 * 2 * 1280 * 1024 * 512,
        moved=20 << 20,
    )(b_all, mask_all, wr, pick, w)


def experts_back_kernel(
    dout_ref, s_ref, gu_ref, gate_ref, wcol_ref, w_ref, db_ref, d_ref, dgu_ref, in_ref, coef_ref
):
    for p in range(ROWS // 256):
        rows = dot(s_ref[p], dout_ref[256 * p : 256 * p + 256, :]).astype(bf16)
        for j in range(2):
            d_ref[j, SLOTS * p : SLOTS * p + SLOTS, :] = rows[SLOTS * j : SLOTS * j + SLOTS]
    dbs = []
    for j in range(2):
        gate = gate_ref[j]
        g = gu_ref[j, :, 0:512].astype(f32)
        u = gu_ref[j, :, 512:1024].astype(f32)
        back = dot(d_ref[j], w_ref[j, :, 1024:1536])
        sig = jax.nn.sigmoid(g)
        silu = g * sig
        inner = silu * u
        coef = gate * jnp.sum(inner * back, axis=1, keepdims=True)
        coef_ref[j] = coef
        in_ref[j] = (inner * gate).astype(bf16)
        dinner = back * gate
        dg = (dinner * u * sig * (1.0 + g * (1.0 - sig))).astype(bf16)
        du = (dinner * silu).astype(bf16)
        dgu_ref[j, :, 0:512] = dg
        dgu_ref[j, :, 512:1024] = du
        db = dot_t(dg, w_ref[j, :, 0:512]) + dot_t(du, w_ref[j, :, 512:1024])
        dbs.append((db + coef * wcol_ref[j : j + 1, :]).astype(bf16))
    for p in range(ROWS // 256):
        part = slice(SLOTS * p, SLOTS * p + SLOTS)
        both = jnp.concatenate([dbs[0][part], dbs[1][part]], axis=0)
        db_ref[256 * p : 256 * p + 256, :] = t_dot(s_ref[p], both).astype(bf16)


def experts_back(dout_all, choices, gu, gate, wcol, w):
    rows = dout_all.shape[0]
    return local_call(
        experts_back_kernel,
        [
            ((rows, 1024), bf16), ((2, FULL, 1024), bf16), ((2, FULL, 1024), bf16),
            ((2, FULL, 512), bf16), ((2, FULL, 1), f32),
        ],
        "experts_back",
        grid=(rows // ROWS,),
        in_specs=[
            tokens(1024), choice, compact(1024), compact(1), fixed((8, 1024)), fixed((2, 1024, 1536)),
        ],
        out_specs=[tokens(1024), compact(1024), compact(1024), compact(512), compact(1)],
        flops=8 * 2 * 1280 * 1024 * 512,
        moved=24 << 20,
    )(dout_all, choices, gu, gate, wcol, w)


def expert_grads_kernel(x_ref, d_ref, dgu_ref, in_ref, out_ref):
    which = pl.program_id(1)

    @pl.when(which < 2)
    def _():
        out_ref[0] = t_dot(x_ref[0], dgu_ref[0]).astype(bf16)

    @pl.when(which == 2)
    def _():
        out_ref[0] = t_dot(d_ref[0], in_ref[0]).astype(bf16)


def expert_grads(x, d, dgu, inner):
    return local_call(
        expert_grads_kernel,
        [((2, 1024, 1536), bf16)],
        "expert_grads",
        grid=(2, 3),
        in_specs=[
            spec((1, FULL, 1024), lambda j, c: (j, 0, 0)),
            spec((1, FULL, 1024), lambda j, c: (j, 0, 0)),
            spec((1, FULL, 512), lambda j, c: (j, 0, jnp.minimum(c, 1))),
            spec((1, FULL, 512), lambda j, c: (j, 0, 0)),
        ],
        out_specs=[spec((1, 1024, 512), lambda j, c: (j, 0, c))],
        flops=3 * 2 * 1280 * 1024 * 512,
        moved=16 << 20,
    )(x, d, dgu, inner)[0]


def mid_back_kernel(
    sum_ref, dout_ref, mix_ref, h_ref, b_ref, gain_ref, wr_ref, mask_ref, wo_ref,
    dh_ref, dattn_ref, do_ref, router_ref, gain_grad_ref,
):
    dout = dout_ref[...].astype(f32)
    b = b_ref[...]
    wr = wr_ref[...]
    h = h_ref[...]
    r = rms(h)
    n = h * r
    gates = chosen_gates(b, wr, mask_ref[...])
    level = jnp.sum(dout * mix_ref[...], axis=-1, keepdims=True)
    taken = (gates * -level).astype(bf16)
    router_ref[...] = t_dot(b, taken)
    db = sum_ref[...] + dot_t(taken, wr)
    gain_grad_ref[...] = jnp.broadcast_to(jnp.sum(db * n, axis=0, keepdims=True), gain_grad_ref.shape)
    ng = db * gain_ref[...]
    dh = dout + r * (ng - n * jnp.mean(ng * n, axis=-1, keepdims=True))
    dh_ref[...] = dh
    dattn = dh.astype(bf16)
    dattn_ref[...] = dattn
    w0, w1 = halves(wo_ref, 0)
    do_ref[...] = (dot_t(dattn[:, :512], w0) + dot_t(dattn[:, 512:], w1)).astype(bf16)


def end_back_kernel(
    dq_ref, dkv_ref, cos_ref, sin_ref, w_ref, x_ref, gain_ref, dh_ref,
    dq_lin_ref, dkv_lin_ref, dx_ref, gain_grad_ref,
):
    cosine, sine = cos_ref[...], -sin_ref[...]
    dq = turned(dq_ref[...], cosine, sine).astype(bf16)
    dkv = dkv_ref[...]
    dk = jnp.concatenate([dkv[:, 256 * i : 256 * i + 128] for i in range(4)], axis=1)
    dv = jnp.concatenate([dkv[:, 256 * i + 128 : 256 * i + 256] for i in range(4)], axis=1)
    dk = turned(dk, cosine, sine).astype(bf16)
    dv = dv.astype(bf16)
    dq_lin_ref[...] = dq
    dkv_lin_ref[:, :512] = dk
    dkv_lin_ref[:, 512:] = dv
    (q0, q1), (wk, wv) = halves(w_ref, 0), halves(w_ref, 64)
    da = dot_t(dq[:, :512], q0) + dot_t(dq[:, 512:], q1) + dot_t(dk, wk) + dot_t(dv, wv)
    x = x_ref[...].astype(f32)
    r = rms(x)
    n = x * r
    gain_grad_ref[...] = jnp.broadcast_to(jnp.sum(da * n, axis=0, keepdims=True), gain_grad_ref.shape)
    ng = da * gain_ref[...]
    dx = dh_ref[...] + r * (ng - n * jnp.mean(ng * n, axis=-1, keepdims=True))
    dx_ref[...] = dx.astype(bf16)


def dense_grads_kernel(a_ref, o_ref, dq_ref, dkv_ref, dattn_ref, *rest):
    small_ref, out_ref = rest if len(rest) == 2 else (None, rest[0])
    a = a_ref[...]
    gq = t_dot(a, dq_ref[...]).astype(bf16)
    gkv = t_dot(a, dkv_ref[...]).astype(bf16)
    go = t_dot(o_ref[...], dattn_ref[...]).astype(bf16)
    for t in range(2):
        part = slice(64 * t, 64 * t + 64)
        for h in range(2):
            side = slice(512 * h, 512 * h + 512)
            out_ref[h, t, 0:64, 0:512] = gq[part, side]
            out_ref[h, t, 64:128, 0:512] = gkv[part, side]
            out_ref[h, t, 128:192, 0:512] = go[part, side]
            if small_ref is not None:
                out_ref[h, t, 0:64, 512:640] = small_ref[h, part, :]
                out_ref[h, t, 64:192, 512:640] = jnp.zeros((128, 128), bf16)


def dense_grads(a, o, dq, dkv, dattn, small=None):
    cols = 512 if small is None else 640
    narrow = spec((128, 128), lambda i: (0, i))
    args = (a, o, dq, dkv, dattn) + (() if small is None else (small,))
    out = local_call(
        dense_grads_kernel,
        [((2, 16, 192, cols), bf16)],
        "dense_grads",
        grid=(8,),
        in_specs=[narrow, narrow] + [fixed((128, 1024))] * 3
        + ([] if small is None else [spec((2, 128, 128), lambda i: (0, i, 0))]),
        out_specs=[spec((2, 2, 192, cols), lambda i: (0, i, 0, 0))],
        flops=3 * 2 * 128 * 1024 * 1024,
        moved=8 << 20,
    )(*args)[0]
    return out.reshape(2, 3072, cols)


def cross_kernel(own_ref, other_ref, out_ref, land, mine, send, recv):
    section, dp = lax.axis_index("section"), lax.axis_index("dp")
    partners = (
        {"section": 1 - section},
        {"dp": lax.rem(dp + 2, 4)},
    )
    barrier = pltpu.get_barrier_semaphore()
    for to in partners:
        pl.semaphore_signal(barrier, inc=1, device_id=to, device_id_type=MESH)
    pl.semaphore_wait(barrier, 2)
    copies = []
    for i, to in enumerate(partners):
        src = other_ref if i == 0 else mine
        c = pltpu.make_async_remote_copy(
            src_ref=src, dst_ref=land.at[i], send_sem=send.at[i], recv_sem=recv.at[i],
            device_id=to, device_id_type=MESH)
        c.start()
        copies.append(c)
        c.wait_recv()
        before = own_ref[...] if i == 0 else mine[...].astype(f32)
        after = (before + land[i].astype(f32)).astype(bf16)
        if i == 0:
            mine[...] = after
        else:
            out_ref[...] = after
    for c in copies:
        c.wait_send()


def cross_sum(own, other, ident):
    rows, cols = own.shape
    return pl.pallas_call(
        cross_kernel,
        out_shape=jax.ShapeDtypeStruct((rows, cols), bf16),
        in_specs=[whole(), whole()],
        out_specs=whole(),
        scratch_shapes=[
            pltpu.VMEM((2, rows, cols), bf16),
            pltpu.VMEM((rows, cols), bf16),
            pltpu.SemaphoreType.DMA((2,)),
            pltpu.SemaphoreType.DMA((2,)),
        ],
        compiler_params=pltpu.CompilerParams(
            collective_id=ident, has_side_effects=True, vmem_limit_bytes=24 << 20),
        name="cross_sum",
    )(own, other)


def qkv_block(layer):
    return spec((1, 2, 16, 128, 640), lambda i: (layer, 0, 0, 0, 0))


def out_block(layer):
    return spec((1, 2, 16, 64, 640), lambda i: (layer, 0, 0, 2, 0))


def forward(x, layer, place, weights, dense, w, masks):
    cosine, sine, lo, hi, pick, _ = place
    gain_attn, gain_moe, wr = dense
    a, q, kv = local_call(
        pre_kernel, [((128, 1024), bf16)] * 3, "pre", in_specs={4: qkv_block(layer)},
        flops=2 * 128 * 1024 * 2048, moved=6 << 20,
    )(x, gain_attn, cosine, sine, weights)
    kv_all = gather_rows(kv, 1)
    o, probs = attend(q, kv_all, lo, hi)
    h, b = local_call(
        post_kernel, [((128, 1024), f32), ((128, 1024), bf16)], "post", in_specs={2: out_block(layer)},
        flops=2 * 128 * 1024 * 1024, moved=4 << 20,
    )(x, o, weights, gain_moe)
    b_all = gather_rows(b, 1)
    y, rows, gu, choices, gate = experts(b_all, masks[1], wr, pick, w)
    mix = scatter_sum(y, 2)
    out = (h + mix).astype(bf16)
    return out, (x, a, q, kv_all, o, probs, h, b, rows, gu, choices, gate, mix)


def backward(dout, saved, layer, place, weights, dense, w, masks):
    cosine, sine, lo, hi, pick, pick_rows = place
    gain_attn, gain_moe, wr = dense
    x, a, q, kv_all, o, probs, h, b, rows, gu, choices, gate, mix = saved
    dout_all = gather_rows(dout, 1)
    wcol = dot_t(pick_rows.astype(bf16), wr)
    db_part, drows, dgu, inner, coef = experts_back(dout_all, choices, gu, gate, wcol, w)
    db_sum = scatter_sum(db_part, 2)
    expert_grad = lax.psum_scatter(
        expert_grads(rows, drows, dgu, inner), "dp", scatter_dimension=1, tiled=True)
    router_cols = jnp.einsum("jrd,jr->jd", rows, coef[:, :, 0].astype(bf16), preferred_element_type=f32)
    router_part = jnp.einsum(
        "jd,je->de", router_cols, pick_rows[:2], preferred_element_type=f32, precision=lax.Precision.HIGHEST)
    dh, dattn, do, router_own, gain_moe_grad = local_call(
        mid_back_kernel,
        [((128, 1024), f32), ((128, 1024), bf16), ((128, 1024), bf16), ((1024, 32), f32), ((8, 1024), f32)],
        "mid_back", in_specs={8: out_block(layer)}, flops=2 * 128 * 1024 * 1024, moved=5 << 20,
    )(db_sum, dout, mix, h, b, gain_moe, wr, masks[0], weights)
    dq, dkv = attend_back(q, o, do, kv_all, probs)
    dkv_sum = scatter_sum(dkv, 2)
    dq_lin, dkv_lin, dx, gain_attn_grad = local_call(
        end_back_kernel,
        [((128, 1024), bf16), ((128, 1024), bf16), ((128, 1024), bf16), ((8, 1024), f32)],
        "end_back", in_specs={4: qkv_block(layer)}, flops=2 * 128 * 1024 * 2048, moved=8 << 20,
    )(dq, dkv_sum, cosine, sine, weights, x, gain_attn, dh)
    small = jnp.concatenate(
        [
            router_part + router_own,
            gain_attn_grad[0][:, None],
            gain_moe_grad[0][:, None],
            jnp.zeros((1024, 30), f32),
        ],
        axis=1,
    ).astype(bf16)
    return dx, expert_grad, (a, o, dq_lin, dkv_lin, dattn), small


def results_kernel(s_ref, query_ref, key_ref, value_ref, out_ref):
    for h in range(2):
        side = slice(512 * h, 512 * h + 512)
        query_ref[:, side] = s_ref[h, :, 0:64, 0:512].reshape(256, 512).astype(f32)
        out_ref[:, side] = s_ref[h, :, 128:192, 0:512].reshape(256, 512).astype(f32)
    key_ref[...] = s_ref[0, :, 64:128, 0:512].reshape(256, 512).astype(f32)
    value_ref[...] = s_ref[1, :, 64:128, 0:512].reshape(256, 512).astype(f32)


def results(summed):
    return local_call(
        results_kernel,
        [((1024, 1024), f32), ((1024, 512), f32), ((1024, 512), f32), ((1024, 1024), f32)],
        "results",
        grid=(4,),
        in_specs=[spec((2, 4, 192, 640), lambda i: (0, i, 0, 0))],
        out_specs=[spec((256, n), lambda i: (i, 0)) for n in (1024, 512, 512, 1024)],
        moved=20 << 20,
    )(summed)


def swapped(x):
    return lax.ppermute(x, "section", [(0, 1), (1, 0)])


def on_device(
    inputs, cotangent, offsets, routes, w_query, w_key, w_value, w_out,
    norm_attn, norm_moe, w_router, w_gate, w_up, w_down,
):
    section = lax.axis_index("section")
    expert = lax.axis_index("expert")
    first = section == 0

    def by_layer(own, other):
        return jnp.where(first, own, other), jnp.where(first, other, own)

    def mine(pair):
        return jnp.where(first, pair[0], pair[1])

    ids = lax.broadcasted_iota(jnp.int32, (1, 1, 1, 32), 3)
    mask_both = jnp.any(routes[0][:, :, :, None] == ids, axis=2).astype(bf16)
    mask_own = mine(mask_both)
    mask_away = jnp.where(first, mask_both[1], mask_both[0])
    start = expert * 64
    left = lax.rem(lax.axis_index("dp"), 2) == 0

    def part(w, there=True):
        if not there:
            return lax.dynamic_slice_in_dim(w, start, 64, axis=0)
        return lax.dynamic_slice(w, (start, jnp.where(left, 0, 512)), (64, 512))

    rows = jnp.concatenate(
        [part(w_query[0]), jnp.where(left, part(w_key[0], False), part(w_value[0], False)), part(w_out[0])],
        axis=0,
    )
    small = jnp.concatenate(
        [part(w_router[0], False), part(norm_attn[0][:, None], False), part(norm_moe[0][:, None], False),
         jnp.zeros((64, 30), bf16)], axis=1)
    extra = jnp.concatenate([mask_away, jnp.zeros((128, 32), bf16)], axis=1)
    extra = jnp.concatenate([extra, small], axis=0)
    extra = jnp.concatenate([extra, jnp.zeros((192, 64), bf16)], axis=1)
    payload = swapped(jnp.concatenate([rows, extra], axis=1))
    mask_other = payload[0:128, 512:544]
    own_rows = jnp.concatenate([mask_own, jnp.zeros((64, 32), bf16)], axis=0)
    payload = jnp.concatenate([payload[:, :576], own_rows, payload[:, 608:]], axis=1)
    shards = jnp.concatenate([w_gate[0], w_up[0], w_down[0]], axis=2)
    weights, away = gather_weights(payload, shards, w_query[0], w_key[0], w_value[0], w_out[0], 3)
    got = jnp.where(
        first,
        jnp.where(left, weights[1, 0, :, :, 512:], weights[1, 1, :, :, 512:]),
        jnp.where(left, weights[0, 0, :, :, 512:], weights[0, 1, :, :, 512:]),
    )
    other_small = got[:, 128:192, 0:64].reshape(1024, 64)
    all_other = got[:, 0:128, 0:32].reshape(2048, 32).T
    all_own = got[:, 0:128, 64:96].reshape(2048, 32).T
    pairs = [
        by_layer(norm_attn.astype(f32), other_small[:, 32][None].astype(f32)),
        by_layer(norm_moe.astype(f32), other_small[:, 33][None].astype(f32)),
        by_layer(w_router[0], other_small[:, :32]),
    ]
    dense = [tuple(p[l] for p in pairs) for l in range(2)]
    masks_own = by_layer(mask_own, mask_other)
    masks_all = by_layer(all_own, all_other)
    masks = [(masks_own[l], masks_all[l]) for l in range(2)]
    expert_w = [lax.all_gather(w, "dp", axis=1, tiled=True) for w in by_layer(shards, away)]

    seq = mine(offsets)
    local = expert * 128 + jnp.arange(128, dtype=jnp.int32)
    steps = jnp.arange(HEAD // 2, dtype=f32) * 2.0 / HEAD
    angles = (local - seq).astype(f32)[:, None] * (rope_base ** (-steps))[None, :]
    cosine = jnp.tile(jnp.cos(angles), (1, 4))
    sine = jnp.tile(jnp.sin(angles), (1, 4))
    pick_rows = (
        lax.broadcasted_iota(jnp.int32, (8, 32), 1)
        == 2 * expert + lax.broadcasted_iota(jnp.int32, (8, 32), 0)
    ).astype(f32)
    place = (cosine, sine, seq[:, None], local[:, None], pick_rows.T, pick_rows)

    x0 = mine(inputs)
    out0, saved0 = forward(x0, 0, place, weights, dense[0], expert_w[0], masks[0])
    out1, saved1 = forward(out0, 1, place, weights, dense[1], expert_w[1], masks[1])
    cot = mine(cotangent)
    dx1, eg1, dg1, small1 = backward(cot, saved1, 1, place, weights, dense[1], expert_w[1], masks[1])
    dense1 = scatter_sum(dense_grads(*dg1), 4, split=True)
    dx0, eg0, dg0, small0 = backward(dx1, saved0, 0, place, weights, dense[0], expert_w[0], masks[0])
    both_small = jnp.pad(jnp.stack([small0, small1]), ((0, 0), (0, 0), (0, 64)))
    dense0 = scatter_sum(dense_grads(*dg0, both_small), 5, split=True)

    def in_place(l0, l1):
        got = swapped(jnp.where(first, l1, l0))
        own = jnp.where(first, l0, l1)
        return jnp.stack([jnp.where(first, own, got), jnp.where(first, got, own)])[None]

    acts = in_place(out0, out1)
    in_grads = in_place(dx0, dx1)

    full1 = jnp.concatenate([dense1, dense0[:, 512:]], axis=1)
    own = jnp.where(first, dense0, full1)
    other = jnp.where(first, full1, dense0).astype(bf16)
    eg_sent = jnp.where(first, eg1, eg0)
    summed, eg_away = gather_split(cross_sum(own, other, 6), eg_sent, 7)
    grad_query, grad_key, grad_value, grad_out = results(summed)
    grad_small = mine(summed[:, :, 0:64, 512:576]).reshape(1024, 64).astype(f32)
    eg = jnp.where(first, eg0, eg1).astype(f32) + eg_away.astype(f32)
    return (
        acts,
        in_grads,
        grad_query[None],
        grad_key[None],
        grad_value[None],
        grad_out[None],
        grad_small[:, 32][None],
        grad_small[:, 33][None],
        grad_small[None, :, :32],
        eg[None, :, :, 0:512],
        eg[None, :, :, 512:1024],
        eg[None, :, :, 1024:1536],
    )


def solution(mesh):
    token = P(None, ("dp", "expert"), None)
    layer_token = P("section", None, ("dp", "expert"), None)
    matrix = P("section", None, None)
    gain = P("section", None)
    expert = P("section", "expert", "dp", None)
    return jax.shard_map(
        on_device,
        mesh=mesh,
        in_specs=(
            token, token, P(None, ("dp", "expert")), layer_token,
            matrix, matrix, matrix, matrix, gain, gain, matrix, expert, expert, expert,
        ),
        out_specs=(
            layer_token, layer_token, matrix, matrix, matrix, matrix, gain, gain, matrix,
            expert, expert, expert,
        ),
        check_vma=False,
    )
```

time: 953 us -> 772 us (0.81)
  waiting for transfers between devices: 64.7 us -> 3.44 us
  matrix products: 41 us -> 4.37 us
  local copies, waits for them, and re-layouts: 63.8 us -> 30.1 us
  Pallas kernels: 700 us -> 676 us
  other arithmetic: 49.3 us -> 31.8 us
    ppermute x7 -> x3, waiting for transfers between devices: 64 us -> 2.67 us  [swapped(): return lax.ppermute(x, 'section', [(0, 1), (1, 0)])]
    pallas_call x1, Pallas kernels: 69.8 us -> 12 us  [cross_sum(): pl.pallas_call(cross_kernel, out_shape=jax.ShapeDtypeStruct((rows, cols),...]
    dot_general x6, matrix products: 41 us -> 4.37 us  [the longest x2 2.79 us: backward(): jnp.einsum('jrd,jr->jd', rows, coef[:, :, 0].astype(bf16), preferred_elem...]
    pallas_call x30 -> x33, Pallas kernels: 573 us -> 606 us  [the longest x8 245 us: gather_call(): pl.pallas_call(functools.partial(gather_kernel, kind), out_shape=outs, in...]
    unnamed x148 -> x118, local copies, waits for them, and re-layouts: 30.3 us -> 16.2 us
    slice x6 -> x3, local copies, waits for them, and re-layouts: 13.9 us -> 1 us  [the longest x1 0.9 us: on_device(): full1 = jnp.concatenate([dense1, dense0[:, 512:]], axis=1)]
    select_n x10 -> x6, other arithmetic: 17.6 us -> 5.68 us  [by_layer(): return (jnp.where(first, own, other), jnp.where(first, other, own))]
  transfers between devices with their start and end apart: 15 -> 7, of which waited for: 4 -> 1; matrix products, arithmetic and copies ran while one was open for 10% -> 4% of each run, Pallas kernels for 69% -> 72%
where the time goes in v2:
time: 772 us; the launch traced here: 765 us
  Pallas kernels  676 us (88%)
  other arithmetic  31.8 us (4%)
  local copies, waits for them, and re-layouts  30.1 us (4%)
  between operations  15.2 us (2%)
    pallas_call x8, Pallas kernels, gather_call(): pl.pallas_call(functools.partial(gather_kernel, kind), out_shape=outs, in...  245 us
    pallas_call x8, Pallas kernels, scatter_sum(): pl.pallas_call(functools.partial(scatter_kernel, split), out_shape=jax.Sh...  235 us
    pallas_call x2, Pallas kernels, attend(): local_call(attend_kernel, [((128, 1024), bf16), ((4, 512, 2048), bf16)],...  32.4 us
    pallas_call x2, Pallas kernels, experts(): local_call(experts_kernel, [((rows, 1024), bf16), ((2, FULL, 1024), bf16)...  29.2 us
    pallas_call x8, Pallas kernels, call(): return pl.pallas_call(kernel, grid=(1,), in_specs=ins, **kinds)(*args)  28 us
    pallas_call x2, Pallas kernels, experts_back(): local_call(experts_back_kernel, [((rows, 1024), bf16), ((2, FULL, 1024),...  27.3 us
    pallas_call x2, Pallas kernels, attend_back(): local_call(attend_back_kernel, [((128, 1024), f32), ((2048, 1024), bf16)]...  25.7 us
    pallas_call x2, Pallas kernels, expert_grads(): local_call(expert_grads_kernel, [((2, 1024, 1536), bf16)], 'expert_grads'...  21.8 us
  transfers between devices with their start and end apart: 7, of which 1 were waited for; matrix products, arithmetic and copies ran while one was open for 4% of the time, Pallas kernels for 72%

profile of v2, /device:TPU:1, one launch (start us, length us, event | category | flops | bytes accessed | tf_op | source)
XLA Modules:
  0.0 764.8 jit_solution(6295337125730313886)
XLA Ops:
  13.5 2.2 collective-permute-start
  15.7 2.6 pad_maximum_fusion.refs_0_
  18.3 2.7 collective-permute-done
  21.9 42.2 %gather_weights.1 = (bf16[2,2,4,4,192,640]{5,4,3,2,1,0:T(8,128)(2,1)}, bf16[2,256,1536]{2,1,0:T(8,128)(2,1)}) custom-call(bf16[192,640]{1,0:T(8,128)(2,1)} %fusion.28.x_ref, bf16[2,256,1536]{2,1,0:T(8,128)(2,1)} %pad_maximum_fusion.refs_0_, bf16[4,4,64,1024]{3,2,1,0:T(8,128)(2,1)} %bitcast.155, bf16[4,4,64,512]{3,2,1,0:T(8,128)(2,1)} %bitcast.165, ...), custom_call_target="tpu_custom_call" | custom-call | tf_op jit(solution)/shard_map/gather_weights/pallas_call | solution.py:153
  64.1 3.7 broadcast_select_fusion.1
  70.1 29.4 %gather_plain.10 = bf16[4,4,128,1024]{3,2,1,0:T(8,128)(2,1)} custom-call(bf16[128,1024]{1,0:T(8,128)(2,1)} %select_bitcast_fusion.2.x_ref.dout_ref), custom_call_target="tpu_custom_call" | custom-call | tf_op jit(solution)/shard_map/gather_plain/pallas_call | solution.py:153
  99.5 2.0 fusion.9
  102.0 3.4 pre.2
  106.8 27.6 %gather_plain.6 = bf16[4,4,128,1024]{3,2,1,0:T(8,128)(2,1)} custom-call(bf16[128,1024]{1,0:T(8,128)(2,1)} %copy-done.23), custom_call_target="tpu_custom_call" | custom-call | tf_op jit(solution)/shard_map/gather_plain/pallas_call | solution.py:153
  134.4 16.1 %attend.2 = (bf16[128,1024]{1,0:T(8,128)(2,1)S(1)}, bf16[4,512,2048]{2,1,0:T(8,128)(2,1)}) custom-call(bf16[128,1024]{1,0:T(8,128)(2,1)S(1)} %get-tuple-element.77.q_ref, bf16[2048,1024]{1,0:T(8,128)(2,1)} %bitcast.129, bf16[2048,1024]{1,0:T(8,128)(2,1)} %bitcast.130, s32[128,1]{1,0:T(8,128)S(1)} %copy.70.lo_ref, s32[128,1]{1,0:T(8,128)S(1)} %iota_add_fusion.hi_ref), custom_call_target="tpu_custom_call" | custom-call | flops 2147483648 | bytes 13631488 | tf_op jit(solution)/shard_map/attend/pallas_call | solution.py:485
  150.6 2.3 post.2
  153.6 30.1 %gather_plain.7 = bf16[4,4,128,1024]{3,2,1,0:T(8,128)(2,1)} custom-call(bf16[128,1024]{1,0:T(8,128)(2,1)} %copy-done.8), custom_call_target="tpu_custom_call" | custom-call | tf_op jit(solution)/shard_map/gather_plain/pallas_call | solution.py:153
  183.7 1.2 broadcast_select_fusion.3
  184.9 1.2 copy.71
  186.1 1.2 copy.76
  187.6 14.6 %experts.2 = (bf16[2048,1024]{1,0:T(8,128)(2,1)}, bf16[2,640,1024]{2,1,0:T(8,128)(2,1)}, bf16[2,640,1024]{2,1,0:T(8,128)(2,1)}, bf16[8,160,256]{2,1,0:T(8,128)(2,1)S(1)}, f32[2,640,1]{2,1,0:T(8,128)S(1)}) custom-call(bf16[2048,1024]{1,0:T(8,128)(2,1)} %bitcast.149, bf16[32,2048]{1,0:T(8,128)(2,1)S(1)} %bitcast.119, ...), custom_call_target="tpu_custom_call" | custom-call | flops 10737418240 | bytes 20971520 | tf_op jit(solution)/shard_map/experts/pallas_call | solution.py:630
  203.9 22.4 %scatter_sum.6.mix_ref = f32[128,1024]{1,0:T(8,128)} custom-call(bf16[4,4,128,1024]{3,2,1,0:T(8,128)(2,1)} %bitcast.145), custom_call_target="tpu_custom_call" | custom-call | tf_op jit(solution)/shard_map/scatter_sum/pallas_call | solution.py:359
  226.3 1.1 add_convert_fusion.3.x_ref
  227.4 3.4 pre.3
  231.4 25.0 %gather_plain.8 = bf16[4,4,128,1024]{3,2,1,0:T(8,128)(2,1)} custom-call(bf16[128,1024]{1,0:T(8,128)(2,1)} %copy-done.24), custom_call_target="tpu_custom_call" | custom-call | tf_op jit(solution)/shard_map/gather_plain/pallas_call | solution.py:153
  256.4 16.2 %attend.3 = (bf16[128,1024]{1,0:T(8,128)(2,1)S(1)}, bf16[4,512,2048]{2,1,0:T(8,128)(2,1)}) custom-call(bf16[128,1024]{1,0:T(8,128)(2,1)S(1)} %get-tuple-element.84.q_ref, bf16[2048,1024]{1,0:T(8,128)(2,1)} %bitcast.133, bf16[2048,1024]{1,0:T(8,128)(2,1)} %bitcast.134, s32[128,1]{1,0:T(8,128)S(1)} %copy.70.lo_ref, s32[128,1]{1,0:T(8,128)S(1)} %iota_add_fusion.hi_ref), custom_call_target="tpu_custom_call" | custom-call | flops 2147483648 | bytes 13631488 | tf_op jit(solution)/shard_map/attend/pallas_call | solution.py:485
  272.7 2.3 post.3
  276.5 23.6 %gather_plain.9 = bf16[4,4,128,1024]{3,2,1,0:T(8,128)(2,1)} custom-call(bf16[128,1024]{1,0:T(8,128)(2,1)} %copy-done.10), custom_call_target="tpu_custom_call" | custom-call | tf_op jit(solution)/shard_map/gather_plain/pallas_call | solution.py:153
  300.1 14.6 %experts.3 = (bf16[2048,1024]{1,0:T(8,128)(2,1)}, bf16[2,640,1024]{2,1,0:T(8,128)(2,1)}, bf16[2,640,1024]{2,1,0:T(8,128)(2,1)}, bf16[8,160,256]{2,1,0:T(8,128)(2,1)S(1)}, f32[2,640,1]{2,1,0:T(8,128)S(1)}) custom-call(bf16[2048,1024]{1,0:T(8,128)(2,1)} %bitcast.150, bf16[32,2048]{1,0:T(8,128)(2,1)S(1)} %bitcast.118, ...), custom_call_target="tpu_custom_call" | custom-call | flops 10737418240 | bytes 20971520 | tf_op jit(solution)/shard_map/experts/pallas_call | solution.py:630
  314.7 13.6 %experts_back.2 = (bf16[2048,1024]{1,0:T(8,128)(2,1)}, bf16[2,640,1024]{2,1,0:T(8,128)(2,1)}, bf16[2,640,1024]{2,1,0:T(8,128)(2,1)}, bf16[2,640,512]{2,1,0:T(8,128)(2,1)}, f32[2,640,1]{2,1,0:T(8,128)S(1)}) custom-call(bf16[2048,1024]{1,0:T(8,128)(2,1)} %bitcast.148, bf16[8,160,256]{2,1,0:T(8,128)(2,1)S(1)} %get-tuple-element.90.s_ref, ...), custom_call_target="tpu_custom_call" | custom-call | flops 10737418240 | bytes 25165824 | tf_op jit(solution)/shard_map/experts_back/pallas_call | solution.py:685
  328.4 1.3 copy-done.7
  329.7 11.0 %expert_grads.2 = bf16[2,1024,1536]{2,1,0:T(8,128)(2,1)} custom-call(bf16[2,640,1024]{2,1,0:T(8,128)(2,1)} %get-tuple-element.119.x_ref, bf16[2,640,1024]{2,1,0:T(8,128)(2,1)} %get-tuple-element.128.d_ref, bf16[2,640,1024]{2,1,0:T(8,128)(2,1)} %get-tuple-element.129.dgu_ref, bf16[2,640,512]{2,1,0:T(8,128)(2,1)S(1)} %copy-done.7), custom_call_target="tpu_custom_call" | custom-call | flops 4026531840 | bytes 16777216 | tf_op jit(solution)/shard_map/expert_grads/pallas_call | solution.py:715
  341.7 21.0 %scatter_sum.7.mix_ref = f32[128,1024]{1,0:T(8,128)} custom-call(bf16[4,4,128,1024]{3,2,1,0:T(8,128)(2,1)} %bitcast.142), custom_call_target="tpu_custom_call" | custom-call | tf_op jit(solution)/shard_map/scatter_sum/pallas_call | solution.py:359
  362.8 29.5 %scatter_sum.8.sum_ref = f32[128,1024]{1,0:T(8,128)} custom-call(bf16[4,4,128,1024]{3,2,1,0:T(8,128)(2,1)} %bitcast.144), custom_call_target="tpu_custom_call" | custom-call | tf_op jit(solution)/shard_map/scatter_sum/pallas_call | solution.py:359
  392.3 3.9 mid_back.2
  397.0 12.8 %attend_back.2 = (f32[128,1024]{1,0:T(8,128)S(1)}, bf16[2048,1024]{1,0:T(8,128)(2,1)}) custom-call(bf16[128,1024]{1,0:T(8,128)(2,1)S(1)} %get-tuple-element.84.q_ref, bf16[128,1024]{1,0:T(8,128)(2,1)S(1)} %get-tuple-element.86.o_ref, bf16[128,1024]{1,0:T(8,128)(2,1)S(1)} %get-tuple-element.94.do_ref, bf16[2048,1024]{1,0:T(8,128)(2,1)} %bitcast.135, ...), custom_call_target="tpu_custom_call" | custom-call | flops 4294967296 | bytes 17825792 | tf_op jit(solution)/shard_map/attend_back/pallas_call | solution.py:534
  409.8 21.6 %scatter_sum.9.dkv_ref = f32[128,1024]{1,0:T(8,128)} custom-call(bf16[4,4,128,1024]{3,2,1,0:T(8,128)(2,1)} %bitcast.146), custom_call_target="tpu_custom_call" | custom-call | tf_op jit(solution)/shard_map/scatter_sum/pallas_call | solution.py:359
  431.4 4.3 end_back.2
  437.1 28.0 %gather_plain.11 = bf16[4,4,128,1024]{3,2,1,0:T(8,128)(2,1)} custom-call(bf16[128,1024]{1,0:T(8,128)(2,1)} %copy-done), custom_call_target="tpu_custom_call" | custom-call | tf_op jit(solution)/shard_map/gather_plain/pallas_call | solution.py:153
  465.1 13.6 %experts_back.3 = (bf16[2048,1024]{1,0:T(8,128)(2,1)}, bf16[2,640,1024]{2,1,0:T(8,128)(2,1)}, bf16[2,640,1024]{2,1,0:T(8,128)(2,1)}, bf16[2,640,512]{2,1,0:T(8,128)(2,1)}, f32[2,640,1]{2,1,0:T(8,128)S(1)}) custom-call(bf16[2048,1024]{1,0:T(8,128)(2,1)} %bitcast.151, bf16[8,160,256]{2,1,0:T(8,128)(2,1)S(1)} %copy-done.34, ...), custom_call_target="tpu_custom_call" | custom-call | flops 10737418240 | bytes 25165824 | tf_op jit(solution)/shard_map/experts_back/pallas_call | solution.py:685
  478.8 1.5 copy-done.6
  480.4 10.8 %expert_grads.3 = bf16[2,1024,1536]{2,1,0:T(8,128)(2,1)} custom-call(bf16[2,640,1024]{2,1,0:T(8,128)(2,1)} %get-tuple-element.114.x_ref, bf16[2,640,1024]{2,1,0:T(8,128)(2,1)} %get-tuple-element.131.d_ref, bf16[2,640,1024]{2,1,0:T(8,128)(2,1)} %get-tuple-element.132.dgu_ref, bf16[2,640,512]{2,1,0:T(8,128)(2,1)S(1)} %copy-done.6), custom_call_target="tpu_custom_call" | custom-call | flops 4026531840 | bytes 16777216 | tf_op jit(solution)/shard_map/expert_grads/pallas_call | solution.py:715
  491.3 0.9 copy-done.5
  492.2 2.0 broadcast_select_fusion.7
  494.4 20.8 %scatter_sum.10.sum_ref = f32[128,1024]{1,0:T(8,128)} custom-call(bf16[4,4,128,1024]{3,2,1,0:T(8,128)(2,1)} %bitcast.143), custom_call_target="tpu_custom_call" | custom-call | tf_op jit(solution)/shard_map/scatter_sum/pallas_call | solution.py:359
  515.2 3.9 mid_back.3
  519.9 12.9 %attend_back.3 = (f32[128,1024]{1,0:T(8,128)S(1)}, bf16[2048,1024]{1,0:T(8,128)(2,1)}) custom-call(bf16[128,1024]{1,0:T(8,128)(2,1)S(1)} %get-tuple-element.77.q_ref, bf16[128,1024]{1,0:T(8,128)(2,1)S(1)} %get-tuple-element.79.o_ref, bf16[128,1024]{1,0:T(8,128)(2,1)S(1)} %get-tuple-element.104.do_ref, bf16[2048,1024]{1,0:T(8,128)(2,1)} %bitcast.131, ...), custom_call_target="tpu_custom_call" | custom-call | flops 4294967296 | bytes 17825792 | tf_op jit(solution)/shard_map/attend_back/pallas_call | solution.py:534
  532.9 25.1 %scatter_sum.11.dkv_ref = f32[128,1024]{1,0:T(8,128)} custom-call(bf16[4,4,128,1024]{3,2,1,0:T(8,128)(2,1)} %bitcast.147), custom_call_target="tpu_custom_call" | custom-call | tf_op jit(solution)/shard_map/scatter_sum/pallas_call | solution.py:359
  558.0 4.4 end_back.3
  563.8 1.4 collective-permute-start.2
  567.0 0.9 copy.85
  568.1 0.9 copy.82
  569.3 2.3 fusion.55
  574.5 6.0 dense_grads.2
  580.6 67.3 %scatter_split.2 = f32[192,640]{1,0:T(8,128)} custom-call(bf16[2,4,4,192,640]{4,3,2,1,0:T(8,128)(2,1)} %bitcast.137), custom_call_target="tpu_custom_call" | custom-call | tf_op jit(solution)/shard_map/scatter_split/pallas_call | solution.py:359
  647.9 0.9 slice.141
  648.8 5.7 dense_grads.3
  654.5 27.4 %scatter_split.3 = f32[192,512]{1,0:T(8,128)} custom-call(bf16[2,4,4,192,512]{4,3,2,1,0:T(8,128)(2,1)} %bitcast.138), custom_call_target="tpu_custom_call" | custom-call | tf_op jit(solution)/shard_map/scatter_split/pallas_call | solution.py:359
  682.0 1.1 select_convert_fusion.other_ref
  683.0 1.1 fusion.23.own_ref
  684.1 12.0 %cross_sum.1.x_ref = bf16[192,640]{1,0:T(8,128)(2,1)S(1)} custom-call(f32[192,640]{1,0:T(8,128)S(1)} %fusion.23.own_ref, bf16[192,640]{1,0:T(8,128)(2,1)S(1)} %select_convert_fusion.other_ref), custom_call_target="tpu_custom_call" | custom-call | tf_op jit(solution)/shard_map/cross_sum/pallas_call | solution.py:849
  696.2 1.1 select_bitcast_fusion.4
  698.1 1.0 select_bitcast_fusion.1
  699.9 2.7 broadcast_select_fusion.refs_0_
  702.7 39.0 %gather_split.1 = (bf16[2,4,4,192,640]{4,3,2,1,0:T(8,128)(2,1)}, bf16[2,256,1536]{2,1,0:T(8,128)(2,1)}) custom-call(bf16[192,640]{1,0:T(8,128)(2,1)} %copy-done.12, bf16[2,256,1536]{2,1,0:T(8,128)(2,1)} %broadcast_select_fusion.refs_0_), custom_call_target="tpu_custom_call" | custom-call | tf_op jit(solution)/shard_map/gather_split/pallas_call | solution.py:153
  741.7 8.0 %results.1 = (f32[1024,1024]{1,0:T(8,128)}, f32[1024,512]{1,0:T(8,128)}, f32[1024,512]{1,0:T(8,128)}, f32[1024,1024]{1,0:T(8,128)}) custom-call(bf16[2,16,192,640]{3,2,1,0:T(8,128)(2,1)} %bitcast.139), custom_call_target="tpu_custom_call" | custom-call | bytes 20971520 | tf_op jit(solution)/shard_map/results/pallas_call | solution.py:941
  749.7 1.2 slice_select_fusion.2
  753.7 2.5 convert_add_fusion
  756.1 1.7 slice_bitcast_fusion
  (194 shorter events, 31.3 us)
Async XLA Ops:
  7.2 180.4 %all-gather.3.cloned.1.call-start = ((), (), s32[]{:S(2)}) async-start(), calls=%async_computation.2 | async-start | bytes 7864320 | tf_op jit(solution)/shard_map/all_gather | solution.py:1015
  13.5 7.5 collective-permute-start
  21.0 0.9 copy-start.48
  21.9 42.2 %copy-start.40 = (bf16[1,2,256,512]{3,2,1,0:T(8,128)(2,1)S(1)}, bf16[1,2,256,512]{3,2,1,0:T(8,128)(2,1)}, u32[]{:S(2)}) copy-start(bf16[1,2,256,512]{3,2,1,0:T(8,128)(2,1)} %param.27) | copy-start | bytes 1572868
  21.9 42.2 %copy-start.41 = (bf16[1,2,256,512]{3,2,1,0:T(8,128)(2,1)S(1)}, bf16[1,2,256,512]{3,2,1,0:T(8,128)(2,1)}, u32[]{:S(2)}) copy-start(bf16[1,2,256,512]{3,2,1,0:T(8,128)(2,1)} %param.26) | copy-start | bytes 1572868
  21.9 42.2 %copy-start.42 = (bf16[1,2,256,512]{3,2,1,0:T(8,128)(2,1)S(1)}, bf16[1,2,256,512]{3,2,1,0:T(8,128)(2,1)}, u32[]{:S(2)}) copy-start(bf16[1,2,256,512]{3,2,1,0:T(8,128)(2,1)} %param.25) | copy-start | bytes 1572868
  67.8 0.8 copy-start.53
  67.8 1.0 copy-start.54
  67.8 1.5 copy-start.49
  67.8 232.4 %all-gather.5.cloned.1.call-start = ((), (), s32[]{:S(2)}) async-start(), calls=%async_computation.3 | async-start | bytes 7864320 | tf_op jit(solution)/shard_map/all_gather | solution.py:1015
  68.5 631.4 %reduce-scatter.3.cloned.1.call-start = ((), (), s32[]{:S(2)}) async-start(), calls=%async_computation.4 | async-start | bytes 7864320 | tf_op jit(solution)/shard_map/reduce_scatter | solution.py:902
  69.3 30.2 %copy-start.50 = (bf16[2,128,1024]{2,1,0:T(8,128)(2,1)S(1)}, bf16[2,128,1024]{2,1,0:T(8,128)(2,1)}, u32[]{:S(2)}) copy-start(bf16[2,128,1024]{2,1,0:T(8,128)(2,1)} %param.14) | copy-start | bytes 1572868
  99.5 2.5 copy-start.55
  99.5 2.5 copy-start.56
  105.4 0.7 copy-start.17
  106.1 0.7 copy-start.23
  152.9 0.7 copy-start.8
  153.6 72.7 %copy-start.3 = (f32[128,1024]{1,0:T(8,128)}, f32[128,1024]{1,0:T(8,128)S(1)}, u32[]{:S(2)}) copy-start(f32[128,1024]{1,0:T(8,128)S(1)} %get-tuple-element.80.h_ref) | copy-start | bytes 1572868
  202.2 0.8 copy-start.33
  203.0 0.8 copy-start.35
  230.7 0.7 copy-start.24
  231.4 25.0 %copy-start.25 = (bf16[128,1024]{1,0:T(8,128)(2,1)}, bf16[128,1024]{1,0:T(8,128)(2,1)S(1)}, u32[]{:S(2)}) copy-start(bf16[128,1024]{1,0:T(8,128)(2,1)S(1)} %get-tuple-element.124.a_ref) | copy-start | bytes 786436
  275.0 0.8 copy-start.4
  275.8 0.7 copy-start.10
  328.4 1.3 copy-start.7
  340.7 359.2 %reduce-scatter.5.cloned.1.call-start = ((), (), s32[]{:S(2)}) async-start(), calls=%async_computation.5 | async-start | bytes 7864320 | tf_op jit(solution)/shard_map/reduce_scatter | solution.py:902
  362.7 29.6 %copy-start.2 = (bf16[128,1024]{1,0:T(8,128)(2,1)S(1)}, bf16[128,1024]{1,0:T(8,128)(2,1)}, u32[]{:S(2)}) copy-start(bf16[128,1024]{1,0:T(8,128)(2,1)} %select_bitcast_fusion.2.x_ref.dout_ref) | copy-start | bytes 786436
  362.7 29.6 %copy-start.11 = (bf16[128,1024]{1,0:T(8,128)(2,1)S(1)}, bf16[128,1024]{1,0:T(8,128)(2,1)}, u32[]{:S(2)}) copy-start(bf16[128,1024]{1,0:T(8,128)(2,1)} %copy-done.10) | copy-start | bytes 786436
  396.2 0.8 copy-start.16
  397.0 12.8 %copy-start.27 = (bf16[128,1024]{1,0:T(8,128)(2,1)}, bf16[128,1024]{1,0:T(8,128)(2,1)S(1)}, u32[]{:S(2)}) copy-start(bf16[128,1024]{1,0:T(8,128)(2,1)S(1)} %get-tuple-element.127.dattn_ref) | copy-start | bytes 786436
  435.7 0.7 copy-start
  436.5 0.7 copy-start.29
  437.1 41.7 %copy-start.31 = (bf16[128,1024]{1,0:T(8,128)(2,1)}, bf16[128,1024]{1,0:T(8,128)(2,1)S(1)}, u32[]{:S(2)}) copy-start(bf16[128,1024]{1,0:T(8,128)(2,1)S(1)} %get-tuple-element.126.dkv_ref) | copy-start | bytes 786436
  437.1 28.0 %copy-start.34 = (bf16[8,160,256]{2,1,0:T(8,128)(2,1)S(1)}, bf16[8,160,256]{2,1,0:T(8,128)(2,1)}, u32[]{:S(2)}) copy-start(bf16[8,160,256]{2,1,0:T(8,128)(2,1)} %copy-done.33) | copy-start | bytes 1966084
  437.1 28.0 %copy-start.36 = (f32[2,640,1]{2,1,0:T(8,128)S(1)}, f32[2,640,1]{2,1,0:T(8,128)}, u32[]{:S(2)}) copy-start(f32[2,640,1]{2,1,0:T(8,128)} %copy-done.35) | copy-start | bytes 15364
  478.8 12.4 %copy-start.13 = (f32[2,640,1]{2,1,0:T(8,128)}, f32[2,640,1]{2,1,0:T(8,128)S(1)}, u32[]{:S(2)}) copy-start(f32[2,640,1]{2,1,0:T(8,128)S(1)} %get-tuple-element.115) | copy-start | bytes 15364
  478.8 1.6 copy-start.6
  491.2 1.0 copy-start.5
  494.2 21.0 %copy-start.1 = (bf16[128,1024]{1,0:T(8,128)(2,1)S(1)}, bf16[128,1024]{1,0:T(8,128)(2,1)}, u32[]{:S(2)}) copy-start(bf16[128,1024]{1,0:T(8,128)(2,1)} %copy-done) | copy-start | bytes 786436
  494.2 21.0 %copy-start.9 = (bf16[128,1024]{1,0:T(8,128)(2,1)S(1)}, bf16[128,1024]{1,0:T(8,128)(2,1)}, u32[]{:S(2)}) copy-start(bf16[128,1024]{1,0:T(8,128)(2,1)} %copy-done.8) | copy-start | bytes 786436
  494.2 202.0 %collective-permute-start.1 = (bf16[128,1024]{1,0:T(8,128)(2,1)}, bf16[128,1024]{1,0:T(8,128)(2,1)}, u32[]{:S(2)}, u32[]{:S(2)}) collective-permute-start(bf16[128,1024]{1,0:T(8,128)(2,1)} %get-tuple-element.144), channel_id=1, source_target_pairs={{0,64},{64,0},{1,65},{65,1},{2,66},{66,2},{3,67},{67,3},{4,68},{68... | collective-permute-start | bytes 786440 | tf_op jit(solution)/shard_map/ppermute | solution.py:953
  519.2 0.8 copy-start.15
  519.9 12.9 %copy-start.19 = (bf16[128,1024]{1,0:T(8,128)(2,1)}, bf16[128,1024]{1,0:T(8,128)(2,1)S(1)}, u32[]{:S(2)}) copy-start(bf16[128,1024]{1,0:T(8,128)(2,1)S(1)} %get-tuple-element.113.dattn_ref) | copy-start | bytes 786436
  562.4 0.7 copy-start.21
  563.1 6.0 copy-start.14
  563.8 134.3 %collective-permute-start.2 = (bf16[128,1024]{1,0:T(8,128)(2,1)}, bf16[128,1024]{1,0:T(8,128)(2,1)}, u32[]{:S(2)}, u32[]{:S(2)}) collective-permute-start(bf16[128,1024]{1,0:T(8,128)(2,1)} %broadcast_select_fusion.5), channel_id=1, source_target_pairs={{0,64},{64,0},{1,65},{65,1},{2,66},{66,2},{3,67},{67,3},{4,68},{68... | collective-permute-start | bytes 786440 | tf_op jit(solution)/shard_map/ppermute | solution.py:953
  569.0 3.2 copy-start.37
  569.3 4.1 copy-start.51
  571.7 1.9 copy-start.52
  572.3 1.3 copy-start.43
  572.3 1.3 copy-start.44
  572.3 1.3 copy-start.45
  572.3 1.3 copy-start.46
  573.4 1.1 copy-start.18
  573.4 1.1 copy-start.20
  573.4 1.1 copy-start.22
  580.5 68.2 %copy-start.26 = (bf16[128,1024]{1,0:T(8,128)(2,1)S(1)}, bf16[128,1024]{1,0:T(8,128)(2,1)}, u32[]{:S(2)}) copy-start(bf16[128,1024]{1,0:T(8,128)(2,1)} %copy-done.25) | copy-start | bytes 786436
  580.5 68.2 %copy-start.28 = (bf16[128,1024]{1,0:T(8,128)(2,1)S(1)}, bf16[128,1024]{1,0:T(8,128)(2,1)}, u32[]{:S(2)}) copy-start(bf16[128,1024]{1,0:T(8,128)(2,1)} %copy-done.27) | copy-start | bytes 786436
  580.5 68.3 %copy-start.30 = (bf16[128,1024]{1,0:T(8,128)(2,1)S(1)}, bf16[128,1024]{1,0:T(8,128)(2,1)}, u32[]{:S(2)}) copy-start(bf16[128,1024]{1,0:T(8,128)(2,1)} %copy-done.29) | copy-start | bytes 786436
  580.5 68.3 %copy-start.32 = (bf16[128,1024]{1,0:T(8,128)(2,1)S(1)}, bf16[128,1024]{1,0:T(8,128)(2,1)}, u32[]{:S(2)}) copy-start(bf16[128,1024]{1,0:T(8,128)(2,1)} %copy-done.31) | copy-start | bytes 786436
  654.5 27.4 %copy-start.39 = (f32[192,640]{1,0:T(8,128)S(1)}, f32[192,640]{1,0:T(8,128)}, u32[]{:S(2)}) copy-start(f32[192,640]{1,0:T(8,128)} %scatter_split.2) | copy-start | bytes 1474564
  681.9 14.2 %copy-start.47 = (bf16[128,1024]{1,0:T(8,128)(2,1)S(1)}, bf16[128,1024]{1,0:T(8,128)(2,1)}, u32[]{:S(2)}) copy-start(bf16[128,1024]{1,0:T(8,128)(2,1)} %get-tuple-element.145) | copy-start | bytes 786436
  696.1 6.5 copy-start.12
  749.7 4.0 copy-start.38
Sparse Core Ops, SparseCore 0:
  67.9 52.5 all-gather.2
  122.7 49.8 all-gather.4
  340.8 84.2 reduce-scatter.2
  491.3 97.3 reduce-scatter.4

commit v3 on v2

--- a/solution.py
+++ b/solution.py
@@ -27,10 +27,11 @@
 
 
 def gather_kernel(kind, x_ref, *refs):
-    split = kind != "plain"
+    split = kind in ("split", "weights")
+    sided = kind in ("swap", "weights")
     if kind == "weights":
         side_ref, wq_ref, wk_ref, wv_ref, wo_ref, out_all, side_out = refs[:7]
-    elif split:
+    elif sided:
         side_ref, out_all, side_out = refs[:3]
     else:
         out_all = refs[0]
@@ -67,7 +68,9 @@
     barrier = pltpu.get_barrier_semaphore()
     greeted = [{"expert": d} for d in (dxr, dxl, dzr, dzl)]
     if split:
-        greeted += [other_core, other_section]
+        greeted.append(other_core)
+    if sided:
+        greeted.append(other_section)
     for to in greeted:
         pl.semaphore_signal(barrier, inc=1, device_id=to, device_id_type=MESH)
     pl.semaphore_wait(barrier, len(greeted))
@@ -87,63 +90,106 @@
     def forward(*piece):
         if split:
             there = out_ref.at[piece]
-            forwards.append(send_to(17 + len(forwards), there, there, other_core))
+            forwards.append(send_to(45 + len(forwards), there, there, other_core))
 
     A, B = pl.ds(0, half), pl.ds(half, half)
     A0, A1 = pl.ds(0, quarter), pl.ds(quarter, quarter)
     B0, B1 = pl.ds(half, quarter), pl.ds(half + quarter, quarter)
     every = slice(None)
-    a_r = copy(0, x_ref.at[A], out_ref.at[z, x, A], dxr)
-    a_l = copy(1, x_ref.at[A], out_ref.at[z, x, A], dxl)
-    b_r = copy(2, x_ref.at[B], out_ref.at[z, x, B], dzr)
-    b_l = copy(3, x_ref.at[B], out_ref.at[z, x, B], dzl)
-    if split:
-        swap = send_to(16, side_ref, side_out, other_section)
+    began = []
+
+    def pair(piece, to_r, to_l, src=None):
+        out = []
+        for to in (to_r, to_l):
+            there = out_ref.at[piece]
+            out.append(copy(len(began), there if src is None else src, there, to))
+            began.append(out[-1])
+        return out
+
+    def single(piece, to):
+        there = out_ref.at[piece]
+        began.append(copy(len(began), there, there, to))
+        return began[-1]
+
+    a_r, a_l = pair((z, x, A), dxr, dxl, x_ref.at[A])
+    b_r, b_l = pair((z, x, B), dzr, dzl, x_ref.at[B])
+    c_r, c_l = pair((z, x, A), dzr, dzl, x_ref.at[A])
+    d_r, d_l = pair((z, x, B), dxr, dxl, x_ref.at[B])
+    if sided:
+        swap = send_to(44, side_ref, side_out, other_section)
     a_r.wait_recv()
-    a2_r = copy(4, out_ref.at[z, xl, A0], out_ref.at[z, xl, A0], dxr)
+    a2_r = single((z, xl, A0), dxr)
+    c1_r, c1_l = pair((z, xl, A), dzr, dzl)
     a_l.wait_recv()
-    a2_l = copy(5, out_ref.at[z, xr, A1], out_ref.at[z, xr, A1], dxl)
+    a2_l = single((z, xr, A1), dxl)
+    c2_r, c2_l = pair((z, xr, A), dzr, dzl)
     b_r.wait_recv()
-    b2_r = copy(6, out_ref.at[zl, x, B0], out_ref.at[zl, x, B0], dzr)
+    b2_r = single((zl, x, B0), dzr)
+    d1_r, d1_l = pair((zl, x, B), dxr, dxl)
     b_l.wait_recv()
-    b2_l = copy(7, out_ref.at[zr, x, B1], out_ref.at[zr, x, B1], dzl)
+    b2_l = single((zr, x, B1), dzl)
+    d2_r, d2_l = pair((zr, x, B), dxr, dxl)
+    last = []
+    c_r.wait_recv()
+    last.append(single((zl, x, A0), dzr))
+    c_l.wait_recv()
+    last.append(single((zr, x, A1), dzl))
+    d_r.wait_recv()
+    last.append(single((z, xl, B0), dxr))
+    d_l.wait_recv()
+    last.append(single((z, xr, B1), dxl))
+    a2_r.wait_recv()
+    c3_r, c3_l = pair((z, x2, A0), dzr, dzl)
+    a2_l.wait_recv()
+    c4_r, c4_l = pair((z, x2, A1), dzr, dzl)
+    b2_r.wait_recv()
+    d3_r, d3_l = pair((z2, x, B0), dxr, dxl)
+    b2_l.wait_recv()
+    d4_r, d4_l = pair((z2, x, B1), dxr, dxl)
+    c1_r.wait_recv()
+    last.append(single((zl, xl, A0), dzr))
+    c1_l.wait_recv()
+    last.append(single((zr, xl, A1), dzl))
+    d1_r.wait_recv()
+    last.append(single((zl, xl, B0), dxr))
+    d1_l.wait_recv()
+    last.append(single((zl, xr, B1), dxl))
     own.wait()
-    a2_r.wait_recv()
-    a2_l.wait_recv()
-    c_r = copy(8, out_ref.at[z, :, A], out_ref.at[z, :, A], dzr)
-    c_l = copy(9, out_ref.at[z, :, A], out_ref.at[z, :, A], dzl)
-    b2_r.wait_recv()
-    b2_l.wait_recv()
-    d_r = copy(10, out_ref.at[:, x, B], out_ref.at[:, x, B], dxr)
-    d_l = copy(11, out_ref.at[:, x, B], out_ref.at[:, x, B], dxl)
     forward(z, every, A)
     forward(every, x, B)
-    c_r.wait_recv()
-    c2_r = copy(12, out_ref.at[zl, :, A0], out_ref.at[zl, :, A0], dzr)
-    c_l.wait_recv()
-    c2_l = copy(13, out_ref.at[zr, :, A1], out_ref.at[zr, :, A1], dzl)
-    d_r.wait_recv()
-    d2_r = copy(14, out_ref.at[:, xl, B0], out_ref.at[:, xl, B0], dxr)
-    d_l.wait_recv()
-    d2_l = copy(15, out_ref.at[:, xr, B1], out_ref.at[:, xr, B1], dxl)
+    c2_r.wait_recv()
+    last.append(single((zl, xr, A0), dzr))
+    c2_l.wait_recv()
+    last.append(single((zr, xr, A1), dzl))
+    d2_r.wait_recv()
+    last.append(single((zr, xl, B0), dxr))
+    d2_l.wait_recv()
+    last.append(single((zr, xr, B1), dxl))
+    c3_r.wait_recv()
+    last.append(single((zl, x2, A0), dzr))
+    c4_l.wait_recv()
+    last.append(single((zr, x2, A1), dzl))
+    d3_r.wait_recv()
+    last.append(single((z2, xl, B0), dxr))
+    d4_l.wait_recv()
+    last.append(single((z2, xr, B1), dxl))
+    c3_l.wait_recv()
+    c4_r.wait_recv()
     forward(zl, every, A)
     forward(zr, every, A)
+    d3_l.wait_recv()
+    d4_r.wait_recv()
     forward(every, xl, B)
     forward(every, xr, B)
-    c2_r.wait_recv()
-    forward(z2, every, A0)
-    c2_l.wait_recv()
-    forward(z2, every, A1)
-    d2_r.wait_recv()
-    forward(every, x2, B0)
-    d2_l.wait_recv()
-    forward(every, x2, B1)
-    for c in (a_r, a_l, b_r, b_l, a2_r, a2_l, b2_r, b2_l, c_r, c_l, d_r, d_l, c2_r, c2_l, d2_r, d2_l):
+    for c in last:
+        c.wait_recv()
+    forward(z2, every, A)
+    forward(every, x2, B)
+    for c in began:
         c.wait_send()
-    if split:
-        for c in forwards + [swap]:
-            c.wait_recv()
-            c.wait_send()
+    for c in forwards + ([swap] if sided else []):
+        c.wait_recv()
+        c.wait_send()
     for c in locals_:
         c.wait()
 
@@ -156,8 +202,8 @@
         in_specs=[memory if held else anywhere for held in in_memory],
         out_specs=[anywhere] * len(outs),
         scratch_shapes=[
-            pltpu.SemaphoreType.DMA((27,)),
-            pltpu.SemaphoreType.DMA((27,)),
+            pltpu.SemaphoreType.DMA((53,)),
+            pltpu.SemaphoreType.DMA((53,)),
             pltpu.SemaphoreType.DMA((7,)),
         ],
         compiler_params=pltpu.CompilerParams(
@@ -172,13 +218,19 @@
     return out.reshape(16 * rows, cols)
 
 
-def gather_split(x, side, ident):
+def gather_swap(x, side, ident):
     rows, cols = x.shape
     out, side_out = gather_call(
-        ident, "split",
-        [jax.ShapeDtypeStruct((2, 4, 4, rows, cols), x.dtype), jax.ShapeDtypeStruct(side.shape, side.dtype)],
+        ident, "swap",
+        [jax.ShapeDtypeStruct((4, 4, rows, cols), x.dtype), jax.ShapeDtypeStruct(side.shape, side.dtype)],
         (True, False), x, side)
-    return out.reshape(2, 16, rows, cols), side_out
+    return out.reshape(16 * rows, cols), side_out
+
+
+def gather_split(x, ident):
+    rows, cols = x.shape
+    out = gather_call(ident, "split", [jax.ShapeDtypeStruct((2, 4, 4, rows, cols), x.dtype)], (True,), x)[0]
+    return out.reshape(2, 16, rows, cols)
 
 
 def gather_weights(x, side, wq, wk, wv, wo, ident):
@@ -191,10 +243,14 @@
     return out.reshape(2, 2, 16, rows, cols), side_out
 
 
-def scatter_kernel(split, x_ref, out_ref, loc, *refs):
+def scatter_kernel(split, x_ref, *refs):
     if split:
-        land, core_send, core_recv = refs[0], refs[-2], refs[-1]
-        refs = refs[1:-2]
+        side_ref, out_ref, side_out, loc, land = refs[:5]
+        core_send, core_recv = refs[-2:]
+        refs = refs[5:-2]
+    else:
+        out_ref, loc = refs[:2]
+        refs = refs[2:]
     s1, l1, l2, t0, m1, n1, m2, send, recv, loc_sem = refs
     z, x, xr, xl, zr, zl, (dxr, dxl, dzr, dzl) = ring_places()
     x2, z2 = lax.rem(x + 2, 4), lax.rem(z + 2, 4)
@@ -218,9 +274,9 @@
         c = pltpu.make_async_copy(part.at[piece], loc.at[i], loc_sem.at[i])
         c.start()
         held.append(c)
-    other_core = {"dp": dp + 1 - 2 * core}
+    other_core, other_section = {"dp": dp + 1 - 2 * core}, {"section": 1 - lax.axis_index("section")}
     barrier = pltpu.get_barrier_semaphore()
-    greeted = [{"expert": d} for d in (dxr, dxl, dzr, dzl)] + ([other_core] if split else [])
+    greeted = [{"expert": d} for d in (dxr, dxl, dzr, dzl)] + ([other_core, other_section] if split else [])
     for to in greeted:
         pl.semaphore_signal(barrier, inc=1, device_id=to, device_id_type=MESH)
     pl.semaphore_wait(barrier, len(greeted))
@@ -232,6 +288,10 @@
                 recv_sem=core_recv.at[i], device_id=other_core, device_id_type=MESH)
             c.start()
             away.append(c)
+        swap = pltpu.make_async_remote_copy(
+            src_ref=side_ref, dst_ref=side_out, send_sem=core_send.at[16], recv_sem=core_recv.at[16],
+            device_id=other_section, device_id_type=MESH)
+        swap.start()
 
     def copy(i, src, dst, to):
         c = pltpu.make_async_remote_copy(
@@ -332,9 +392,15 @@
         c.wait_send()
     for c in away:
         c.wait_send()
-
-
-def scatter_sum(x, ident, split=False):
+    if split:
+        swap.wait_recv()
+        swap.wait_send()
+
+
+def scatter_sum(x, ident, side=None):
+    split = side is not None
+    anywhere = pl.BlockSpec(memory_space=pl.ANY)
+    summed, held = jax.ShapeDtypeStruct((x.shape[-2] // 16, x.shape[-1]), f32), whole()
     rows, cols = x.shape[-2] // 16, x.shape[-1]
     q = rows // 4
     piece = (4, q, cols)
@@ -355,17 +421,17 @@
         pltpu.SemaphoreType.DMA((count,)),
     ]
     if split:
-        scratch += [pltpu.SemaphoreType.DMA((16,)), pltpu.SemaphoreType.DMA((16,))]
+        scratch += [pltpu.SemaphoreType.DMA((17,)), pltpu.SemaphoreType.DMA((17,))]
     return pl.pallas_call(
         functools.partial(scatter_kernel, split),
-        out_shape=jax.ShapeDtypeStruct((rows, cols), f32),
-        in_specs=[pl.BlockSpec(memory_space=pl.ANY)],
-        out_specs=pl.BlockSpec(memory_space=pltpu.VMEM),
+        out_shape=[summed, jax.ShapeDtypeStruct(side.shape, side.dtype)] if split else summed,
+        in_specs=[anywhere] * (2 if split else 1),
+        out_specs=[held, anywhere] if split else held,
         scratch_shapes=scratch,
         compiler_params=pltpu.CompilerParams(
             collective_id=ident, has_side_effects=True, vmem_limit_bytes=56 << 20),
         name="scatter_split" if split else "scatter_sum",
-    )(x.reshape(x.shape[:-2] + (4, 4, rows, cols)))
+    )(x.reshape(x.shape[:-2] + (4, 4, rows, cols)), *([side] if split else []))
 
 
 def spec(shape, index):
@@ -569,7 +635,7 @@
 ROWS = 1024
 
 
-def experts_kernel(b_ref, mask_ref, wr_ref, pick_ref, w_ref, y_ref, x_ref, gu_ref, s_ref, gate_ref):
+def experts_kernel(b_ref, mask_ref, wr_ref, pick_ref, w0_ref, w1_ref, y_ref, x_ref, gu_ref, s_ref, gate_ref):
     row, col = lax.broadcasted_iota(jnp.int32, (256, 256), 0), lanes((256, 256))
     before = ((row < col) & ((row < 128) == (col < 128))).astype(bf16)
     slot_ids = lax.broadcasted_iota(jnp.int32, (SLOTS, 256), 0)
@@ -598,12 +664,12 @@
     ys = []
     for j in range(2):
         x = x_ref[j]
-        g = dot(x, w_ref[j, :, 0:512])
-        u = dot(x, w_ref[j, :, 512:1024])
+        g = dot(x, (w0_ref, w1_ref)[j][0, :, 0:512])
+        u = dot(x, (w0_ref, w1_ref)[j][0, :, 512:1024])
         gu_ref[j, :, 0:512] = g.astype(bf16)
         gu_ref[j, :, 512:1024] = u.astype(bf16)
         inner = g * jax.nn.sigmoid(g) * u
-        ys.append(dot_t((inner * gate_ref[j]).astype(bf16), w_ref[j, :, 1024:1536]).astype(bf16))
+        ys.append(dot_t((inner * gate_ref[j]).astype(bf16), (w0_ref, w1_ref)[j][0, :, 1024:1536]).astype(bf16))
     for p in range(ROWS // 256):
         part = slice(SLOTS * p, SLOTS * p + SLOTS)
         both = jnp.concatenate([ys[0][part], ys[1][part]], axis=0)
@@ -640,16 +706,17 @@
             spec((32, ROWS), lambda i: (0, i)),
             fixed((1024, 32)),
             fixed((32, 8)),
-            fixed((2, 1024, 1536)),
+            fixed((1, 1024, 1536)),
+            fixed((1, 1024, 1536)),
         ],
         out_specs=[tokens(1024), compact(1024), compact(1024), choice, compact(1)],
         flops=8 * 2 * 1280 * 1024 * 512,
         moved=20 << 20,
-    )(b_all, mask_all, wr, pick, w)
+    )(b_all, mask_all, wr, pick, *w)
 
 
 def experts_back_kernel(
-    dout_ref, s_ref, gu_ref, gate_ref, wcol_ref, w_ref, db_ref, d_ref, dgu_ref, in_ref, coef_ref
+    dout_ref, s_ref, gu_ref, gate_ref, wcol_ref, w0_ref, w1_ref, db_ref, d_ref, dgu_ref, in_ref, coef_ref
 ):
     for p in range(ROWS // 256):
         rows = dot(s_ref[p], dout_ref[256 * p : 256 * p + 256, :]).astype(bf16)
@@ -660,7 +727,7 @@
         gate = gate_ref[j]
         g = gu_ref[j, :, 0:512].astype(f32)
         u = gu_ref[j, :, 512:1024].astype(f32)
-        back = dot(d_ref[j], w_ref[j, :, 1024:1536])
+        back = dot(d_ref[j], (w0_ref, w1_ref)[j][0, :, 1024:1536])
         sig = jax.nn.sigmoid(g)
         silu = g * sig
         inner = silu * u
@@ -672,7 +739,7 @@
         du = (dinner * silu).astype(bf16)
         dgu_ref[j, :, 0:512] = dg
         dgu_ref[j, :, 512:1024] = du
-        db = dot_t(dg, w_ref[j, :, 0:512]) + dot_t(du, w_ref[j, :, 512:1024])
+        db = dot_t(dg, (w0_ref, w1_ref)[j][0, :, 0:512]) + dot_t(du, (w0_ref, w1_ref)[j][0, :, 512:1024])
         dbs.append((db + coef * wcol_ref[j : j + 1, :]).astype(bf16))
     for p in range(ROWS // 256):
         part = slice(SLOTS * p, SLOTS * p + SLOTS)
@@ -691,12 +758,13 @@
         "experts_back",
         grid=(rows // ROWS,),
         in_specs=[
-            tokens(1024), choice, compact(1024), compact(1), fixed((8, 1024)), fixed((2, 1024, 1536)),
+            tokens(1024), choice, compact(1024), compact(1), fixed((8, 1024)), fixed((1, 1024, 1536)),
+            fixed((1, 1024, 1536)),
         ],
         out_specs=[tokens(1024), compact(1024), compact(1024), compact(512), compact(1)],
         flops=8 * 2 * 1280 * 1024 * 512,
         moved=24 << 20,
-    )(dout_all, choices, gu, gate, wcol, w)
+    )(dout_all, choices, gu, gate, wcol, *w)
 
 
 def expert_grads_kernel(x_ref, d_ref, dgu_ref, in_ref, out_ref):
@@ -779,40 +847,41 @@
     dx_ref[...] = dx.astype(bf16)
 
 
-def dense_grads_kernel(a_ref, o_ref, dq_ref, dkv_ref, dattn_ref, *rest):
-    small_ref, out_ref = rest if len(rest) == 2 else (None, rest[0])
-    a = a_ref[...]
-    gq = t_dot(a, dq_ref[...]).astype(bf16)
-    gkv = t_dot(a, dkv_ref[...]).astype(bf16)
-    go = t_dot(o_ref[...], dattn_ref[...]).astype(bf16)
+def dense_grads_kernel(*refs):
+    small_ref, out_ref = refs[10:]
+    for layer in range(2):
+        a_ref, o_ref, dq_ref, dkv_ref, dattn_ref = refs[5 * layer : 5 * layer + 5]
+        a = a_ref[...]
+        gq = t_dot(a, dq_ref[...]).astype(bf16)
+        gkv = t_dot(a, dkv_ref[...]).astype(bf16)
+        go = t_dot(o_ref[...], dattn_ref[...]).astype(bf16)
+        cols = slice(512 * layer, 512 * layer + 512)
+        for t in range(2):
+            part = slice(64 * t, 64 * t + 64)
+            for h in range(2):
+                side = slice(512 * h, 512 * h + 512)
+                out_ref[h, t, 0:64, cols] = gq[part, side]
+                out_ref[h, t, 64:128, cols] = gkv[part, side]
+                out_ref[h, t, 128:192, cols] = go[part, side]
     for t in range(2):
-        part = slice(64 * t, 64 * t + 64)
         for h in range(2):
-            side = slice(512 * h, 512 * h + 512)
-            out_ref[h, t, 0:64, 0:512] = gq[part, side]
-            out_ref[h, t, 64:128, 0:512] = gkv[part, side]
-            out_ref[h, t, 128:192, 0:512] = go[part, side]
-            if small_ref is not None:
-                out_ref[h, t, 0:64, 512:640] = small_ref[h, part, :]
-                out_ref[h, t, 64:192, 512:640] = jnp.zeros((128, 128), bf16)
-
-
-def dense_grads(a, o, dq, dkv, dattn, small=None):
-    cols = 512 if small is None else 640
+            out_ref[h, t, 0:64, 1024:1152] = small_ref[h, 64 * t : 64 * t + 64, :]
+            out_ref[h, t, 64:192, 1024:1152] = jnp.zeros((128, 128), bf16)
+
+
+def dense_grads(layer0, layer1, small):
     narrow = spec((128, 128), lambda i: (0, i))
-    args = (a, o, dq, dkv, dattn) + (() if small is None else (small,))
     out = local_call(
         dense_grads_kernel,
-        [((2, 16, 192, cols), bf16)],
+        [((2, 16, 192, 1152), bf16)],
         "dense_grads",
         grid=(8,),
-        in_specs=[narrow, narrow] + [fixed((128, 1024))] * 3
-        + ([] if small is None else [spec((2, 128, 128), lambda i: (0, i, 0))]),
-        out_specs=[spec((2, 2, 192, cols), lambda i: (0, i, 0, 0))],
-        flops=3 * 2 * 128 * 1024 * 1024,
-        moved=8 << 20,
-    )(*args)[0]
-    return out.reshape(2, 3072, cols)
+        in_specs=([narrow, narrow] + [fixed((128, 1024))] * 3) * 2 + [spec((2, 128, 128), lambda i: (0, i, 0))],
+        out_specs=[spec((2, 2, 192, 1152), lambda i: (0, i, 0, 0))],
+        flops=6 * 2 * 128 * 1024 * 1024,
+        moved=18 << 20,
+    )(*layer0, *layer1, small)[0]
+    return out.reshape(2, 3072, 1152)
 
 
 def cross_kernel(own_ref, other_ref, out_ref, land, mine, send, recv):
@@ -878,7 +947,10 @@
         pre_kernel, [((128, 1024), bf16)] * 3, "pre", in_specs={4: qkv_block(layer)},
         flops=2 * 128 * 1024 * 2048, moved=6 << 20,
     )(x, gain_attn, cosine, sine, weights)
-    kv_all = gather_rows(kv, 1)
+    if callable(w):
+        kv_all, w = w(kv)
+    else:
+        kv_all = gather_rows(kv, 1)
     o, probs = attend(q, kv_all, lo, hi)
     h, b = local_call(
         post_kernel, [((128, 1024), f32), ((128, 1024), bf16)], "post", in_specs={2: out_block(layer)},
@@ -888,14 +960,15 @@
     y, rows, gu, choices, gate = experts(b_all, masks[1], wr, pick, w)
     mix = scatter_sum(y, 2)
     out = (h + mix).astype(bf16)
-    return out, (x, a, q, kv_all, o, probs, h, b, rows, gu, choices, gate, mix)
-
-
-def backward(dout, saved, layer, place, weights, dense, w, masks):
+    return out, w, (x, a, q, kv_all, o, probs, h, b, rows, gu, choices, gate, mix)
+
+
+def backward(dout, dout_all, saved, layer, place, weights, dense, w, masks):
     cosine, sine, lo, hi, pick, pick_rows = place
     gain_attn, gain_moe, wr = dense
     x, a, q, kv_all, o, probs, h, b, rows, gu, choices, gate, mix = saved
-    dout_all = gather_rows(dout, 1)
+    if dout_all is None:
+        dout_all = gather_rows(dout, 1)
     wcol = dot_t(pick_rows.astype(bf16), wr)
     db_part, drows, dgu, inner, coef = experts_back(dout_all, choices, gu, gate, wcol, w)
     db_sum = scatter_sum(db_part, 2)
@@ -994,7 +1067,7 @@
     own_rows = jnp.concatenate([mask_own, jnp.zeros((64, 32), bf16)], axis=0)
     payload = jnp.concatenate([payload[:, :576], own_rows, payload[:, 608:]], axis=1)
     shards = jnp.concatenate([w_gate[0], w_up[0], w_down[0]], axis=2)
-    weights, away = gather_weights(payload, shards, w_query[0], w_key[0], w_value[0], w_out[0], 3)
+    weights, away0 = gather_weights(payload, shards[0:1], w_query[0], w_key[0], w_value[0], w_out[0], 3)
     got = jnp.where(
         first,
         jnp.where(left, weights[1, 0, :, :, 512:], weights[1, 1, :, :, 512:]),
@@ -1012,7 +1085,21 @@
     masks_own = by_layer(mask_own, mask_other)
     masks_all = by_layer(all_own, all_other)
     masks = [(masks_own[l], masks_all[l]) for l in range(2)]
-    expert_w = [lax.all_gather(w, "dp", axis=1, tiled=True) for w in by_layer(shards, away)]
+
+    def over_dp(w):
+        return lax.all_gather(w, "dp", axis=1, tiled=True)
+
+    def first_kv(kv):
+        kv, expert_w[0][0], expert_w[1][0] = lax.optimization_barrier((kv, expert_w[0][0], expert_w[1][0]))
+        expert_w[0][0] = over_dp(expert_w[0][0])
+        expert_w[1][0] = over_dp(expert_w[1][0])
+        kv_all, away1 = gather_swap(kv, shards[1:2], 8)
+        second = by_layer(shards[1:2], away1)
+        for l in range(2):
+            expert_w[l].append(over_dp(second[l]))
+        return kv_all, expert_w[0]
+
+    expert_w = [[w] for w in by_layer(shards[0:1], away0)]
 
     seq = mine(offsets)
     local = expert * 128 + jnp.arange(128, dtype=jnp.int32)
@@ -1027,14 +1114,16 @@
     place = (cosine, sine, seq[:, None], local[:, None], pick_rows.T, pick_rows)
 
     x0 = mine(inputs)
-    out0, saved0 = forward(x0, 0, place, weights, dense[0], expert_w[0], masks[0])
-    out1, saved1 = forward(out0, 1, place, weights, dense[1], expert_w[1], masks[1])
+    out0, _, saved0 = forward(x0, 0, place, weights, dense[0], first_kv, masks[0])
+    out1, _, saved1 = forward(out0, 1, place, weights, dense[1], expert_w[1], masks[1])
     cot = mine(cotangent)
-    dx1, eg1, dg1, small1 = backward(cot, saved1, 1, place, weights, dense[1], expert_w[1], masks[1])
-    dense1 = scatter_sum(dense_grads(*dg1), 4, split=True)
-    dx0, eg0, dg0, small0 = backward(dx1, saved0, 0, place, weights, dense[0], expert_w[0], masks[0])
+    later, _ = lax.optimization_barrier((cot, saved0[4]))
+    cot_all = gather_rows(later, 1)
+    dx1, eg1, dg1, small1 = backward(cot, cot_all, saved1, 1, place, weights, dense[1], expert_w[1], masks[1])
+    dx0, eg0, dg0, small0 = backward(dx1, None, saved0, 0, place, weights, dense[0], expert_w[0], masks[0])
+    eg_sent = jnp.where(first, eg1, eg0)
     both_small = jnp.pad(jnp.stack([small0, small1]), ((0, 0), (0, 0), (0, 64)))
-    dense0 = scatter_sum(dense_grads(*dg0, both_small), 5, split=True)
+    dense_sum, eg_away = scatter_sum(dense_grads(dg0, dg1, both_small), 4, eg_sent)
 
     def in_place(l0, l1):
         got = swapped(jnp.where(first, l1, l0))
@@ -1044,11 +1133,12 @@
     acts = in_place(out0, out1)
     in_grads = in_place(dx0, dx1)
 
-    full1 = jnp.concatenate([dense1, dense0[:, 512:]], axis=1)
-    own = jnp.where(first, dense0, full1)
-    other = jnp.where(first, full1, dense0).astype(bf16)
-    eg_sent = jnp.where(first, eg1, eg0)
-    summed, eg_away = gather_split(cross_sum(own, other, 6), eg_sent, 7)
+    tail = dense_sum[:, 1024:]
+    full0 = jnp.concatenate([dense_sum[:, :512], tail], axis=1)
+    full1 = dense_sum[:, 512:]
+    own = jnp.where(first, full0, full1)
+    other = jnp.where(first, full1, full0).astype(bf16)
+    summed = gather_split(cross_sum(own, other, 6), 7)
     grad_query, grad_key, grad_value, grad_out = results(summed)
     grad_small = mine(summed[:, :, 0:64, 512:576]).reshape(1024, 64).astype(f32)
     eg = jnp.where(first, eg0, eg1).astype(f32) + eg_away.astype(f32)

time: 772 us -> 729 us (0.944)
  Pallas kernels: 676 us -> 630 us
    pallas_call x8, Pallas kernels: 245 us -> 215 us  [gather_call(): pl.pallas_call(functools.partial(gather_kernel, kind), out_shape=outs, in...]
    pallas_call x10 -> x8, Pallas kernels: 247 us -> 227 us  [the longest x7 218 us: scatter_sum(): pl.pallas_call(functools.partial(scatter_kernel, split), out_shape=[summe...]
    unnamed x118 -> x110, local copies, waits for them, and re-layouts: 16.2 us -> 18.9 us
  transfers between devices with their start and end apart: 7 -> 9, of which waited for: 1 -> 2; matrix products, arithmetic and copies ran while one was open for 4% -> 4% of each run, Pallas kernels for 72% -> 57%
where the time goes in v3:
time: 729 us; the launch traced here: 723 us
  Pallas kernels  630 us (86%)
  other arithmetic  33.6 us (5%)
  local copies, waits for them, and re-layouts  33 us (5%)
  between operations  15.3 us (2%)
    pallas_call x7, Pallas kernels, scatter_sum(): pl.pallas_call(functools.partial(scatter_kernel, split), out_shape=[summe...  218 us
    pallas_call x8, Pallas kernels, gather_call(): pl.pallas_call(functools.partial(gather_kernel, kind), out_shape=outs, in...  215 us
    pallas_call x2, Pallas kernels, attend(): local_call(attend_kernel, [((128, 1024), bf16), ((4, 512, 2048), bf16)],...  31.5 us
    pallas_call x2, Pallas kernels, experts(): local_call(experts_kernel, [((rows, 1024), bf16), ((2, FULL, 1024), bf16)...  29.5 us
    pallas_call x8, Pallas kernels, call(): return pl.pallas_call(kernel, grid=(1,), in_specs=ins, **kinds)(*args)  28.1 us
    pallas_call x2, Pallas kernels, experts_back(): local_call(experts_back_kernel, [((rows, 1024), bf16), ((2, FULL, 1024),...  27.8 us
    pallas_call x2, Pallas kernels, attend_back(): local_call(attend_back_kernel, [((128, 1024), f32), ((2048, 1024), bf16)]...  25.8 us
    pallas_call x2, Pallas kernels, expert_grads(): local_call(expert_grads_kernel, [((2, 1024, 1536), bf16)], 'expert_grads'...  21.6 us
  transfers between devices with their start and end apart: 9, of which 2 were waited for; matrix products, arithmetic and copies ran while one was open for 4% of the time, Pallas kernels for 57%

profile of v3, /device:TPU:1, one launch (start us, length us, event | category | flops | bytes accessed | tf_op | source)
XLA Modules:
  0.0 722.6 jit_solution(15186121116707528754)
XLA Ops:
  12.0 2.2 collective-permute-start
  15.0 1.5 pad_maximum_fusion
  16.6 0.9 slice.172.refs_0_
  17.8 1.7 collective-permute-done
  20.4 36.5 %gather_weights.1 = (bf16[2,2,4,4,192,640]{5,4,3,2,1,0:T(8,128)(2,1)}, bf16[1,256,1536]{2,1,0:T(8,128)(2,1)}) custom-call(bf16[192,640]{1,0:T(8,128)(2,1)} %fusion.27.x_ref, bf16[1,256,1536]{2,1,0:T(8,128)(2,1)} %slice.172.refs_0_, bf16[4,4,64,1024]{3,2,1,0:T(8,128)(2,1)} %bitcast.153, bf16[4,4,64,512]{3,2,1,0:T(8,128)(2,1)} %bitcast.157, ...), custom_call_target="tpu_custom_call" | custom-call | tf_op jit(solution)/shard_map/gather_weights/pallas_call | solution.py:199
  56.9 2.1 fusion.9
  59.9 1.6 broadcast_select_fusion.3
  61.5 3.4 pre.2
  66.2 33.8 %gather_swap.1 = (bf16[4,4,128,1024]{3,2,1,0:T(8,128)(2,1)}, bf16[1,256,1536]{2,1,0:T(8,128)(2,1)}) custom-call(bf16[128,1024]{1,0:T(8,128)(2,1)} %copy-done.29, bf16[1,256,1536]{2,1,0:T(8,128)(2,1)} %get-tuple-element.165.refs_0_), custom_call_target="tpu_custom_call" | custom-call | tf_op jit(solution)/shard_map/gather_swap/pallas_call | solution.py:199
  100.1 2.4 broadcast_select_fusion.1
  105.8 15.8 %attend.2 = (bf16[128,1024]{1,0:T(8,128)(2,1)S(1)}, bf16[4,512,2048]{2,1,0:T(8,128)(2,1)}) custom-call(bf16[128,1024]{1,0:T(8,128)(2,1)S(1)} %get-tuple-element.83.q_ref, bf16[2048,1024]{1,0:T(8,128)(2,1)} %bitcast.132, bf16[2048,1024]{1,0:T(8,128)(2,1)} %bitcast.133, s32[128,1]{1,0:T(8,128)S(1)} %copy.70.lo_ref, s32[128,1]{1,0:T(8,128)S(1)} %iota_add_fusion.hi_ref), custom_call_target="tpu_custom_call" | custom-call | flops 2147483648 | bytes 13631488 | tf_op jit(solution)/shard_map/attend/pallas_call | solution.py:551
  121.6 2.3 post.2
  124.6 24.8 %gather_plain.5 = bf16[4,4,128,1024]{3,2,1,0:T(8,128)(2,1)} custom-call(bf16[128,1024]{1,0:T(8,128)(2,1)} %copy-done.8), custom_call_target="tpu_custom_call" | custom-call | tf_op jit(solution)/shard_map/gather_plain/pallas_call | solution.py:199
  149.4 1.0 broadcast_select_fusion.5
  150.4 1.3 copy.71
  151.9 24.4 %gather_plain.8 = bf16[4,4,128,1024]{3,2,1,0:T(8,128)(2,1)} custom-call(bf16[128,1024]{1,0:T(8,128)(2,1)} %select_bitcast_fusion.2.x_ref.dout_ref), custom_call_target="tpu_custom_call" | custom-call | tf_op jit(solution)/shard_map/gather_plain/pallas_call | solution.py:199
  176.3 1.0 bitcast_select_fusion
  177.5 14.9 %experts.2 = (bf16[2048,1024]{1,0:T(8,128)(2,1)}, bf16[2,640,1024]{2,1,0:T(8,128)(2,1)}, bf16[2,640,1024]{2,1,0:T(8,128)(2,1)}, bf16[8,160,256]{2,1,0:T(8,128)(2,1)S(1)}, f32[2,640,1]{2,1,0:T(8,128)S(1)}) custom-call(bf16[2048,1024]{1,0:T(8,128)(2,1)} %bitcast.147, bf16[32,2048]{1,0:T(8,128)(2,1)S(1)} %bitcast.118, ...), custom_call_target="tpu_custom_call" | custom-call | flops 10737418240 | bytes 20971520 | tf_op jit(solution)/shard_map/experts/pallas_call | solution.py:696
  194.0 23.1 %scatter_sum.6.mix_ref = f32[128,1024]{1,0:T(8,128)} custom-call(bf16[4,4,128,1024]{3,2,1,0:T(8,128)(2,1)} %bitcast.143), custom_call_target="tpu_custom_call" | custom-call | tf_op jit(solution)/shard_map/scatter_sum/pallas_call | solution.py:425
  217.1 1.1 add_convert_fusion.3.x_ref
  218.2 3.4 pre.3
  222.3 22.3 %gather_plain.6 = bf16[4,4,128,1024]{3,2,1,0:T(8,128)(2,1)} custom-call(bf16[128,1024]{1,0:T(8,128)(2,1)} %copy-done.28), custom_call_target="tpu_custom_call" | custom-call | tf_op jit(solution)/shard_map/gather_plain/pallas_call | solution.py:199
  244.7 15.8 %attend.3 = (bf16[128,1024]{1,0:T(8,128)(2,1)S(1)}, bf16[4,512,2048]{2,1,0:T(8,128)(2,1)}) custom-call(bf16[128,1024]{1,0:T(8,128)(2,1)S(1)} %get-tuple-element.94.q_ref, bf16[2048,1024]{1,0:T(8,128)(2,1)} %bitcast.128, bf16[2048,1024]{1,0:T(8,128)(2,1)} %bitcast.129, s32[128,1]{1,0:T(8,128)S(1)} %copy.70.lo_ref, s32[128,1]{1,0:T(8,128)S(1)} %iota_add_fusion.hi_ref), custom_call_target="tpu_custom_call" | custom-call | flops 2147483648 | bytes 13631488 | tf_op jit(solution)/shard_map/attend/pallas_call | solution.py:551
  260.4 2.3 post.3
  264.2 19.8 %gather_plain.7 = bf16[4,4,128,1024]{3,2,1,0:T(8,128)(2,1)} custom-call(bf16[128,1024]{1,0:T(8,128)(2,1)} %copy-done.10), custom_call_target="tpu_custom_call" | custom-call | tf_op jit(solution)/shard_map/gather_plain/pallas_call | solution.py:199
  284.1 14.6 %experts.3 = (bf16[2048,1024]{1,0:T(8,128)(2,1)}, bf16[2,640,1024]{2,1,0:T(8,128)(2,1)}, bf16[2,640,1024]{2,1,0:T(8,128)(2,1)}, bf16[8,160,256]{2,1,0:T(8,128)(2,1)S(1)}, f32[2,640,1]{2,1,0:T(8,128)S(1)}) custom-call(bf16[2048,1024]{1,0:T(8,128)(2,1)} %bitcast.148, bf16[32,2048]{1,0:T(8,128)(2,1)S(1)} %bitcast.117, ...), custom_call_target="tpu_custom_call" | custom-call | flops 10737418240 | bytes 20971520 | tf_op jit(solution)/shard_map/experts/pallas_call | solution.py:696
  298.7 14.1 %experts_back.2 = (bf16[2048,1024]{1,0:T(8,128)(2,1)}, bf16[2,640,1024]{2,1,0:T(8,128)(2,1)}, bf16[2,640,1024]{2,1,0:T(8,128)(2,1)}, bf16[2,640,512]{2,1,0:T(8,128)(2,1)}, f32[2,640,1]{2,1,0:T(8,128)S(1)}) custom-call(bf16[2048,1024]{1,0:T(8,128)(2,1)} %bitcast.146, bf16[8,160,256]{2,1,0:T(8,128)(2,1)S(1)} %get-tuple-element.102.s_ref, ...), custom_call_target="tpu_custom_call" | custom-call | flops 10737418240 | bytes 25165824 | tf_op jit(solution)/shard_map/experts_back/pallas_call | solution.py:752
  312.8 1.3 copy-done.7
  314.1 10.8 %expert_grads.2 = bf16[2,1024,1536]{2,1,0:T(8,128)(2,1)} custom-call(bf16[2,640,1024]{2,1,0:T(8,128)(2,1)} %get-tuple-element.135.x_ref, bf16[2,640,1024]{2,1,0:T(8,128)(2,1)} %get-tuple-element.140.d_ref, bf16[2,640,1024]{2,1,0:T(8,128)(2,1)} %get-tuple-element.141.dgu_ref, bf16[2,640,512]{2,1,0:T(8,128)(2,1)S(1)} %copy-done.7), custom_call_target="tpu_custom_call" | custom-call | flops 4026531840 | bytes 16777216 | tf_op jit(solution)/shard_map/expert_grads/pallas_call | solution.py:783
  326.0 20.9 %scatter_sum.7.mix_ref = f32[128,1024]{1,0:T(8,128)} custom-call(bf16[4,4,128,1024]{3,2,1,0:T(8,128)(2,1)} %bitcast.140), custom_call_target="tpu_custom_call" | custom-call | tf_op jit(solution)/shard_map/scatter_sum/pallas_call | solution.py:425
  346.9 25.8 %scatter_sum.8.sum_ref = f32[128,1024]{1,0:T(8,128)} custom-call(bf16[4,4,128,1024]{3,2,1,0:T(8,128)(2,1)} %bitcast.142), custom_call_target="tpu_custom_call" | custom-call | tf_op jit(solution)/shard_map/scatter_sum/pallas_call | solution.py:425
  372.7 3.9 mid_back.2
  377.5 12.9 %attend_back.2 = (f32[128,1024]{1,0:T(8,128)S(1)}, bf16[2048,1024]{1,0:T(8,128)(2,1)}) custom-call(bf16[128,1024]{1,0:T(8,128)(2,1)S(1)} %get-tuple-element.94.q_ref, bf16[128,1024]{1,0:T(8,128)(2,1)S(1)} %get-tuple-element.96.o_ref.refs_6_, bf16[128,1024]{1,0:T(8,128)(2,1)S(1)} %get-tuple-element.106.do_ref, bf16[2048,1024]{1,0:T(8,128)(2,1)} %bitcast.130, ...), custom_call_target="tpu_custom_call" | custom-call | flops 4294967296 | bytes 17825792 | tf_op jit(solution)/shard_map/attend_back/pallas_call | solution.py:600
  390.4 21.7 %scatter_sum.9.dkv_ref = f32[128,1024]{1,0:T(8,128)} custom-call(bf16[4,4,128,1024]{3,2,1,0:T(8,128)(2,1)} %bitcast.144), custom_call_target="tpu_custom_call" | custom-call | tf_op jit(solution)/shard_map/scatter_sum/pallas_call | solution.py:425
  412.1 4.4 end_back.2
  417.9 21.6 %gather_plain.9 = bf16[4,4,128,1024]{3,2,1,0:T(8,128)(2,1)} custom-call(bf16[128,1024]{1,0:T(8,128)(2,1)} %copy-done), custom_call_target="tpu_custom_call" | custom-call | tf_op jit(solution)/shard_map/gather_plain/pallas_call | solution.py:199
  439.5 13.7 %experts_back.3 = (bf16[2048,1024]{1,0:T(8,128)(2,1)}, bf16[2,640,1024]{2,1,0:T(8,128)(2,1)}, bf16[2,640,1024]{2,1,0:T(8,128)(2,1)}, bf16[2,640,512]{2,1,0:T(8,128)(2,1)}, f32[2,640,1]{2,1,0:T(8,128)S(1)}) custom-call(bf16[2048,1024]{1,0:T(8,128)(2,1)} %bitcast.149, bf16[8,160,256]{2,1,0:T(8,128)(2,1)S(1)} %copy-done.31, ...), custom_call_target="tpu_custom_call" | custom-call | flops 10737418240 | bytes 25165824 | tf_op jit(solution)/shard_map/experts_back/pallas_call | solution.py:752
  453.2 1.5 copy-done.6
  454.8 10.8 %expert_grads.3 = bf16[2,1024,1536]{2,1,0:T(8,128)(2,1)} custom-call(bf16[2,640,1024]{2,1,0:T(8,128)(2,1)} %get-tuple-element.130.x_ref, bf16[2,640,1024]{2,1,0:T(8,128)(2,1)} %get-tuple-element.143.d_ref, bf16[2,640,1024]{2,1,0:T(8,128)(2,1)} %get-tuple-element.144.dgu_ref, bf16[2,640,512]{2,1,0:T(8,128)(2,1)S(1)} %copy-done.6), custom_call_target="tpu_custom_call" | custom-call | flops 4026531840 | bytes 16777216 | tf_op jit(solution)/shard_map/expert_grads/pallas_call | solution.py:783
  465.7 0.9 copy-done.5
  466.6 2.0 broadcast_select_fusion.9
  469.0 20.7 %scatter_sum.10.sum_ref = f32[128,1024]{1,0:T(8,128)} custom-call(bf16[4,4,128,1024]{3,2,1,0:T(8,128)(2,1)} %bitcast.141), custom_call_target="tpu_custom_call" | custom-call | tf_op jit(solution)/shard_map/scatter_sum/pallas_call | solution.py:425
  489.8 3.9 mid_back.3
  494.5 12.9 %attend_back.3 = (f32[128,1024]{1,0:T(8,128)S(1)}, bf16[2048,1024]{1,0:T(8,128)(2,1)}) custom-call(bf16[128,1024]{1,0:T(8,128)(2,1)S(1)} %get-tuple-element.83.q_ref, bf16[128,1024]{1,0:T(8,128)(2,1)S(1)} %get-tuple-element.88.o_ref.refs_1_, bf16[128,1024]{1,0:T(8,128)(2,1)S(1)} %get-tuple-element.116.do_ref, bf16[2048,1024]{1,0:T(8,128)(2,1)} %bitcast.134, ...), custom_call_target="tpu_custom_call" | custom-call | flops 4294967296 | bytes 17825792 | tf_op jit(solution)/shard_map/attend_back/pallas_call | solution.py:600
  507.4 24.1 %scatter_sum.11.dkv_ref = f32[128,1024]{1,0:T(8,128)} custom-call(bf16[4,4,128,1024]{3,2,1,0:T(8,128)(2,1)} %bitcast.145), custom_call_target="tpu_custom_call" | custom-call | tf_op jit(solution)/shard_map/scatter_sum/pallas_call | solution.py:425
  531.5 4.5 end_back.3
  542.1 2.3 fusion.54
  546.4 1.6 fusion.13.refs_10_
  548.0 9.7 %dense_grads.1 = bf16[2,16,192,1152]{3,2,1,0:T(8,128)(2,1)} custom-call(bf16[128,1024]{1,0:T(8,128)(2,1)S(1)} %copy-done.18, bf16[128,1024]{1,0:T(8,128)(2,1)S(1)} %get-tuple-element.88.o_ref.refs_1_, bf16[128,1024]{1,0:T(8,128)(2,1)S(1)} %get-tuple-element.123.refs_2_, bf16[128,1024]{1,0:T(8,128)(2,1)S(1)} %copy-done.27, bf16[128,1024]{1,0:T(8,128)(2,1)S(1)} %copy-done.25, ...), custom_call_target="tpu_custom_call" | custom-call | flops 1610612736 | bytes 18874368 | tf_op jit(solution)/shard_map/dense_grads/pallas_call | solution.py:874
  557.7 1.0 select_bitcast_fusion.4
  559.6 1.0 select_bitcast_fusion.1
  561.6 2.7 broadcast_select_fusion.refs_0_
  564.3 81.4 %scatter_split.1 = (f32[192,1152]{1,0:T(8,128)}, bf16[2,256,1536]{2,1,0:T(8,128)(2,1)}) custom-call(bf16[2,4,4,192,1152]{4,3,2,1,0:T(8,128)(2,1)} %bitcast.136, bf16[2,256,1536]{2,1,0:T(8,128)(2,1)} %broadcast_select_fusion.refs_0_), custom_call_target="tpu_custom_call" | custom-call | tf_op jit(solution)/shard_map/scatter_split/pallas_call | solution.py:425
  646.7 1.0 slice.157
  647.7 1.1 slice_select_fusion.2.own_ref
  648.8 1.1 select_convert_fusion.other_ref
  649.9 15.0 %cross_sum.1.x_ref = bf16[192,640]{1,0:T(8,128)(2,1)S(1)} custom-call(f32[192,640]{1,0:T(8,128)S(1)} %slice_select_fusion.2.own_ref, bf16[192,640]{1,0:T(8,128)(2,1)S(1)} %select_convert_fusion.other_ref), custom_call_target="tpu_custom_call" | custom-call | tf_op jit(solution)/shard_map/cross_sum/pallas_call | solution.py:918
  665.6 31.8 %gather_split.1 = bf16[2,4,4,192,640]{4,3,2,1,0:T(8,128)(2,1)} custom-call(bf16[192,640]{1,0:T(8,128)(2,1)} %copy-done.12), custom_call_target="tpu_custom_call" | custom-call | tf_op jit(solution)/shard_map/gather_split/pallas_call | solution.py:199
  697.3 8.0 %results.1 = (f32[1024,1024]{1,0:T(8,128)}, f32[1024,512]{1,0:T(8,128)}, f32[1024,512]{1,0:T(8,128)}, f32[1024,1024]{1,0:T(8,128)}) custom-call(bf16[2,16,192,640]{3,2,1,0:T(8,128)(2,1)} %bitcast.137), custom_call_target="tpu_custom_call" | custom-call | bytes 20971520 | tf_op jit(solution)/shard_map/results/pallas_call | solution.py:1014
  705.3 1.2 slice_select_fusion.3
  706.6 1.1 fusion.52
  707.7 1.8 copy.96
  711.1 2.6 convert_add_fusion
  713.7 1.7 slice_bitcast_fusion
  (192 shorter events, 34.8 us)
Async XLA Ops:
  7.2 170.3 %all-gather.5.cloned.1.call-start = ((), (), s32[]{:S(2)}) async-start(), calls=%async_computation.2 | async-start | bytes 3932160 | tf_op jit(solution)/shard_map/all_gather | solution.py:1090
  12.0 5.8 copy-start.45
  12.0 7.5 %collective-permute-start = (bf16[192,640]{1,0:T(8,128)(2,1)S(1)}, bf16[192,640]{1,0:T(8,128)(2,1)S(1)}, u32[]{:S(2)}, u32[]{:S(2)}) collective-permute-start(bf16[192,640]{1,0:T(8,128)(2,1)S(1)} %fusion.30), channel_id=1, source_target_pairs={{0,64},{64,0},{1,65},{65,1},{2,66},{66,2},{3,67},{67,3},{4,68},{68... | collective-permute-start | bytes 737288 | tf_op jit(solution)/shard_map/ppermute | solution.py:1026
  19.5 37.4 %copy-start.44 = (bf16[192,640]{1,0:T(8,128)(2,1)}, bf16[192,640]{1,0:T(8,128)(2,1)S(1)}, u32[]{:S(2)}) copy-start(bf16[192,640]{1,0:T(8,128)(2,1)S(1)} %collective-permute-done) | copy-start | bytes 737284
  56.8 3.0 copy-start.50
  56.9 3.0 copy-start.43
  59.0 0.9 copy-start.36
  64.8 0.7 copy-start.17
  65.5 0.7 copy-start.29
  65.6 111.9 %all-gather.7.cloned.1.call-start = ((), (), s32[]{:S(2)}) async-start(), calls=%async_computation.3 | async-start | bytes 3932160 | tf_op jit(solution)/shard_map/all_gather | solution.py:1090
  100.0 4.0 copy-start.49
  100.0 4.9 copy-start.52
  100.0 5.0 copy-start.46
  102.5 181.5 %all-gather.9.cloned.1.call-start = ((), (), s32[]{:S(2)}) async-start(), calls=%async_computation.4 | async-start | bytes 3932160 | tf_op jit(solution)/shard_map/all_gather | solution.py:1090
  103.3 180.8 %all-gather.11.cloned.1.call-start = ((), (), s32[]{:S(2)}) async-start(), calls=%async_computation.5 | async-start | bytes 3932160 | tf_op jit(solution)/shard_map/all_gather | solution.py:1090
  103.8 457.6 %reduce-scatter.3.cloned.1.call-start = ((), (), s32[]{:S(2)}) async-start(), calls=%async_computation.6 | async-start | bytes 7864320 | tf_op jit(solution)/shard_map/reduce_scatter | solution.py:975
  105.8 15.8 %copy-start.51 = (bf16[1,1024]{1,0:T(2,128)(2,1)S(1)}, bf16[1,1024]{1,0:T(2,128)(2,1)}, u32[]{:S(2)}) copy-start(bf16[1,1024]{1,0:T(2,128)(2,1)} %param.23) | copy-start | bytes 6148
  123.9 0.7 copy-start.8
  124.6 92.5 %copy-start.3 = (f32[128,1024]{1,0:T(8,128)}, f32[128,1024]{1,0:T(8,128)S(1)}, u32[]{:S(2)}) copy-start(f32[128,1024]{1,0:T(8,128)S(1)} %get-tuple-element.89.h_ref) | copy-start | bytes 1572868
  124.6 24.8 %copy-start.37 = (bf16[16,192,128]{2,1,0:T(8,128)(2,1)S(1)}, bf16[16,192,128]{2,1,0:T(8,128)(2,1)}, u32[]{:S(2)}) copy-start(bf16[16,192,128]{2,1,0:T(8,128)(2,1)} %copy-done.36) | copy-start | bytes 2359300
  192.3 0.8 copy-start.30
  193.2 0.8 copy-start.32
  221.6 0.7 copy-start.28
  222.3 38.1 %copy-start.19 = (bf16[128,1024]{1,0:T(8,128)(2,1)}, bf16[128,1024]{1,0:T(8,128)(2,1)S(1)}, u32[]{:S(2)}) copy-start(bf16[128,1024]{1,0:T(8,128)(2,1)S(1)} %get-tuple-element.126.refs_5_) | copy-start | bytes 786436
  262.7 0.8 copy-start.4
  263.5 0.7 copy-start.10
  312.8 1.3 copy-start.7
  325.0 236.6 %reduce-scatter.5.cloned.1.call-start = ((), (), s32[]{:S(2)}) async-start(), calls=%async_computation.7 | async-start | bytes 7864320 | tf_op jit(solution)/shard_map/reduce_scatter | solution.py:975
  346.9 25.8 %copy-start.2 = (bf16[128,1024]{1,0:T(8,128)(2,1)S(1)}, bf16[128,1024]{1,0:T(8,128)(2,1)}, u32[]{:S(2)}) copy-start(bf16[128,1024]{1,0:T(8,128)(2,1)} %select_bitcast_fusion.2.x_ref.dout_ref) | copy-start | bytes 786436
  346.9 25.8 %copy-start.11 = (bf16[128,1024]{1,0:T(8,128)(2,1)S(1)}, bf16[128,1024]{1,0:T(8,128)(2,1)}, u32[]{:S(2)}) copy-start(bf16[128,1024]{1,0:T(8,128)(2,1)} %copy-done.10) | copy-start | bytes 786436
  376.7 0.8 copy-start.16
  377.5 12.9 %copy-start.21 = (bf16[128,1024]{1,0:T(8,128)(2,1)}, bf16[128,1024]{1,0:T(8,128)(2,1)S(1)}, u32[]{:S(2)}) copy-start(bf16[128,1024]{1,0:T(8,128)(2,1)S(1)} %get-tuple-element.129.refs_9_) | copy-start | bytes 786436
  416.5 0.7 copy-start
  417.2 0.7 copy-start.22
  417.9 35.3 %copy-start.23 = (bf16[128,1024]{1,0:T(8,128)(2,1)}, bf16[128,1024]{1,0:T(8,128)(2,1)S(1)}, u32[]{:S(2)}) copy-start(bf16[128,1024]{1,0:T(8,128)(2,1)S(1)} %get-tuple-element.128.refs_8_) | copy-start | bytes 786436
  417.9 21.6 %copy-start.31 = (bf16[8,160,256]{2,1,0:T(8,128)(2,1)S(1)}, bf16[8,160,256]{2,1,0:T(8,128)(2,1)}, u32[]{:S(2)}) copy-start(bf16[8,160,256]{2,1,0:T(8,128)(2,1)} %copy-done.30) | copy-start | bytes 1966084
  417.9 21.6 %copy-start.33 = (f32[2,640,1]{2,1,0:T(8,128)S(1)}, f32[2,640,1]{2,1,0:T(8,128)}, u32[]{:S(2)}) copy-start(f32[2,640,1]{2,1,0:T(8,128)} %copy-done.32) | copy-start | bytes 15364
  453.2 12.4 %copy-start.13 = (f32[2,640,1]{2,1,0:T(8,128)}, f32[2,640,1]{2,1,0:T(8,128)S(1)}, u32[]{:S(2)}) copy-start(f32[2,640,1]{2,1,0:T(8,128)S(1)} %get-tuple-element.131) | copy-start | bytes 15364
  453.2 1.6 copy-start.6
  465.6 1.0 copy-start.5
  468.6 21.2 %copy-start.1 = (bf16[128,1024]{1,0:T(8,128)(2,1)S(1)}, bf16[128,1024]{1,0:T(8,128)(2,1)}, u32[]{:S(2)}) copy-start(bf16[128,1024]{1,0:T(8,128)(2,1)} %copy-done) | copy-start | bytes 786436
  468.6 21.2 %copy-start.9 = (bf16[128,1024]{1,0:T(8,128)(2,1)S(1)}, bf16[128,1024]{1,0:T(8,128)(2,1)}, u32[]{:S(2)}) copy-start(bf16[128,1024]{1,0:T(8,128)(2,1)} %copy-done.8) | copy-start | bytes 786436
  468.6 89.1 %collective-permute-start.1 = (bf16[128,1024]{1,0:T(8,128)(2,1)}, bf16[128,1024]{1,0:T(8,128)(2,1)}, u32[]{:S(2)}, u32[]{:S(2)}) collective-permute-start(bf16[128,1024]{1,0:T(8,128)(2,1)} %get-tuple-element.156), channel_id=1, source_target_pairs={{0,64},{64,0},{1,65},{65,1},{2,66},{66,2},{3,67},{67,3},{4,68},{68... | collective-permute-start | bytes 786440 | tf_op jit(solution)/shard_map/ppermute | solution.py:1026
  493.7 0.8 copy-start.15
  494.5 12.9 %copy-start.24 = (bf16[128,1024]{1,0:T(8,128)(2,1)}, bf16[128,1024]{1,0:T(8,128)(2,1)S(1)}, u32[]{:S(2)}) copy-start(bf16[128,1024]{1,0:T(8,128)(2,1)S(1)} %get-tuple-element.125.refs_4_) | copy-start | bytes 786436
  536.0 0.7 copy-start.26
  536.7 5.1 copy-start.14
  537.4 22.1 %collective-permute-start.2 = (bf16[128,1024]{1,0:T(8,128)(2,1)}, bf16[128,1024]{1,0:T(8,128)(2,1)}, u32[]{:S(2)}, u32[]{:S(2)}) collective-permute-start(bf16[128,1024]{1,0:T(8,128)(2,1)} %broadcast_select_fusion.7), channel_id=1, source_target_pairs={{0,64},{64,0},{1,65},{65,1},{2,66},{66,2},{3,67},{67,3},{4,68},{68... | collective-permute-start | bytes 786440 | tf_op jit(solution)/shard_map/ppermute | solution.py:1026
  541.8 3.2 copy-start.34
  542.1 4.1 copy-start.47
  544.4 1.8 copy-start.48
  545.1 1.3 copy-start.38
  545.1 1.3 copy-start.39
  545.1 1.3 copy-start.40
  545.1 1.3 copy-start.41
  546.2 1.8 copy-start.18
  546.2 1.8 copy-start.20
  546.2 1.8 copy-start.25
  546.2 1.8 copy-start.27
  548.0 9.7 %copy-start.42 = (bf16[128,1024]{1,0:T(8,128)(2,1)S(1)}, bf16[128,1024]{1,0:T(8,128)(2,1)}, u32[]{:S(2)}) copy-start(bf16[128,1024]{1,0:T(8,128)(2,1)} %get-tuple-element.157) | copy-start | bytes 786436
  664.9 0.7 copy-start.12
  705.3 5.8 copy-start.35
Sparse Core Ops, SparseCore 0:
  65.7 43.0 all-gather.4
  111.1 29.5 all-gather.6
  142.9 31.9 all-gather.8
  177.0 31.9 all-gather.10
  325.1 80.3 reduce-scatter.2
  465.7 95.8 reduce-scatter.4

commit v4 on v3

--- a/solution.py
+++ b/solution.py
@@ -447,7 +447,7 @@
 
 
 def local_call(kernel, outs, name, grid=None, in_specs=None, out_specs=None, flops=0, moved=0):
-    params = pltpu.CompilerParams(vmem_limit_bytes=52 << 20)
+    params = pltpu.CompilerParams(vmem_limit_bytes=60 << 20)
     kinds = dict(
         out_shape=[jax.ShapeDtypeStruct(s, d) for s, d in outs],
         compiler_params=params,
@@ -644,7 +644,7 @@
         b = b_ref[256 * p : 256 * p + 256, :]
         mask = mask_ref[:, 256 * p : 256 * p + 256]
         chosen = mask.astype(f32) > 0.5
-        logits = lax.dot_general(wr_ref[...], b, (((0,), (1,)), ((), ())), preferred_element_type=f32)
+        logits = dot_t(wr_ref[...], b)
         top = jnp.max(jnp.where(chosen, logits, masked_score), axis=0, keepdims=True)
         e = jnp.where(chosen, jnp.exp(jnp.where(chosen, logits - top, 0.0)), 0.0)
         gates = e / jnp.sum(e, axis=0, keepdims=True)
@@ -658,9 +658,10 @@
             s = jnp.where(hit, 1.0, 0.0)
             part = slice(SLOTS * p, SLOTS * p + SLOTS)
             gate_ref[j, part, :] = jnp.sum(s * gate, axis=1, keepdims=True)
-            s = s.astype(bf16)
-            s_ref[p, SLOTS * j : SLOTS * j + SLOTS, :] = s
-            x_ref[j, part, :] = dot(s, b).astype(bf16)
+            s_ref[p, SLOTS * j : SLOTS * j + SLOTS, :] = s.astype(bf16)
+        rows = dot(s_ref[p], b).astype(bf16)
+        for j in range(2):
+            x_ref[j, part, :] = rows[SLOTS * j : SLOTS * j + SLOTS]
     ys = []
     for j in range(2):
         x = x_ref[j]
@@ -704,7 +705,7 @@
         in_specs=[
             tokens(1024),
             spec((32, ROWS), lambda i: (0, i)),
-            fixed((1024, 32)),
+            fixed((32, 1024)),
             fixed((32, 8)),
             fixed((1, 1024, 1536)),
             fixed((1, 1024, 1536)),
@@ -768,30 +769,21 @@
 
 
 def expert_grads_kernel(x_ref, d_ref, dgu_ref, in_ref, out_ref):
-    which = pl.program_id(1)
-
-    @pl.when(which < 2)
-    def _():
-        out_ref[0] = t_dot(x_ref[0], dgu_ref[0]).astype(bf16)
-
-    @pl.when(which == 2)
-    def _():
-        out_ref[0] = t_dot(d_ref[0], in_ref[0]).astype(bf16)
+    out_ref[0, :, 0:1024] = t_dot(x_ref[0], dgu_ref[0]).astype(bf16)
+    out_ref[0, :, 1024:1536] = t_dot(d_ref[0], in_ref[0]).astype(bf16)
 
 
 def expert_grads(x, d, dgu, inner):
+    def one(cols):
+        return spec((1, FULL, cols), lambda j: (j, 0, 0))
+
     return local_call(
         expert_grads_kernel,
         [((2, 1024, 1536), bf16)],
         "expert_grads",
-        grid=(2, 3),
-        in_specs=[
-            spec((1, FULL, 1024), lambda j, c: (j, 0, 0)),
-            spec((1, FULL, 1024), lambda j, c: (j, 0, 0)),
-            spec((1, FULL, 512), lambda j, c: (j, 0, jnp.minimum(c, 1))),
-            spec((1, FULL, 512), lambda j, c: (j, 0, 0)),
-        ],
-        out_specs=[spec((1, 1024, 512), lambda j, c: (j, 0, c))],
+        grid=(2,),
+        in_specs=[one(1024), one(1024), one(1024), one(512)],
+        out_specs=[spec((1, 1024, 1536), lambda j: (j, 0, 0))],
         flops=3 * 2 * 1280 * 1024 * 512,
         moved=16 << 20,
     )(x, d, dgu, inner)[0]
@@ -810,7 +802,7 @@
     gates = chosen_gates(b, wr, mask_ref[...])
     level = jnp.sum(dout * mix_ref[...], axis=-1, keepdims=True)
     taken = (gates * -level).astype(bf16)
-    router_ref[...] = t_dot(b, taken)
+    router_ref[...] = t_dot(taken, b)
     db = sum_ref[...] + dot_t(taken, wr)
     gain_grad_ref[...] = jnp.broadcast_to(jnp.sum(db * n, axis=0, keepdims=True), gain_grad_ref.shape)
     ng = db * gain_ref[...]
@@ -863,10 +855,10 @@
                 out_ref[h, t, 0:64, cols] = gq[part, side]
                 out_ref[h, t, 64:128, cols] = gkv[part, side]
                 out_ref[h, t, 128:192, cols] = go[part, side]
-    for t in range(2):
-        for h in range(2):
-            out_ref[h, t, 0:64, 1024:1152] = small_ref[h, 64 * t : 64 * t + 64, :]
-            out_ref[h, t, 64:192, 1024:1152] = jnp.zeros((128, 128), bf16)
+    for h in range(2):
+        out_ref[h, 0, 0:64, 1024:1152] = small_ref[h]
+        out_ref[h, 0, 64:192, 1024:1152] = jnp.zeros((128, 128), bf16)
+        out_ref[h, 1, :, 1024:1152] = jnp.zeros((192, 128), bf16)
 
 
 def dense_grads(layer0, layer1, small):
@@ -876,7 +868,7 @@
         [((2, 16, 192, 1152), bf16)],
         "dense_grads",
         grid=(8,),
-        in_specs=([narrow, narrow] + [fixed((128, 1024))] * 3) * 2 + [spec((2, 128, 128), lambda i: (0, i, 0))],
+        in_specs=([narrow, narrow] + [fixed((128, 1024))] * 3) * 2 + [spec((2, 64, 128), lambda i: (0, 0, i))],
         out_specs=[spec((2, 2, 192, 1152), lambda i: (0, i, 0, 0))],
         flops=6 * 2 * 128 * 1024 * 1024,
         moved=18 << 20,
@@ -957,7 +949,7 @@
         flops=2 * 128 * 1024 * 1024, moved=4 << 20,
     )(x, o, weights, gain_moe)
     b_all = gather_rows(b, 1)
-    y, rows, gu, choices, gate = experts(b_all, masks[1], wr, pick, w)
+    y, rows, gu, choices, gate = experts(b_all, masks[1], wr.T, pick, w)
     mix = scatter_sum(y, 2)
     out = (h + mix).astype(bf16)
     return out, w, (x, a, q, kv_all, o, probs, h, b, rows, gu, choices, gate, mix)
@@ -976,10 +968,10 @@
         expert_grads(rows, drows, dgu, inner), "dp", scatter_dimension=1, tiled=True)
     router_cols = jnp.einsum("jrd,jr->jd", rows, coef[:, :, 0].astype(bf16), preferred_element_type=f32)
     router_part = jnp.einsum(
-        "jd,je->de", router_cols, pick_rows[:2], preferred_element_type=f32, precision=lax.Precision.HIGHEST)
+        "je,jd->ed", pick_rows[:2], router_cols, preferred_element_type=f32, precision=lax.Precision.HIGHEST)
     dh, dattn, do, router_own, gain_moe_grad = local_call(
         mid_back_kernel,
-        [((128, 1024), f32), ((128, 1024), bf16), ((128, 1024), bf16), ((1024, 32), f32), ((8, 1024), f32)],
+        [((128, 1024), f32), ((128, 1024), bf16), ((128, 1024), bf16), ((32, 1024), f32), ((8, 1024), f32)],
         "mid_back", in_specs={8: out_block(layer)}, flops=2 * 128 * 1024 * 1024, moved=5 << 20,
     )(db_sum, dout, mix, h, b, gain_moe, wr, masks[0], weights)
     dq, dkv = attend_back(q, o, do, kv_all, probs)
@@ -990,13 +982,7 @@
         "end_back", in_specs={4: qkv_block(layer)}, flops=2 * 128 * 1024 * 2048, moved=8 << 20,
     )(dq, dkv_sum, cosine, sine, weights, x, gain_attn, dh)
     small = jnp.concatenate(
-        [
-            router_part + router_own,
-            gain_attn_grad[0][:, None],
-            gain_moe_grad[0][:, None],
-            jnp.zeros((1024, 30), f32),
-        ],
-        axis=1,
+        [router_part + router_own, gain_attn_grad[0:1], gain_moe_grad[0:1], jnp.zeros((30, 1024), f32)], axis=0
     ).astype(bf16)
     return dx, expert_grad, (a, o, dq_lin, dkv_lin, dattn), small
 
@@ -1122,7 +1108,7 @@
     dx1, eg1, dg1, small1 = backward(cot, cot_all, saved1, 1, place, weights, dense[1], expert_w[1], masks[1])
     dx0, eg0, dg0, small0 = backward(dx1, None, saved0, 0, place, weights, dense[0], expert_w[0], masks[0])
     eg_sent = jnp.where(first, eg1, eg0)
-    both_small = jnp.pad(jnp.stack([small0, small1]), ((0, 0), (0, 0), (0, 64)))
+    both_small = jnp.stack([small0, small1])
     dense_sum, eg_away = scatter_sum(dense_grads(dg0, dg1, both_small), 4, eg_sent)
 
     def in_place(l0, l1):
@@ -1140,7 +1126,7 @@
     other = jnp.where(first, full1, full0).astype(bf16)
     summed = gather_split(cross_sum(own, other, 6), 7)
     grad_query, grad_key, grad_value, grad_out = results(summed)
-    grad_small = mine(summed[:, :, 0:64, 512:576]).reshape(1024, 64).astype(f32)
+    grad_small = mine(summed[:, ::2, 0:64, 512:640]).transpose(1, 0, 2).reshape(64, 1024).astype(f32)
     eg = jnp.where(first, eg0, eg1).astype(f32) + eg_away.astype(f32)
     return (
         acts,
@@ -1149,9 +1135,9 @@
         grad_key[None],
         grad_value[None],
         grad_out[None],
-        grad_small[:, 32][None],
-        grad_small[:, 33][None],
-        grad_small[None, :, :32],
+        grad_small[32:33],
+        grad_small[33:34],
+        grad_small[:32].T[None],
         eg[None, :, :, 0:512],
         eg[None, :, :, 512:1024],
         eg[None, :, :, 1024:1536],

time: 729 us -> 714 us (0.979)
  local copies, waits for them, and re-layouts: 33 us -> 20.4 us
    unnamed x110 -> x49, local copies, waits for them, and re-layouts: 18.9 us -> 2.11 us
    pallas_call x8, Pallas kernels: 28.1 us -> 35.5 us  [call(): return pl.pallas_call(kernel, grid=(1,), in_specs=ins, **kinds)(*args)]
  transfers between devices with their start and end apart: 9 -> 9, of which waited for: 2 -> 1; matrix products, arithmetic and copies ran while one was open for 4% -> 4% of each run, Pallas kernels for 57% -> 59%
where the time goes in v4:
time: 714 us; the launch traced here: 707 us
  Pallas kernels  627 us (88%)
  other arithmetic  30.3 us (4%)
  local copies, waits for them, and re-layouts  20.4 us (3%)
  between operations  15.1 us (2%)
    pallas_call x8, Pallas kernels, gather_call(): pl.pallas_call(functools.partial(gather_kernel, kind), out_shape=outs, in...  213 us
    pallas_call x7, Pallas kernels, scatter_sum(): pl.pallas_call(functools.partial(scatter_kernel, split), out_shape=[summe...  211 us
    pallas_call x8, Pallas kernels, call(): return pl.pallas_call(kernel, grid=(1,), in_specs=ins, **kinds)(*args)  35.5 us
    pallas_call x2, Pallas kernels, attend(): local_call(attend_kernel, [((128, 1024), bf16), ((4, 512, 2048), bf16)],...  32.1 us
    pallas_call x2, Pallas kernels, experts(): local_call(experts_kernel, [((rows, 1024), bf16), ((2, FULL, 1024), bf16)...  28.3 us
    pallas_call x2, Pallas kernels, experts_back(): local_call(experts_back_kernel, [((rows, 1024), bf16), ((2, FULL, 1024),...  27.9 us
    pallas_call x2, Pallas kernels, attend_back(): local_call(attend_back_kernel, [((128, 1024), f32), ((2048, 1024), bf16)]...  25.9 us
    pallas_call x2, Pallas kernels, expert_grads(): local_call(expert_grads_kernel, [((2, 1024, 1536), bf16)], 'expert_grads'...  18.7 us
  transfers between devices with their start and end apart: 9, of which 1 were waited for; matrix products, arithmetic and copies ran while one was open for 4% of the time, Pallas kernels for 59%

profile of v4, /device:TPU:1, one launch (start us, length us, event | category | flops | bytes accessed | tf_op | source)
XLA Modules:
  0.0 707.4 jit_solution(16328568958204073341)
XLA Ops:
  10.1 0.8 dynamic-slice_bitcast_fusion.1
  10.9 0.9 dynamic-slice_bitcast_fusion
  12.0 2.2 collective-permute-start
  15.0 1.5 pad_maximum_fusion
  18.0 0.9 slice.185.refs_0_
  21.2 36.2 %gather_weights.1 = (bf16[2,2,4,4,192,640]{5,4,3,2,1,0:T(8,128)(2,1)}, bf16[1,256,1536]{2,1,0:T(8,128)(2,1)}) custom-call(bf16[192,640]{1,0:T(8,128)(2,1)} %fusion.10.x_ref, bf16[1,256,1536]{2,1,0:T(8,128)(2,1)} %slice.185.refs_0_, bf16[4,4,64,1024]{3,2,1,0:T(8,128)(2,1)} %bitcast.167, bf16[4,4,64,512]{3,2,1,0:T(8,128)(2,1)} %bitcast.171, ...), custom_call_target="tpu_custom_call" | custom-call | tf_op jit(solution)/shard_map/gather_weights/pallas_call | solution.py:199
  57.4 2.1 fusion.1
  60.6 1.6 broadcast_select_fusion.3
  62.2 4.2 pre.2
  66.5 33.3 %gather_swap.1 = (bf16[4,4,128,1024]{3,2,1,0:T(8,128)(2,1)}, bf16[1,256,1536]{2,1,0:T(8,128)(2,1)}) custom-call(bf16[128,1024]{1,0:T(8,128)(2,1)} %get-tuple-element.86.x_ref, bf16[1,256,1536]{2,1,0:T(8,128)(2,1)} %get-tuple-element.165.refs_0_), custom_call_target="tpu_custom_call" | custom-call | tf_op jit(solution)/shard_map/gather_swap/pallas_call | solution.py:199
  99.8 2.4 broadcast_select_fusion.1
  108.3 0.8 copy.70
  109.2 0.8 copy.64
  110.0 15.9 %attend.2 = (bf16[128,1024]{1,0:T(8,128)(2,1)}, bf16[4,512,2048]{2,1,0:T(8,128)(2,1)}) custom-call(bf16[128,1024]{1,0:T(8,128)(2,1)} %get-tuple-element.83.q_ref, bf16[2048,1024]{1,0:T(8,128)(2,1)} %bitcast.145, bf16[2048,1024]{1,0:T(8,128)(2,1)} %bitcast.146, s32[128,1]{1,0:T(8,128)} %copy.63.lo_ref, s32[128,1]{1,0:T(8,128)} %iota_add_fusion.hi_ref), custom_call_target="tpu_custom_call" | custom-call | flops 2147483648 | bytes 13631488 | tf_op jit(solution)/shard_map/attend/pallas_call | solution.py:551
  126.5 3.3 post.2
  129.8 24.5 %gather_plain.5 = bf16[4,4,128,1024]{3,2,1,0:T(8,128)(2,1)} custom-call(bf16[128,1024]{1,0:T(8,128)(2,1)} %get-tuple-element.90.x_ref.b_ref), custom_call_target="tpu_custom_call" | custom-call | tf_op jit(solution)/shard_map/gather_plain/pallas_call | solution.py:199
  154.4 24.4 %gather_plain.8 = bf16[4,4,128,1024]{3,2,1,0:T(8,128)(2,1)} custom-call(bf16[128,1024]{1,0:T(8,128)(2,1)} %select_bitcast_fusion.2.x_ref.dout_ref), custom_call_target="tpu_custom_call" | custom-call | tf_op jit(solution)/shard_map/gather_plain/pallas_call | solution.py:199
  178.8 0.8 fusion.29.wcol_ref
  179.7 14.1 %experts.2 = (bf16[2048,1024]{1,0:T(8,128)(2,1)}, bf16[2,640,1024]{2,1,0:T(8,128)(2,1)}, bf16[2,640,1024]{2,1,0:T(8,128)(2,1)}, bf16[8,160,256]{2,1,0:T(8,128)(2,1)}, f32[2,640,1]{2,1,0:T(8,128)}) custom-call(bf16[2048,1024]{1,0:T(8,128)(2,1)} %bitcast.161, bf16[32,2048]{1,0:T(8,128)(2,1)} %bitcast.179, bf16[32,1024]{1,0:T(8,128)(2,1)} %copy.66.wr_ref, ...), custom_call_target="tpu_custom_call" | custom-call | flops 10737418240 | bytes 20971520 | tf_op jit(solution)/shard_map/experts/pallas_call | solution.py:697
  193.8 24.3 %scatter_sum.6.mix_ref = f32[128,1024]{1,0:T(8,128)} custom-call(bf16[4,4,128,1024]{3,2,1,0:T(8,128)(2,1)} %bitcast.157), custom_call_target="tpu_custom_call" | custom-call | tf_op jit(solution)/shard_map/scatter_sum/pallas_call | solution.py:425
  218.1 1.8 add_convert_fusion.1.x_ref
  219.9 4.2 pre.3
  224.2 22.0 %gather_plain.6 = bf16[4,4,128,1024]{3,2,1,0:T(8,128)(2,1)} custom-call(bf16[128,1024]{1,0:T(8,128)(2,1)} %get-tuple-element.95.x_ref), custom_call_target="tpu_custom_call" | custom-call | tf_op jit(solution)/shard_map/gather_plain/pallas_call | solution.py:199
  246.1 16.2 %attend.3 = (bf16[128,1024]{1,0:T(8,128)(2,1)}, bf16[4,512,2048]{2,1,0:T(8,128)(2,1)}) custom-call(bf16[128,1024]{1,0:T(8,128)(2,1)} %get-tuple-element.94.q_ref, bf16[2048,1024]{1,0:T(8,128)(2,1)} %bitcast.141, bf16[2048,1024]{1,0:T(8,128)(2,1)} %bitcast.142, s32[128,1]{1,0:T(8,128)} %copy.63.lo_ref, s32[128,1]{1,0:T(8,128)} %iota_add_fusion.hi_ref), custom_call_target="tpu_custom_call" | custom-call | flops 2147483648 | bytes 13631488 | tf_op jit(solution)/shard_map/attend/pallas_call | solution.py:551
  262.4 3.3 post.3
  265.6 20.0 %gather_plain.7 = bf16[4,4,128,1024]{3,2,1,0:T(8,128)(2,1)} custom-call(bf16[128,1024]{1,0:T(8,128)(2,1)} %get-tuple-element.98.x_ref.b_ref), custom_call_target="tpu_custom_call" | custom-call | tf_op jit(solution)/shard_map/gather_plain/pallas_call | solution.py:199
  285.7 14.1 %experts.3 = (bf16[2048,1024]{1,0:T(8,128)(2,1)}, bf16[2,640,1024]{2,1,0:T(8,128)(2,1)}, bf16[2,640,1024]{2,1,0:T(8,128)(2,1)}, bf16[8,160,256]{2,1,0:T(8,128)(2,1)}, f32[2,640,1]{2,1,0:T(8,128)}) custom-call(bf16[2048,1024]{1,0:T(8,128)(2,1)} %bitcast.162, bf16[32,2048]{1,0:T(8,128)(2,1)} %bitcast.178, bf16[32,1024]{1,0:T(8,128)(2,1)} %copy.71.wr_ref, ...), custom_call_target="tpu_custom_call" | custom-call | flops 10737418240 | bytes 20971520 | tf_op jit(solution)/shard_map/experts/pallas_call | solution.py:697
  299.8 13.9 %experts_back.2 = (bf16[2048,1024]{1,0:T(8,128)(2,1)}, bf16[2,640,1024]{2,1,0:T(8,128)(2,1)}, bf16[2,640,1024]{2,1,0:T(8,128)(2,1)}, bf16[2,640,512]{2,1,0:T(8,128)(2,1)}, f32[2,640,1]{2,1,0:T(8,128)}) custom-call(bf16[2048,1024]{1,0:T(8,128)(2,1)} %bitcast.160, bf16[8,160,256]{2,1,0:T(8,128)(2,1)} %get-tuple-element.102.s_ref, ...), custom_call_target="tpu_custom_call" | custom-call | flops 10737418240 | bytes 25165824 | tf_op jit(solution)/shard_map/experts_back/pallas_call | solution.py:753
  313.7 9.4 %expert_grads.2 = bf16[2,1024,1536]{2,1,0:T(8,128)(2,1)} custom-call(bf16[2,640,1024]{2,1,0:T(8,128)(2,1)} %get-tuple-element.135.x_ref, bf16[2,640,1024]{2,1,0:T(8,128)(2,1)} %get-tuple-element.140.d_ref, bf16[2,640,1024]{2,1,0:T(8,128)(2,1)} %get-tuple-element.141.dgu_ref, bf16[2,640,512]{2,1,0:T(8,128)(2,1)} %get-tuple-element.142.in_ref), custom_call_target="tpu_custom_call" | custom-call | flops 4026531840 | bytes 16777216 | tf_op jit(solution)/shard_map/expert_grads/pallas_call | solution.py:780
  323.9 0.8 fusion.28.wcol_ref
  324.7 20.8 %scatter_sum.7.mix_ref = f32[128,1024]{1,0:T(8,128)} custom-call(bf16[4,4,128,1024]{3,2,1,0:T(8,128)(2,1)} %bitcast.155), custom_call_target="tpu_custom_call" | custom-call | tf_op jit(solution)/shard_map/scatter_sum/pallas_call | solution.py:425
  345.5 25.9 %scatter_sum.8.sum_ref = f32[128,1024]{1,0:T(8,128)} custom-call(bf16[4,4,128,1024]{3,2,1,0:T(8,128)(2,1)} %bitcast.156), custom_call_target="tpu_custom_call" | custom-call | tf_op jit(solution)/shard_map/scatter_sum/pallas_call | solution.py:425
  371.5 4.8 mid_back.2
  376.3 12.8 %attend_back.2 = (f32[128,1024]{1,0:T(8,128)}, bf16[2048,1024]{1,0:T(8,128)(2,1)}) custom-call(bf16[128,1024]{1,0:T(8,128)(2,1)} %get-tuple-element.94.q_ref, bf16[128,1024]{1,0:T(8,128)(2,1)} %get-tuple-element.96.o_ref.refs_6_, bf16[128,1024]{1,0:T(8,128)(2,1)} %get-tuple-element.106.do_ref, bf16[2048,1024]{1,0:T(8,128)(2,1)} %bitcast.143, ...), custom_call_target="tpu_custom_call" | custom-call | flops 4294967296 | bytes 17825792 | tf_op jit(solution)/shard_map/attend_back/pallas_call | solution.py:600
  389.1 20.4 %scatter_sum.9.dkv_ref = f32[128,1024]{1,0:T(8,128)} custom-call(bf16[4,4,128,1024]{3,2,1,0:T(8,128)(2,1)} %bitcast.158), custom_call_target="tpu_custom_call" | custom-call | tf_op jit(solution)/shard_map/scatter_sum/pallas_call | solution.py:425
  409.5 5.3 end_back.2
  414.8 21.6 %gather_plain.9 = bf16[4,4,128,1024]{3,2,1,0:T(8,128)(2,1)} custom-call(bf16[128,1024]{1,0:T(8,128)(2,1)} %get-tuple-element.111.x_ref.dout_ref), custom_call_target="tpu_custom_call" | custom-call | tf_op jit(solution)/shard_map/gather_plain/pallas_call | solution.py:199
  436.4 13.9 %experts_back.3 = (bf16[2048,1024]{1,0:T(8,128)(2,1)}, bf16[2,640,1024]{2,1,0:T(8,128)(2,1)}, bf16[2,640,1024]{2,1,0:T(8,128)(2,1)}, bf16[2,640,512]{2,1,0:T(8,128)(2,1)}, f32[2,640,1]{2,1,0:T(8,128)}) custom-call(bf16[2048,1024]{1,0:T(8,128)(2,1)} %bitcast.163, bf16[8,160,256]{2,1,0:T(8,128)(2,1)} %get-tuple-element.112.s_ref, ...), custom_call_target="tpu_custom_call" | custom-call | flops 10737418240 | bytes 25165824 | tf_op jit(solution)/shard_map/experts_back/pallas_call | solution.py:753
  450.4 9.3 %expert_grads.3 = bf16[2,1024,1536]{2,1,0:T(8,128)(2,1)} custom-call(bf16[2,640,1024]{2,1,0:T(8,128)(2,1)} %get-tuple-element.130.x_ref, bf16[2,640,1024]{2,1,0:T(8,128)(2,1)} %get-tuple-element.143.d_ref, bf16[2,640,1024]{2,1,0:T(8,128)(2,1)} %get-tuple-element.144.dgu_ref, bf16[2,640,512]{2,1,0:T(8,128)(2,1)} %get-tuple-element.145.in_ref), custom_call_target="tpu_custom_call" | custom-call | flops 4026531840 | bytes 16777216 | tf_op jit(solution)/shard_map/expert_grads/pallas_call | solution.py:780
  459.8 0.8 copy-done.3
  460.9 0.8 broadcast_select_fusion.9
  461.7 1.3 collective-permute-start.1
  463.3 20.2 %scatter_sum.10.sum_ref = f32[128,1024]{1,0:T(8,128)} custom-call(bf16[4,4,128,1024]{3,2,1,0:T(8,128)(2,1)} %bitcast.154), custom_call_target="tpu_custom_call" | custom-call | tf_op jit(solution)/shard_map/scatter_sum/pallas_call | solution.py:425
  483.5 4.8 mid_back.3
  488.3 13.1 %attend_back.3 = (f32[128,1024]{1,0:T(8,128)}, bf16[2048,1024]{1,0:T(8,128)(2,1)}) custom-call(bf16[128,1024]{1,0:T(8,128)(2,1)} %get-tuple-element.83.q_ref, bf16[128,1024]{1,0:T(8,128)(2,1)} %get-tuple-element.88.o_ref.refs_1_, bf16[128,1024]{1,0:T(8,128)(2,1)} %get-tuple-element.116.do_ref, bf16[2048,1024]{1,0:T(8,128)(2,1)} %bitcast.147, ...), custom_call_target="tpu_custom_call" | custom-call | flops 4294967296 | bytes 17825792 | tf_op jit(solution)/shard_map/attend_back/pallas_call | solution.py:600
  501.4 23.5 %scatter_sum.11.dkv_ref = f32[128,1024]{1,0:T(8,128)} custom-call(bf16[4,4,128,1024]{3,2,1,0:T(8,128)(2,1)} %bitcast.159), custom_call_target="tpu_custom_call" | custom-call | tf_op jit(solution)/shard_map/scatter_sum/pallas_call | solution.py:425
  525.2 5.6 end_back.3
  531.6 1.7 collective-permute-start.2
  538.7 10.0 %dense_grads.1 = bf16[2,16,192,1152]{3,2,1,0:T(8,128)(2,1)} custom-call(bf16[128,1024]{1,0:T(8,128)(2,1)} %get-tuple-element.122.refs_0_, bf16[128,1024]{1,0:T(8,128)(2,1)} %get-tuple-element.88.o_ref.refs_1_, bf16[128,1024]{1,0:T(8,128)(2,1)} %get-tuple-element.123.refs_2_, bf16[128,1024]{1,0:T(8,128)(2,1)} %get-tuple-element.124.refs_3_, ...), custom_call_target="tpu_custom_call" | custom-call | flops 1610612736 | bytes 18874368 | tf_op jit(solution)/shard_map/dense_grads/pallas_call | solution.py:866
  548.7 0.8 maximum_bitcast_fusion
  549.6 0.8 maximum_bitcast_fusion.1
  550.4 5.0 reduce-scatter.5.cloned.1.call-done
  555.4 2.7 broadcast_select_fusion.refs_0_
  558.2 75.8 %scatter_split.1 = (f32[192,1152]{1,0:T(8,128)}, bf16[2,256,1536]{2,1,0:T(8,128)(2,1)}) custom-call(bf16[2,4,4,192,1152]{4,3,2,1,0:T(8,128)(2,1)} %bitcast.149, bf16[2,256,1536]{2,1,0:T(8,128)(2,1)} %broadcast_select_fusion.refs_0_), custom_call_target="tpu_custom_call" | custom-call | tf_op jit(solution)/shard_map/scatter_split/pallas_call | solution.py:425
  634.0 0.9 slice.167
  634.9 1.0 slice.166
  635.9 1.1 select_convert_fusion.other_ref
  637.0 1.1 slice_select_fusion.2.own_ref
  638.1 15.2 %cross_sum.1.x_ref = bf16[192,640]{1,0:T(8,128)(2,1)S(1)} custom-call(f32[192,640]{1,0:T(8,128)S(1)} %slice_select_fusion.2.own_ref, bf16[192,640]{1,0:T(8,128)(2,1)S(1)} %select_convert_fusion.other_ref), custom_call_target="tpu_custom_call" | custom-call | tf_op jit(solution)/shard_map/cross_sum/pallas_call | solution.py:910
  654.1 31.3 %gather_split.1 = bf16[2,4,4,192,640]{4,3,2,1,0:T(8,128)(2,1)} custom-call(bf16[192,640]{1,0:T(8,128)(2,1)} %copy-done), custom_call_target="tpu_custom_call" | custom-call | tf_op jit(solution)/shard_map/gather_split/pallas_call | solution.py:199
  685.4 1.0 slice.169
  687.7 8.7 %results.1 = (f32[1024,1024]{1,0:T(8,128)}, f32[1024,512]{1,0:T(8,128)}, f32[1024,512]{1,0:T(8,128)}, f32[1024,1024]{1,0:T(8,128)}) custom-call(bf16[2,16,192,640]{3,2,1,0:T(8,128)(2,1)} %bitcast.151), custom_call_target="tpu_custom_call" | custom-call | bytes 20971520 | tf_op jit(solution)/shard_map/results/pallas_call | solution.py:1000
  696.4 2.0 convert_add_fusion
  698.4 1.7 slice_bitcast_fusion
  (130 shorter events, 25.1 us)
Async XLA Ops:
  7.2 172.5 %all-gather.5.cloned.1.call-start = ((), (), s32[]{:S(2)}) async-start(), calls=%async_computation.2 | async-start | bytes 3932160 | tf_op jit(solution)/shard_map/all_gather | solution.py:1076
  12.0 7.0 copy-start.16
  12.0 7.7 %collective-permute-start = (bf16[192,640]{1,0:T(8,128)(2,1)S(1)}, bf16[192,640]{1,0:T(8,128)(2,1)S(1)}, u32[]{:S(2)}, u32[]{:S(2)}) collective-permute-start(bf16[192,640]{1,0:T(8,128)(2,1)S(1)} %fusion.13), channel_id=1, source_target_pairs={{0,64},{64,0},{1,65},{65,1},{2,66},{66,2},{3,67},{67,3},{4,68},{68... | collective-permute-start | bytes 737288 | tf_op jit(solution)/shard_map/ppermute | solution.py:1012
  57.4 2.5 copy-start.21
  57.4 3.1 copy-start.13
  66.4 113.2 %all-gather.7.cloned.1.call-start = ((), (), s32[]{:S(2)}) async-start(), calls=%async_computation.3 | async-start | bytes 3932160 | tf_op jit(solution)/shard_map/all_gather | solution.py:1076
  99.8 3.8 copy-start.20
  99.8 4.0 copy-start.23
  102.2 3.6 copy-start.17
  102.3 183.4 %all-gather.9.cloned.1.call-start = ((), (), s32[]{:S(2)}) async-start(), calls=%async_computation.4 | async-start | bytes 3932160 | tf_op jit(solution)/shard_map/all_gather | solution.py:1076
  103.0 182.6 %all-gather.11.cloned.1.call-start = ((), (), s32[]{:S(2)}) async-start(), calls=%async_computation.5 | async-start | bytes 3932160 | tf_op jit(solution)/shard_map/all_gather | solution.py:1076
  103.6 446.9 %reduce-scatter.3.cloned.1.call-start = ((), (), s32[]{:S(2)}) async-start(), calls=%async_computation.6 | async-start | bytes 7864320 | tf_op jit(solution)/shard_map/reduce_scatter | solution.py:967
  106.6 72.2 %copy-start.9 = (bf16[1024,32]{1,0:T(8,128)(2,1)}, bf16[1024,32]{1,0:T(8,128)(2,1)S(1)}, u32[]{:S(2)}) copy-start(bf16[1024,32]{1,0:T(8,128)(2,1)S(1)} %get-tuple-element.172.wr_ref) | copy-start | bytes 196612
  106.6 217.3 %copy-start.8 = (bf16[1024,32]{1,0:T(8,128)(2,1)}, bf16[1024,32]{1,0:T(8,128)(2,1)S(1)}, u32[]{:S(2)}) copy-start(bf16[1024,32]{1,0:T(8,128)(2,1)S(1)} %get-tuple-element.173.wr_ref) | copy-start | bytes 196612
  110.0 15.9 %copy-start.22 = (bf16[1,1024]{1,0:T(2,128)(2,1)S(1)}, bf16[1,1024]{1,0:T(2,128)(2,1)}, u32[]{:S(2)}) copy-start(bf16[1,1024]{1,0:T(2,128)(2,1)} %param.23) | copy-start | bytes 6148
  193.8 24.3 %copy-start.10 = (f32[128,1024]{1,0:T(8,128)S(1)}, f32[128,1024]{1,0:T(8,128)}, u32[]{:S(2)}) copy-start(f32[128,1024]{1,0:T(8,128)} %get-tuple-element.89.h_ref) | copy-start | bytes 1572868
  323.2 232.3 %reduce-scatter.5.cloned.1.call-start = ((), (), s32[]{:S(2)}) async-start(), calls=%async_computation.7 | async-start | bytes 7864320 | tf_op jit(solution)/shard_map/reduce_scatter | solution.py:967
  459.6 0.9 copy-start.3
  459.6 1.1 copy-start.6
  459.6 1.3 copy-start.11
  459.6 3.4 copy-start.14
  461.7 86.9 %collective-permute-start.1 = (bf16[128,1024]{1,0:T(8,128)(2,1)}, bf16[128,1024]{1,0:T(8,128)(2,1)S(1)}, u32[]{:S(2)}, u32[]{:S(2)}) collective-permute-start(bf16[128,1024]{1,0:T(8,128)(2,1)} %get-tuple-element.156), channel_id=1, source_target_pairs={{0,64},{64,0},{1,65},{65,1},{2,66},{66,2},{3,67},{67,3},{4,68},{68... | collective-permute-start | bytes 786440 | tf_op jit(solution)/shard_map/ppermute | solution.py:1012
  501.4 23.6 %copy-start.15 = (f32[2,640,1]{2,1,0:T(8,128)S(1)}, f32[2,640,1]{2,1,0:T(8,128)}, u32[]{:S(2)}) copy-start(f32[2,640,1]{2,1,0:T(8,128)} %get-tuple-element.131) | copy-start | bytes 15364
  525.2 5.6 copy-start.7
  525.2 11.1 %copy-start.2 = (bf16[2,640,1024]{2,1,0:T(8,128)(2,1)S(1)}, bf16[2,640,1024]{2,1,0:T(8,128)(2,1)}, u32[]{:S(2)}) copy-start(bf16[2,640,1024]{2,1,0:T(8,128)(2,1)} %get-tuple-element.135.x_ref) | copy-start | bytes 7864324
  530.8 6.3 copy-start.1
  531.6 18.0 %collective-permute-start.2 = (bf16[128,1024]{1,0:T(8,128)(2,1)}, bf16[128,1024]{1,0:T(8,128)(2,1)S(1)}, u32[]{:S(2)}, u32[]{:S(2)}) collective-permute-start(bf16[128,1024]{1,0:T(8,128)(2,1)} %broadcast_select_fusion.7), channel_id=1, source_target_pairs={{0,64},{64,0},{1,65},{65,1},{2,66},{66,2},{3,67},{67,3},{4,68},{68... | collective-permute-start | bytes 786440 | tf_op jit(solution)/shard_map/ppermute | solution.py:1012
  536.3 1.5 copy-start.18
  536.3 1.5 copy-start.19
  538.7 10.9 %copy-start.12 = (bf16[128,1024]{1,0:T(8,128)(2,1)S(1)}, bf16[128,1024]{1,0:T(8,128)(2,1)}, u32[]{:S(2)}) copy-start(bf16[128,1024]{1,0:T(8,128)(2,1)} %get-tuple-element.121) | copy-start | bytes 786436
  653.4 0.7 copy-start
  687.7 8.7 %copy-start.4 = (bf16[2,256,1536]{2,1,0:T(8,128)(2,1)S(1)}, bf16[2,256,1536]{2,1,0:T(8,128)(2,1)}, u32[]{:S(2)}) copy-start(bf16[2,256,1536]{2,1,0:T(8,128)(2,1)} %reduce-scatter.3.cloned.1.call-done) | copy-start | bytes 4718596
  687.7 8.7 %copy-start.5 = (bf16[2,256,1536]{2,1,0:T(8,128)(2,1)S(1)}, bf16[2,256,1536]{2,1,0:T(8,128)(2,1)}, u32[]{:S(2)}) copy-start(bf16[2,256,1536]{2,1,0:T(8,128)(2,1)} %reduce-scatter.5.cloned.1.call-done) | copy-start | bytes 4718596
Sparse Core Ops, SparseCore 0:
  66.6 42.5 all-gather.4
  111.4 29.4 all-gather.6
  143.2 31.9 all-gather.8
  177.3 31.9 all-gather.10
  323.3 79.0 reduce-scatter.2
  459.8 95.6 reduce-scatter.4

commit v5 on v4

--- a/solution.py
+++ b/solution.py
@@ -848,7 +848,7 @@
         gkv = t_dot(a, dkv_ref[...]).astype(bf16)
         go = t_dot(o_ref[...], dattn_ref[...]).astype(bf16)
         cols = slice(512 * layer, 512 * layer + 512)
-        for t in range(2):
+        for t in range(4):
             part = slice(64 * t, 64 * t + 64)
             for h in range(2):
                 side = slice(512 * h, 512 * h + 512)
@@ -856,20 +856,21 @@
                 out_ref[h, t, 64:128, cols] = gkv[part, side]
                 out_ref[h, t, 128:192, cols] = go[part, side]
     for h in range(2):
-        out_ref[h, 0, 0:64, 1024:1152] = small_ref[h]
-        out_ref[h, 0, 64:192, 1024:1152] = jnp.zeros((128, 128), bf16)
-        out_ref[h, 1, :, 1024:1152] = jnp.zeros((192, 128), bf16)
+        for t in (0, 2):
+            out_ref[h, t, 0:64, 1024:1152] = small_ref[h, :, 64 * t : 64 * t + 128]
+            out_ref[h, t, 64:192, 1024:1152] = jnp.zeros((128, 128), bf16)
+            out_ref[h, t + 1, :, 1024:1152] = jnp.zeros((192, 128), bf16)
 
 
 def dense_grads(layer0, layer1, small):
-    narrow = spec((128, 128), lambda i: (0, i))
+    narrow = spec((128, 256), lambda i: (0, i))
     out = local_call(
         dense_grads_kernel,
         [((2, 16, 192, 1152), bf16)],
         "dense_grads",
-        grid=(8,),
-        in_specs=([narrow, narrow] + [fixed((128, 1024))] * 3) * 2 + [spec((2, 64, 128), lambda i: (0, 0, i))],
-        out_specs=[spec((2, 2, 192, 1152), lambda i: (0, i, 0, 0))],
+        grid=(4,),
+        in_specs=([narrow, narrow] + [fixed((128, 1024))] * 3) * 2 + [spec((2, 64, 256), lambda i: (0, 0, i))],
+        out_specs=[spec((2, 4, 192, 1152), lambda i: (0, i, 0, 0))],
         flops=6 * 2 * 128 * 1024 * 1024,
         moved=18 << 20,
     )(*layer0, *layer1, small)[0]
@@ -959,13 +960,13 @@
     cosine, sine, lo, hi, pick, pick_rows = place
     gain_attn, gain_moe, wr = dense
     x, a, q, kv_all, o, probs, h, b, rows, gu, choices, gate, mix = saved
-    if dout_all is None:
-        dout_all = gather_rows(dout, 1)
+    dout_all, mix = lax.optimization_barrier((dout_all, mix))
     wcol = dot_t(pick_rows.astype(bf16), wr)
     db_part, drows, dgu, inner, coef = experts_back(dout_all, choices, gu, gate, wcol, w)
+    expert_grad = expert_grads(rows, drows, dgu, inner)
+    db_part, expert_grad = lax.optimization_barrier((db_part, expert_grad))
     db_sum = scatter_sum(db_part, 2)
-    expert_grad = lax.psum_scatter(
-        expert_grads(rows, drows, dgu, inner), "dp", scatter_dimension=1, tiled=True)
+    expert_grad = lax.psum_scatter(expert_grad, "dp", scatter_dimension=1, tiled=True)
     router_cols = jnp.einsum("jrd,jr->jd", rows, coef[:, :, 0].astype(bf16), preferred_element_type=f32)
     router_part = jnp.einsum(
         "je,jd->ed", pick_rows[:2], router_cols, preferred_element_type=f32, precision=lax.Precision.HIGHEST)
@@ -1106,7 +1107,8 @@
     later, _ = lax.optimization_barrier((cot, saved0[4]))
     cot_all = gather_rows(later, 1)
     dx1, eg1, dg1, small1 = backward(cot, cot_all, saved1, 1, place, weights, dense[1], expert_w[1], masks[1])
-    dx0, eg0, dg0, small0 = backward(dx1, None, saved0, 0, place, weights, dense[0], expert_w[0], masks[0])
+    dx1_all, eg1 = lax.optimization_barrier((gather_rows(dx1, 1), eg1))
+    dx0, eg0, dg0, small0 = backward(dx1, dx1_all, saved0, 0, place, weights, dense[0], expert_w[0], masks[0])
     eg_sent = jnp.where(first, eg1, eg0)
     both_small = jnp.stack([small0, small1])
     dense_sum, eg_away = scatter_sum(dense_grads(dg0, dg1, both_small), 4, eg_sent)

time: 714 us -> 711 us (level)
  transfers between devices with their start and end apart: 9 -> 9, of which waited for: 1 -> 2; matrix products, arithmetic and copies ran while one was open for 4% -> 4% of each run, Pallas kernels for 59% -> 52%
where the time goes in v5:
time: 711 us; the launch traced here: 705 us
  Pallas kernels  626 us (88%)
  other arithmetic  29.7 us (4%)
  local copies, waits for them, and re-layouts  19.3 us (3%)
  between operations  15 us (2%)
  waiting for transfers between devices  8.43 us (1%)
    pallas_call x8, Pallas kernels, gather_call(): pl.pallas_call(functools.partial(gather_kernel, kind), out_shape=outs, in...  214 us
    pallas_call x7, Pallas kernels, scatter_sum(): pl.pallas_call(functools.partial(scatter_kernel, split), out_shape=[summe...  208 us
    pallas_call x8, Pallas kernels, call(): return pl.pallas_call(kernel, grid=(1,), in_specs=ins, **kinds)(*args)  35.4 us
    pallas_call x2, Pallas kernels, attend(): local_call(attend_kernel, [((128, 1024), bf16), ((4, 512, 2048), bf16)],...  31.9 us
    pallas_call x2, Pallas kernels, experts_back(): local_call(experts_back_kernel, [((rows, 1024), bf16), ((2, FULL, 1024),...  28.3 us
    pallas_call x2, Pallas kernels, experts(): local_call(experts_kernel, [((rows, 1024), bf16), ((2, FULL, 1024), bf16)...  28.3 us
    pallas_call x2, Pallas kernels, attend_back(): local_call(attend_back_kernel, [((128, 1024), f32), ((2048, 1024), bf16)]...  27.3 us
    pallas_call x2, Pallas kernels, expert_grads(): local_call(expert_grads_kernel, [((2, 1024, 1536), bf16)], 'expert_grads'...  18.7 us
  transfers between devices with their start and end apart: 9, of which 2 were waited for; matrix products, arithmetic and copies ran while one was open for 4% of the time, Pallas kernels for 52%

profile of v5, /device:TPU:1, one launch (start us, length us, event | category | flops | bytes accessed | tf_op | source)
XLA Modules:
  0.0 705.0 jit_solution(16811745185328267891)
XLA Ops:
  10.1 0.8 dynamic-slice_bitcast_fusion.1
  10.9 0.9 dynamic-slice_bitcast_fusion
  12.0 2.2 collective-permute-start
  15.0 1.5 pad_maximum_fusion
  18.1 0.9 slice.185.refs_0_
  20.4 0.8 fusion.10.x_ref
  21.2 36.2 %gather_weights.1 = (bf16[2,2,4,4,192,640]{5,4,3,2,1,0:T(8,128)(2,1)}, bf16[1,256,1536]{2,1,0:T(8,128)(2,1)}) custom-call(bf16[192,640]{1,0:T(8,128)(2,1)} %fusion.10.x_ref, bf16[1,256,1536]{2,1,0:T(8,128)(2,1)} %slice.185.refs_0_, bf16[4,4,64,1024]{3,2,1,0:T(8,128)(2,1)} %bitcast.167, bf16[4,4,64,512]{3,2,1,0:T(8,128)(2,1)} %bitcast.171, ...), custom_call_target="tpu_custom_call" | custom-call | tf_op jit(solution)/shard_map/gather_weights/pallas_call | solution.py:199
  57.4 2.1 fusion.1
  60.6 1.6 broadcast_select_fusion.3
  62.2 4.2 pre.2
  66.5 33.3 %gather_swap.1 = (bf16[4,4,128,1024]{3,2,1,0:T(8,128)(2,1)}, bf16[1,256,1536]{2,1,0:T(8,128)(2,1)}) custom-call(bf16[128,1024]{1,0:T(8,128)(2,1)} %get-tuple-element.96.x_ref, bf16[1,256,1536]{2,1,0:T(8,128)(2,1)} %get-tuple-element.185.refs_0_), custom_call_target="tpu_custom_call" | custom-call | tf_op jit(solution)/shard_map/gather_swap/pallas_call | solution.py:199
  99.8 2.4 broadcast_select_fusion.1
  108.4 0.8 copy.70
  109.2 0.8 copy.64
  110.1 16.0 %attend.2 = (bf16[128,1024]{1,0:T(8,128)(2,1)}, bf16[4,512,2048]{2,1,0:T(8,128)(2,1)}) custom-call(bf16[128,1024]{1,0:T(8,128)(2,1)} %get-tuple-element.93.q_ref, bf16[2048,1024]{1,0:T(8,128)(2,1)} %bitcast.145, bf16[2048,1024]{1,0:T(8,128)(2,1)} %bitcast.146, s32[128,1]{1,0:T(8,128)} %copy.63.lo_ref, s32[128,1]{1,0:T(8,128)} %iota_add_fusion.hi_ref), custom_call_target="tpu_custom_call" | custom-call | flops 2147483648 | bytes 13631488 | tf_op jit(solution)/shard_map/attend/pallas_call | solution.py:551
  126.6 3.3 post.2
  129.9 24.5 %gather_plain.5 = bf16[4,4,128,1024]{3,2,1,0:T(8,128)(2,1)} custom-call(bf16[128,1024]{1,0:T(8,128)(2,1)} %get-tuple-element.100.x_ref.b_ref), custom_call_target="tpu_custom_call" | custom-call | tf_op jit(solution)/shard_map/gather_plain/pallas_call | solution.py:199
  154.4 24.5 %gather_plain.8 = bf16[4,4,128,1024]{3,2,1,0:T(8,128)(2,1)} custom-call(bf16[128,1024]{1,0:T(8,128)(2,1)} %select_bitcast_fusion.2.x_ref.dout_ref), custom_call_target="tpu_custom_call" | custom-call | tf_op jit(solution)/shard_map/gather_plain/pallas_call | solution.py:199
  178.9 0.8 fusion.29.wcol_ref
  179.8 14.1 %experts.2 = (bf16[2048,1024]{1,0:T(8,128)(2,1)}, bf16[2,640,1024]{2,1,0:T(8,128)(2,1)}, bf16[2,640,1024]{2,1,0:T(8,128)(2,1)}, bf16[8,160,256]{2,1,0:T(8,128)(2,1)}, f32[2,640,1]{2,1,0:T(8,128)}) custom-call(bf16[2048,1024]{1,0:T(8,128)(2,1)} %bitcast.161, bf16[32,2048]{1,0:T(8,128)(2,1)} %bitcast.179, bf16[32,1024]{1,0:T(8,128)(2,1)} %copy.66.wr_ref, ...), custom_call_target="tpu_custom_call" | custom-call | flops 10737418240 | bytes 20971520 | tf_op jit(solution)/shard_map/experts/pallas_call | solution.py:697
  193.9 24.2 %scatter_sum.6.mix_ref = f32[128,1024]{1,0:T(8,128)} custom-call(bf16[4,4,128,1024]{3,2,1,0:T(8,128)(2,1)} %bitcast.157), custom_call_target="tpu_custom_call" | custom-call | tf_op jit(solution)/shard_map/scatter_sum/pallas_call | solution.py:425
  218.1 1.8 add_convert_fusion.1.x_ref
  219.9 4.2 pre.3
  224.2 22.0 %gather_plain.6 = bf16[4,4,128,1024]{3,2,1,0:T(8,128)(2,1)} custom-call(bf16[128,1024]{1,0:T(8,128)(2,1)} %get-tuple-element.105.x_ref), custom_call_target="tpu_custom_call" | custom-call | tf_op jit(solution)/shard_map/gather_plain/pallas_call | solution.py:199
  246.2 15.9 %attend.3 = (bf16[128,1024]{1,0:T(8,128)(2,1)}, bf16[4,512,2048]{2,1,0:T(8,128)(2,1)}) custom-call(bf16[128,1024]{1,0:T(8,128)(2,1)} %get-tuple-element.104.q_ref, bf16[2048,1024]{1,0:T(8,128)(2,1)} %bitcast.141, bf16[2048,1024]{1,0:T(8,128)(2,1)} %bitcast.142, s32[128,1]{1,0:T(8,128)} %copy.63.lo_ref, s32[128,1]{1,0:T(8,128)} %iota_add_fusion.hi_ref), custom_call_target="tpu_custom_call" | custom-call | flops 2147483648 | bytes 13631488 | tf_op jit(solution)/shard_map/attend/pallas_call | solution.py:551
  262.1 3.3 post.3
  265.4 19.9 %gather_plain.7 = bf16[4,4,128,1024]{3,2,1,0:T(8,128)(2,1)} custom-call(bf16[128,1024]{1,0:T(8,128)(2,1)} %get-tuple-element.108.x_ref.b_ref), custom_call_target="tpu_custom_call" | custom-call | tf_op jit(solution)/shard_map/gather_plain/pallas_call | solution.py:199
  285.4 14.1 %experts.3 = (bf16[2048,1024]{1,0:T(8,128)(2,1)}, bf16[2,640,1024]{2,1,0:T(8,128)(2,1)}, bf16[2,640,1024]{2,1,0:T(8,128)(2,1)}, bf16[8,160,256]{2,1,0:T(8,128)(2,1)}, f32[2,640,1]{2,1,0:T(8,128)}) custom-call(bf16[2048,1024]{1,0:T(8,128)(2,1)} %bitcast.162, bf16[32,2048]{1,0:T(8,128)(2,1)} %bitcast.178, bf16[32,1024]{1,0:T(8,128)(2,1)} %copy.71.wr_ref, ...), custom_call_target="tpu_custom_call" | custom-call | flops 10737418240 | bytes 20971520 | tf_op jit(solution)/shard_map/experts/pallas_call | solution.py:697
  299.5 20.8 %scatter_sum.7.mix_ref = f32[128,1024]{1,0:T(8,128)} custom-call(bf16[4,4,128,1024]{3,2,1,0:T(8,128)(2,1)} %bitcast.156), custom_call_target="tpu_custom_call" | custom-call | tf_op jit(solution)/shard_map/scatter_sum/pallas_call | solution.py:425
  320.4 14.4 %experts_back.2 = (bf16[2048,1024]{1,0:T(8,128)(2,1)}, bf16[2,640,1024]{2,1,0:T(8,128)(2,1)}, bf16[2,640,1024]{2,1,0:T(8,128)(2,1)}, bf16[2,640,512]{2,1,0:T(8,128)(2,1)}, f32[2,640,1]{2,1,0:T(8,128)}) custom-call(bf16[2048,1024]{1,0:T(8,128)(2,1)} %bitcast.160, bf16[8,160,256]{2,1,0:T(8,128)(2,1)} %get-tuple-element.113.s_ref, ...), custom_call_target="tpu_custom_call" | custom-call | flops 10737418240 | bytes 25165824 | tf_op jit(solution)/shard_map/experts_back/pallas_call | solution.py:753
  334.7 9.3 %expert_grads.2 = bf16[2,1024,1536]{2,1,0:T(8,128)(2,1)} custom-call(bf16[2,640,1024]{2,1,0:T(8,128)(2,1)} %get-tuple-element.117.x_ref, bf16[2,640,1024]{2,1,0:T(8,128)(2,1)} %get-tuple-element.118.d_ref, bf16[2,640,1024]{2,1,0:T(8,128)(2,1)} %get-tuple-element.119.dgu_ref, bf16[2,640,512]{2,1,0:T(8,128)(2,1)} %get-tuple-element.120.in_ref), custom_call_target="tpu_custom_call" | custom-call | flops 4026531840 | bytes 16777216 | tf_op jit(solution)/shard_map/expert_grads/pallas_call | solution.py:780
  344.8 0.8 fusion.28.wcol_ref
  345.6 20.1 %scatter_sum.8.sum_ref = f32[128,1024]{1,0:T(8,128)} custom-call(bf16[4,4,128,1024]{3,2,1,0:T(8,128)(2,1)} %bitcast.155), custom_call_target="tpu_custom_call" | custom-call | tf_op jit(solution)/shard_map/scatter_sum/pallas_call | solution.py:425
  365.7 4.8 mid_back.2
  370.4 13.3 %attend_back.2 = (f32[128,1024]{1,0:T(8,128)}, bf16[2048,1024]{1,0:T(8,128)(2,1)}) custom-call(bf16[128,1024]{1,0:T(8,128)(2,1)} %get-tuple-element.104.q_ref, bf16[128,1024]{1,0:T(8,128)(2,1)} %get-tuple-element.106.o_ref.refs_6_, bf16[128,1024]{1,0:T(8,128)(2,1)} %get-tuple-element.123.do_ref, bf16[2048,1024]{1,0:T(8,128)(2,1)} %bitcast.143, ...), custom_call_target="tpu_custom_call" | custom-call | flops 4294967296 | bytes 17825792 | tf_op jit(solution)/shard_map/attend_back/pallas_call | solution.py:600
  383.7 22.2 %scatter_sum.9.dkv_ref = f32[128,1024]{1,0:T(8,128)} custom-call(bf16[4,4,128,1024]{3,2,1,0:T(8,128)(2,1)} %bitcast.158), custom_call_target="tpu_custom_call" | custom-call | tf_op jit(solution)/shard_map/scatter_sum/pallas_call | solution.py:425
  406.0 5.3 end_back.2
  411.3 21.7 %gather_plain.9 = bf16[4,4,128,1024]{3,2,1,0:T(8,128)(2,1)} custom-call(bf16[128,1024]{1,0:T(8,128)(2,1)} %get-tuple-element.128.x_ref.dout_ref), custom_call_target="tpu_custom_call" | custom-call | tf_op jit(solution)/shard_map/gather_plain/pallas_call | solution.py:199
  433.0 13.9 %experts_back.3 = (bf16[2048,1024]{1,0:T(8,128)(2,1)}, bf16[2,640,1024]{2,1,0:T(8,128)(2,1)}, bf16[2,640,1024]{2,1,0:T(8,128)(2,1)}, bf16[2,640,512]{2,1,0:T(8,128)(2,1)}, f32[2,640,1]{2,1,0:T(8,128)}) custom-call(bf16[2048,1024]{1,0:T(8,128)(2,1)} %bitcast.163, bf16[8,160,256]{2,1,0:T(8,128)(2,1)} %get-tuple-element.132.s_ref, ...), custom_call_target="tpu_custom_call" | custom-call | flops 10737418240 | bytes 25165824 | tf_op jit(solution)/shard_map/experts_back/pallas_call | solution.py:753
  446.9 9.3 %expert_grads.3 = bf16[2,1024,1536]{2,1,0:T(8,128)(2,1)} custom-call(bf16[2,640,1024]{2,1,0:T(8,128)(2,1)} %get-tuple-element.136.x_ref, bf16[2,640,1024]{2,1,0:T(8,128)(2,1)} %get-tuple-element.137.d_ref, bf16[2,640,1024]{2,1,0:T(8,128)(2,1)} %get-tuple-element.138.dgu_ref, bf16[2,640,512]{2,1,0:T(8,128)(2,1)} %get-tuple-element.139.in_ref), custom_call_target="tpu_custom_call" | custom-call | flops 4026531840 | bytes 16777216 | tf_op jit(solution)/shard_map/expert_grads/pallas_call | solution.py:780
  456.4 1.5 convert_reduce_fusion.2
  457.9 1.2 broadcast_select_fusion.9
  461.7 2.9 collective-permute-done.1
  464.6 0.8 maximum_bitcast_fusion
  465.7 20.5 %scatter_sum.10.sum_ref = f32[128,1024]{1,0:T(8,128)} custom-call(bf16[4,4,128,1024]{3,2,1,0:T(8,128)(2,1)} %bitcast.154), custom_call_target="tpu_custom_call" | custom-call | tf_op jit(solution)/shard_map/scatter_sum/pallas_call | solution.py:425
  486.2 4.8 mid_back.3
  491.0 14.0 %attend_back.3 = (f32[128,1024]{1,0:T(8,128)}, bf16[2048,1024]{1,0:T(8,128)(2,1)}) custom-call(bf16[128,1024]{1,0:T(8,128)(2,1)} %get-tuple-element.93.q_ref, bf16[128,1024]{1,0:T(8,128)(2,1)} %get-tuple-element.98.o_ref.refs_1_, bf16[128,1024]{1,0:T(8,128)(2,1)} %get-tuple-element.142.do_ref, bf16[2048,1024]{1,0:T(8,128)(2,1)} %bitcast.147, ...), custom_call_target="tpu_custom_call" | custom-call | flops 4294967296 | bytes 17825792 | tf_op jit(solution)/shard_map/attend_back/pallas_call | solution.py:600
  505.0 23.8 %scatter_sum.11.dkv_ref = f32[128,1024]{1,0:T(8,128)} custom-call(bf16[4,4,128,1024]{3,2,1,0:T(8,128)(2,1)} %bitcast.159), custom_call_target="tpu_custom_call" | custom-call | tf_op jit(solution)/shard_map/scatter_sum/pallas_call | solution.py:425
  528.9 5.4 end_back.3
  538.3 8.6 %dense_grads.1 = bf16[2,16,192,1152]{3,2,1,0:T(8,128)(2,1)} custom-call(bf16[128,1024]{1,0:T(8,128)(2,1)} %get-tuple-element.148.refs_0_, bf16[128,1024]{1,0:T(8,128)(2,1)} %get-tuple-element.98.o_ref.refs_1_, bf16[128,1024]{1,0:T(8,128)(2,1)} %get-tuple-element.149.refs_2_, bf16[128,1024]{1,0:T(8,128)(2,1)} %get-tuple-element.150.refs_3_, ...), custom_call_target="tpu_custom_call" | custom-call | flops 1610612736 | bytes 18874368 | tf_op jit(solution)/shard_map/dense_grads/pallas_call | solution.py:867
  546.9 0.8 maximum_bitcast_fusion.1
  547.8 4.2 reduce-scatter.5.cloned.1.call-done
  552.0 1.3 broadcast_select_fusion.refs_0_
  553.3 76.1 %scatter_split.1 = (f32[192,1152]{1,0:T(8,128)}, bf16[2,256,1536]{2,1,0:T(8,128)(2,1)}) custom-call(bf16[2,4,4,192,1152]{4,3,2,1,0:T(8,128)(2,1)} %bitcast.149, bf16[2,256,1536]{2,1,0:T(8,128)(2,1)} %broadcast_select_fusion.refs_0_), custom_call_target="tpu_custom_call" | custom-call | tf_op jit(solution)/shard_map/scatter_split/pallas_call | solution.py:425
  629.4 0.9 slice.167
  630.3 1.0 slice.166
  631.3 1.1 select_convert_fusion.other_ref
  632.4 1.1 slice_select_fusion.2.own_ref
  633.5 17.3 %cross_sum.1.x_ref = bf16[192,640]{1,0:T(8,128)(2,1)S(1)} custom-call(f32[192,640]{1,0:T(8,128)S(1)} %slice_select_fusion.2.own_ref, bf16[192,640]{1,0:T(8,128)(2,1)S(1)} %select_convert_fusion.other_ref), custom_call_target="tpu_custom_call" | custom-call | tf_op jit(solution)/shard_map/cross_sum/pallas_call | solution.py:911
  651.5 32.3 %gather_split.1 = bf16[2,4,4,192,640]{4,3,2,1,0:T(8,128)(2,1)} custom-call(bf16[192,640]{1,0:T(8,128)(2,1)} %copy-done), custom_call_target="tpu_custom_call" | custom-call | tf_op jit(solution)/shard_map/gather_split/pallas_call | solution.py:199
  683.8 1.0 slice.169
  686.1 8.1 %results.1 = (f32[1024,1024]{1,0:T(8,128)}, f32[1024,512]{1,0:T(8,128)}, f32[1024,512]{1,0:T(8,128)}, f32[1024,1024]{1,0:T(8,128)}) custom-call(bf16[2,16,192,640]{3,2,1,0:T(8,128)(2,1)} %bitcast.151), custom_call_target="tpu_custom_call" | custom-call | bytes 20971520 | tf_op jit(solution)/shard_map/results/pallas_call | solution.py:1001
  694.2 2.0 convert_add_fusion
  696.2 1.7 slice_bitcast_fusion
  (126 shorter events, 24.1 us)
Async XLA Ops:
  7.2 172.6 %all-gather.5.cloned.1.call-start = ((), (), s32[]{:S(2)}) async-start(), calls=%async_computation.2 | async-start | bytes 3932160 | tf_op jit(solution)/shard_map/all_gather | solution.py:1077
  12.0 7.0 copy-start.14
  12.0 7.7 %collective-permute-start = (bf16[192,640]{1,0:T(8,128)(2,1)S(1)}, bf16[192,640]{1,0:T(8,128)(2,1)S(1)}, u32[]{:S(2)}, u32[]{:S(2)}) collective-permute-start(bf16[192,640]{1,0:T(8,128)(2,1)S(1)} %fusion.13), channel_id=1, source_target_pairs={{0,64},{64,0},{1,65},{65,1},{2,66},{66,2},{3,67},{67,3},{4,68},{68... | collective-permute-start | bytes 737288 | tf_op jit(solution)/shard_map/ppermute | solution.py:1013
  57.4 2.5 copy-start.19
  57.4 3.1 copy-start.12
  66.4 113.3 %all-gather.7.cloned.1.call-start = ((), (), s32[]{:S(2)}) async-start(), calls=%async_computation.3 | async-start | bytes 3932160 | tf_op jit(solution)/shard_map/all_gather | solution.py:1077
  99.8 3.8 copy-start.18
  99.8 4.0 copy-start.21
  102.2 3.6 copy-start.15
  102.3 183.1 %all-gather.9.cloned.1.call-start = ((), (), s32[]{:S(2)}) async-start(), calls=%async_computation.4 | async-start | bytes 3932160 | tf_op jit(solution)/shard_map/all_gather | solution.py:1077
  103.0 182.4 %all-gather.11.cloned.1.call-start = ((), (), s32[]{:S(2)}) async-start(), calls=%async_computation.5 | async-start | bytes 3932160 | tf_op jit(solution)/shard_map/all_gather | solution.py:1077
  103.6 329.4 %reduce-scatter.3.cloned.1.call-start = ((), (), s32[]{:S(2)}) async-start(), calls=%async_computation.6 | async-start | bytes 7864320 | tf_op jit(solution)/shard_map/reduce_scatter | solution.py:969
  106.6 72.3 %copy-start.9 = (bf16[1024,32]{1,0:T(8,128)(2,1)}, bf16[1024,32]{1,0:T(8,128)(2,1)S(1)}, u32[]{:S(2)}) copy-start(bf16[1024,32]{1,0:T(8,128)(2,1)S(1)} %get-tuple-element.192.wr_ref) | copy-start | bytes 196612
  106.6 238.2 %copy-start.8 = (bf16[1024,32]{1,0:T(8,128)(2,1)}, bf16[1024,32]{1,0:T(8,128)(2,1)S(1)}, u32[]{:S(2)}) copy-start(bf16[1024,32]{1,0:T(8,128)(2,1)S(1)} %get-tuple-element.193.wr_ref) | copy-start | bytes 196612
  110.1 16.0 %copy-start.20 = (bf16[1,1024]{1,0:T(2,128)(2,1)S(1)}, bf16[1,1024]{1,0:T(2,128)(2,1)}, u32[]{:S(2)}) copy-start(bf16[1,1024]{1,0:T(2,128)(2,1)} %param.23) | copy-start | bytes 6148
  193.9 24.2 %copy-start.10 = (f32[128,1024]{1,0:T(8,128)S(1)}, f32[128,1024]{1,0:T(8,128)}, u32[]{:S(2)}) copy-start(f32[128,1024]{1,0:T(8,128)} %get-tuple-element.99.h_ref) | copy-start | bytes 1572868
  344.1 207.9 %reduce-scatter.5.cloned.1.call-start = ((), (), s32[]{:S(2)}) async-start(), calls=%async_computation.7 | async-start | bytes 7864320 | tf_op jit(solution)/shard_map/reduce_scatter | solution.py:969
  456.3 1.6 copy-start.3
  456.3 1.6 copy-start.6
  456.3 3.9 copy-start.2
  456.4 5.3 copy-start.16
  459.1 5.5 collective-permute-start.1
  460.2 5.3 copy-start.13
  528.9 5.5 copy-start.7
  528.9 7.8 %copy-start.1 = (bf16[2,640,1024]{2,1,0:T(8,128)(2,1)S(1)}, bf16[2,640,1024]{2,1,0:T(8,128)(2,1)}, u32[]{:S(2)}) copy-start(bf16[2,640,1024]{2,1,0:T(8,128)(2,1)} %get-tuple-element.136.x_ref) | copy-start | bytes 7864324
  534.4 3.1 copy-start.17
  534.4 12.4 %collective-permute-start.2 = (bf16[128,1024]{1,0:T(8,128)(2,1)S(1)}, bf16[128,1024]{1,0:T(8,128)(2,1)S(1)}, u32[]{:S(2)}, u32[]{:S(2)}) collective-permute-start(bf16[128,1024]{1,0:T(8,128)(2,1)S(1)} %broadcast_select_fusion.7), channel_id=1, source_target_pairs={{0,64},{64,0},{1,65},{65,1},{2,66},{66,2},{3,67},{67,3},{4,68},{68... | collective-permute-start | bytes 786440 | tf_op jit(solution)/shard_map/ppermute | solution.py:1013
  538.3 8.6 %copy-start.11 = (bf16[128,1024]{1,0:T(8,128)(2,1)S(1)}, bf16[128,1024]{1,0:T(8,128)(2,1)}, u32[]{:S(2)}) copy-start(bf16[128,1024]{1,0:T(8,128)(2,1)} %get-tuple-element.147) | copy-start | bytes 786436
  546.9 5.1 copy-start.4
  650.8 0.7 copy-start
  686.1 8.1 %copy-start.5 = (bf16[2,256,1536]{2,1,0:T(8,128)(2,1)S(1)}, bf16[2,256,1536]{2,1,0:T(8,128)(2,1)}, u32[]{:S(2)}) copy-start(bf16[2,256,1536]{2,1,0:T(8,128)(2,1)} %reduce-scatter.5.cloned.1.call-done) | copy-start | bytes 4718596
Sparse Core Ops, SparseCore 0:
  66.6 42.5 all-gather.4
  111.4 29.5 all-gather.6
  143.2 31.9 all-gather.8
  177.3 31.9 all-gather.10
  344.2 82.0 reduce-scatter.2
  456.4 95.4 reduce-scatter.4
